TPU v7x, 32 devices: a whole 2x2x4 slice. The times are simulated.
32 devices in a mesh: dp: 4 (over z), shard: 8 (over y, x, core).
Axes of the slice: x: 2, y: 2, z: 4, core: 2. Of those that a mesh axis runs over, the one named last changes fastest.
Arguments:
- roi_features: bfloat16 [32, 512, 2048], P(('dp', 'shard')), may hold values from -150 to 150
- doc_ids: int32 [32, 512], P(('dp', 'shard')), may hold values from 0 to 5, never falling along the last dimension, each value on 1 to 160 neighbouring positions
- w_roi: bfloat16 [2048, 768], P('shard'), may hold values from -0.125 to 0.125
- bn_gain: bfloat16 [768], P('shard'), may hold values from 0.099609375 to 1.8984375
- bn_beta: bfloat16 [768], P('shard'), may hold values from -3 to 3
- w_qkv: bfloat16 [768, 2304], P('shard'), may hold values from -0.21875 to 0.21875
- w_out: bfloat16 [768, 768], P('shard'), may hold values from -0.625 to 0.625
- ln1_gain: bfloat16 [768], P('shard'), may hold values from 0.099609375 to 1.8984375
- ln1_beta: bfloat16 [768], P('shard'), may hold values from -3 to 3
- w_up: bfloat16 [768, 3072], P('shard'), may hold values from -0.21875 to 0.21875
- w_down: bfloat16 [3072, 768], P('shard'), may hold values from -0.21875 to 0.21875
- ln2_gain: bfloat16 [768], P('shard'), may hold values from 0.099609375 to 1.8984375
- ln2_beta: bfloat16 [768], P('shard'), may hold values from -3 to 3
- cotangent: bfloat16 [32, 512, 768], P(('dp', 'shard')), may hold values from -6 to 6
Outputs:
- layer_out: bfloat16 [32, 512, 768], P(('dp', 'shard'))
- roi_grad: float32 [32, 512, 2048], P(('dp', 'shard'))
- grad_w_roi: float32 [2048, 768], P('shard')
- grad_bn_gain: float32 [768], P('shard')
- grad_bn_beta: float32 [768], P('shard')
- grad_w_qkv: float32 [768, 2304], P('shard')
- grad_w_out: float32 [768, 768], P('shard')
- grad_ln1_gain: float32 [768], P('shard')
- grad_ln1_beta: float32 [768], P('shard')
- grad_w_up: float32 [768, 3072], P('shard')
- grad_w_down: float32 [3072, 768], P('shard')
- grad_ln2_gain: float32 [768], P('shard')
- grad_ln2_beta: float32 [768], P('shard')
- bn_mean: float32 [768], replicated
- bn_var: float32 [768], replicated
Inputs may be any that keep to these rules, and one draw needn't show every extreme that they name: `doc_ids`: document numbers never fall along a packed row, and each document holds 1 to 160 tokens.
All inputs are finite; a program needn't handle non-finite values.
Results may differ from a plain program's by a relative error of at most 0.015.
Values may be sent and summed in bfloat16 or wider, within the bound.
No kernel may reach another device: no remote copies, remote signals or barrier semaphores. Data moves between devices by JAX's collectives and lax.ppermute only.
A program may use at most 192 MiB of HBM per device.

v0:
```python
import functools
import math

import jax
import jax.numpy as jnp
from jax import lax
from jax.experimental import pallas as pl
from jax.experimental.pallas import tpu as pltpu
from jax.sharding import PartitionSpec as P

HEAD_DIM = 64
EPSILON = 1e-05
SCORE_SCALE = 0.125
MASKED = -1000000000.0
CORE, ACROSS, ALONG = 1, 2, 4
TILE = 256
F32, LOW = jnp.float32, jnp.bfloat16

ERFC_RATE = 0.33
ERFC = (
    0.18636612594127655,
    0.18283699452877045,
    0.20192526280879974,
    0.04500619322061539,
    0.4125494658946991,
    -0.3554469347000122,
    0.46269258856773376,
    -0.13592977821826935,
)


def direct_mesh():
    return lax.axis_size("shard") == 8 and lax.axis_size("dp") == 4


def swap(values, step, axis="shard"):
    size = lax.axis_size(axis)
    return lax.ppermute(values, axis, [(i, i ^ step) for i in range(size)])


def add_low(*terms):
    total = terms[0].astype(F32)
    for term in terms[1:]:
        total = total + term.astype(F32)
    return total.astype(LOW)


def sum_everywhere(part):
    if not direct_mesh():
        return lax.psum(part, ("dp", "shard"))
    part = part + swap(part, CORE)
    part = (part + swap(part, 1, "dp")) + (swap(part, 2, "dp") + swap(part, 3, "dp"))
    return (part + swap(part, ACROSS)) + (swap(part, ALONG) + swap(part, ACROSS | ALONG))


def tie(values, *after):
    return lax.optimization_barrier((values, after))[0]


class OwnedSum:
    def __init__(self, halves):
        self.direct = direct_mesh()
        if self.direct:
            self.mine, self.got = halves[0], swap(halves[1], CORE)
            rows = self.mine.shape[1] // 2
            self.cuts = ((slice(0, rows), 1, 2), (slice(rows, None), 2, 1))
        else:
            whole = halves[0].reshape(-1, halves[0].shape[-1])
            self.part = lax.psum_scatter(whole, "shard", scatter_dimension=0, tiled=True)

    def plane_one(self, *after):
        if not self.direct:
            return self.part
        self.mine, self.got = tie((self.mine, self.got), *after)
        mine, got = self.mine, self.got
        sent = [
            add_low(jnp.stack([mine[near, cut], mine[3, cut]]), jnp.stack([got[near, cut], got[3, cut]]))
            for cut, near, _ in self.cuts
        ]
        self.came = [swap(part, 2 * near) for part, (_, near, _) in zip(sent, self.cuts)]
        return sent

    def plane_two(self, *after):
        if not self.direct:
            return self.part
        self.mine, self.got, self.came = tie((self.mine, self.got, self.came), *after)
        passed = [
            add_low(self.mine[far, cut], self.got[far, cut], came[1]) for came, (cut, _, far) in zip(self.came, self.cuts)
        ]
        self.back = [swap(part, 2 * far) for part, (_, _, far) in zip(passed, self.cuts)]
        return passed

    def plane_done(self, *after):
        if not self.direct:
            return self.part
        mine, got, came, back = tie((self.mine, self.got, self.came, self.back), *after)
        return jnp.concatenate(
            [add_low(mine[0, cut], got[0, cut], c[0], b) for c, b, (cut, _, _) in zip(came, back, self.cuts)]
        )


class LineSum:
    def __init__(self, part):
        self.part = part
        self.pairs = ([(0, 1), (3, 2)], [(1, 2), (2, 1)], [(1, 0), (2, 3)])
        self.number = 0

    def step(self, *after):
        if not direct_mesh():
            return self.part
        if self.number == 0:
            self.part = tie(self.part, *after)
        else:
            self.part = add_low(*tie((self.part, self.came), *after))
        self.came = lax.ppermute(self.part, "dp", self.pairs[self.number])
        self.number += 1
        return self.part

    def total(self):
        if not direct_mesh():
            return lax.psum(self.part, "dp").astype(F32)
        place = lax.axis_index("dp")
        return jnp.where((place == 1) | (place == 2), self.part, self.came).astype(F32)


def dot(left, right, left_dim=1, right_dim=0):
    return lax.dot_general(
        left, right, (((left_dim,), (right_dim,)), ((), ())), preferred_element_type=F32
    )


def wait_all(copies):
    for copy in copies:
        copy.wait()


def start_all(copies):
    for copy in copies:
        copy.start()
    return copies


def part(index, size):
    return pl.ds(pl.multiple_of(index * size, size), size)


def by_rows(count, body):
    @pl.loop(0, count // 128)
    def _(i):
        body(part(i, 128))


def piece_copies(pieces, places, target, sems, source_columns=None, columns=slice(None)):
    copies = []
    for i, piece in enumerate(pieces):
        rows = piece.shape[0]
        source = piece if source_columns is None else piece.at[:, source_columns]
        at = part(places[i], rows) if len(pieces) > 1 else pl.ds(0, rows)
        copies.append(pltpu.make_async_copy(source, target.at[at, columns], sems.at[i]))
    return copies


def put_blocks(halves, places, values, columns, work, section=0):
    if len(halves) == 1:
        halves[0][0, part(section, values.shape[0]), columns] = values.astype(LOW)
        return
    rows = values.shape[0] // 8
    work[...] = values.astype(LOW)
    for rel in range(8):
        halves[rel & 1][rel >> 1, part(section, rows), columns] = work[part(places[rel], rows), :]


def row_blocks(halves, places, make, rows=None):
    chips = halves[0].shape[0]
    rows = rows or halves[0].shape[1]
    if len(halves) == 1:
        step = min(rows, 512)

        @pl.loop(0, rows // step)
        def _(i):
            at = pl.multiple_of(i * step, step)
            halves[0][0, pl.ds(at, step)] = make(at, step).astype(LOW)

        return

    @pl.loop(0, chips)
    def _(j):
        for k in range(2):
            halves[k][j, :rows] = make(places[2 * j + k] * rows, rows).astype(LOW)


def lanes(first, size):
    return pl.ds(pl.multiple_of(first, 128), size)


def batch_scale(sums_ref, tokens):
    mean = sums_ref[0:1, :] * (1.0 / tokens)
    var = sums_ref[1:2, :] * (1.0 / tokens) - mean * mean
    return mean, var, lax.rsqrt(var + EPSILON)


def embed(projected_ref, sums_ref, tokens, rows=slice(None)):
    mean, _, inv = batch_scale(sums_ref, tokens)
    return (projected_ref[rows, :] - mean) * inv * sums_ref[2:3, :] + sums_ref[3:4, :]


def normalize(values):
    center = values - jnp.mean(values, axis=-1, keepdims=True)
    inv = lax.rsqrt(jnp.mean(center * center, axis=-1, keepdims=True) + EPSILON)
    return center * inv, inv


def normalize_back(scaled, normed, inv):
    return inv * (
        scaled
        - jnp.mean(scaled, axis=-1, keepdims=True)
        - normed * jnp.mean(scaled * normed, axis=-1, keepdims=True)
    )


def gelu_pair(values):
    t = 1.0 / (1.0 + (ERFC_RATE * 0.7071067811865476) * jnp.abs(values))
    poly = 0.5 * ERFC[-1]
    for factor in ERFC[-2::-1]:
        poly = poly * t + 0.5 * factor
    bell = jnp.exp(values * values * -0.5)
    tail = poly * t * bell
    share = jnp.where(values < 0, tail, 1.0 - tail)
    return values * share, share + values * bell * 0.3989422804014327


def size_of(array):
    return math.prod(array.shape) * jnp.dtype(array.dtype).itemsize


def call(kernel, args, outs, scratch, name, spare=6, far=(), near=(), out_near=(), sems=()):
    spaces = [pltpu.HBM if i in far else pltpu.VMEM for i in range(len(args))]
    spaces[0] = pltpu.SMEM
    held = [a for i, a in enumerate(args) if i and i not in far and i not in near]
    held += [a for i, a in enumerate(outs) if i not in out_near] + list(scratch)
    args = [
        pltpu.with_memory_space_constraint(a, pltpu.HBM if i in far else pltpu.VMEM) if i in far or i in near else a
        for i, a in enumerate(args)
    ]
    return pl.pallas_call(
        kernel,
        in_specs=[pl.BlockSpec(memory_space=space) for space in spaces],
        out_specs=[pl.BlockSpec(memory_space=pltpu.VMEM)] * len(outs),
        out_shape=[pltpu.VMEM(a.shape, a.dtype) if i in out_near else a for i, a in enumerate(outs)],
        scratch_shapes=list(scratch) + [pltpu.SemaphoreType.DMA(count) for count in sems],
        compiler_params=pltpu.CompilerParams(vmem_limit_bytes=sum(map(size_of, held)) + spare * 2**20),
        cost_estimate=pl.CostEstimate(flops=1024, bytes_accessed=1024, transcendentals=0),
        name=name,
    )(*args)


def shape(dims, kind=F32):
    return jax.ShapeDtypeStruct(tuple(dims), kind)


def column_sum(values):
    return jnp.sum(values, axis=0, keepdims=True)


def project_kernel(count, places, x_ref, params_ref, *refs):
    pieces, (out_ref, sums_ref, weight, sems) = refs[:count], refs[count:]
    wait_all(start_all(piece_copies(pieces, places, weight, sems)))
    sums_ref[...] = params_ref[...]

    @pl.loop(0, out_ref.shape[1] // TILE)
    def _(n):
        cols = part(n, TILE)
        values = dot(x_ref[...], weight[:, cols])
        out_ref[:, cols] = values
        sums_ref[0:1, cols] = column_sum(values)
        sums_ref[1:2, cols] = column_sum(values * values)


def attend_kernel(count, tokens, places, projected_ref, sums_ref, doc_row, doc_col, *refs):
    pieces = refs[:count]
    packed_out, mixed_out, lse_out, weight, embedded, sems = refs[count:]
    length, width = projected_ref.shape

    def fetch(c):
        return piece_copies(pieces, places, weight, sems.at[c], part(c, width), part(c, width))

    for c in range(3):
        start_all(fetch(c))

    @functools.partial(by_rows, length)
    def _(rows):
        embedded[rows, :] = embed(projected_ref, sums_ref, tokens, rows).astype(LOW)

    @pl.loop(0, 3)
    def _(c):
        wait_all(fetch(c))
        for n in range(width // TILE):
            cols = part(c * (width // TILE) + n, TILE)
            packed_out[cols, :] = dot(embedded[...], weight[:, cols]).T.astype(LOW)

    same = doc_col[...] == doc_row[...]
    heads = width // HEAD_DIM

    @pl.loop(0, heads, unroll=3)
    def _(head):
        queries = packed_out[part(head, HEAD_DIM), :] * jnp.asarray(SCORE_SCALE, LOW)
        keys = packed_out[part(head + heads, HEAD_DIM), :]
        values = packed_out[part(head + 2 * heads, HEAD_DIM), :]
        scores = jnp.where(same, dot(keys, queries, 0, 0), MASKED)
        top = jnp.max(scores, axis=0, keepdims=True)
        expo = jnp.exp(scores - top)
        total = jnp.sum(expo, axis=0, keepdims=True)
        mixed = dot(values, expo.astype(LOW)) * (1.0 / total)
        mixed_out[part(head, HEAD_DIM), :] = mixed.astype(LOW)
        lse_out[pl.ds(head, 1), :] = top + jnp.log(total)


def expand_kernel(count, tokens, places, projected_ref, sums_ref, mixed_ref, *refs):
    pieces, ups, refs = refs[:count], refs[count : 2 * count], refs[2 * count :]
    hat_out, inv_out, active_out, slope_out, weight_out, weight_up, low_one, sems_out, sems_up = refs
    length, width = projected_ref.shape
    copies_out = start_all(piece_copies(pieces, places, weight_out, sems_out, pl.ds(3 * width, width)))

    def fetch(c):
        return piece_copies(ups, places, weight_up, sems_up.at[c], part(c, width), part(c, width))

    for c in range(4):
        start_all(fetch(c))
    wait_all(copies_out)
    hat_out[...] = dot(mixed_ref[...], weight_out[...], 0, 0)

    @functools.partial(by_rows, length)
    def _(rows):
        hat, inv = normalize(embed(projected_ref, sums_ref, tokens, rows) + hat_out[rows, :])
        hat_out[rows, :] = hat
        inv_out[rows, :] = inv
        low_one[rows, :] = (hat * sums_ref[4:5, :] + sums_ref[5:6, :]).astype(LOW)

    @pl.loop(0, 4)
    def _(c):
        wait_all(fetch(c))
        for n in range(width // TILE):
            cols = part(c * (width // TILE) + n, TILE)
            active, slope = gelu_pair(dot(low_one[...], weight_up[:, cols]))
            active_out[:, cols] = active.astype(LOW)
            slope_out[:, cols] = slope.astype(LOW)


def contract_kernel(count, places, hat_ref, sums_ref, grad_ref, active_ref, *refs):
    pieces, refs = refs[:count], refs[count:]
    halves, (layer_out, back_out, grads_out, weight, branch, low_back, sems) = refs[:-7], refs[-7:]
    length, width = hat_ref.shape
    copies = start_all(piece_copies(pieces, places, weight, sems))

    @functools.partial(by_rows, length)
    def _(rows):
        branch[rows, :] = hat_ref[rows, :] * sums_ref[4:5, :] + sums_ref[5:6, :]

    wait_all(copies)

    @pl.loop(0, 4)
    def _(c):
        branch[...] += dot(active_ref[:, part(c, width)], weight[part(c, width), :])

    grads_out[...] = jnp.zeros_like(grads_out)

    @functools.partial(by_rows, length)
    def _(rows):
        hat, inv = normalize(branch[rows, :])
        layer_out[rows, :] = (hat * sums_ref[6:7, :] + sums_ref[7:8, :]).astype(LOW)
        gradient = grad_ref[rows, :].astype(F32)
        grads_out[0:1, :] += column_sum(gradient * hat)
        grads_out[1:2, :] += column_sum(gradient)
        back = normalize_back(gradient * sums_ref[6:7, :], hat, inv)
        back_out[rows, :] = back
        low_back[rows, :] = back.astype(LOW)

    row_blocks(halves, places, lambda at, n: dot(active_ref[:, lanes(at, n)], low_back[...], 0, 0))


def hidden_back_kernel(count, places, back_ref, hat_ref, sums_ref, slope_ref, *refs):
    pieces, refs = refs[:count], refs[count:]
    halves, (hidden_out, weight, low_back, low_one, work, sems) = refs[:-6], refs[-6:]
    length, width = hat_ref.shape
    copies = start_all(piece_copies(pieces, places, weight, sems))

    @functools.partial(by_rows, length)
    def _(rows):
        low_back[rows, :] = back_ref[rows, :].astype(LOW)
        low_one[:, rows] = (hat_ref[rows, :] * sums_ref[4:5, :] + sums_ref[5:6, :]).T.astype(LOW)

    wait_all(copies)

    @pl.loop(0, 4)
    def _(c):
        for n in range(width // TILE):
            cols = part(c * (width // TILE) + n, TILE)
            values = (dot(low_back[...], weight[cols, :], 1, 1) * slope_ref[:, cols].astype(F32)).astype(LOW)
            hidden_out[:, cols] = values
            put_blocks(halves, places, dot(low_one[...], values), slice(n * TILE, (n + 1) * TILE), work.at[n % 2], c)


def attend_back_head(head, first_head, packed_ref, mixed_back, lse_ref, same, out_ref, step, start):
    width = packed_ref.shape[0] // 3
    at = part(head + first_head, HEAD_DIM)
    queries = packed_ref[at, :] * jnp.asarray(SCORE_SCALE, LOW)
    at = part(head + first_head + width // HEAD_DIM, HEAD_DIM)
    keys = packed_ref[at, :]
    at = part(head + first_head + 2 * width // HEAD_DIM, HEAD_DIM)
    values = packed_ref[at, :]
    scores = jnp.where(same, dot(keys, queries, 0, 0), MASKED)
    probs = jnp.exp(scores - lse_ref[pl.ds(head + first_head, 1), :])
    grad_probs = dot(values, mixed_back, 0, 0)
    grad_values = dot(mixed_back, probs.astype(LOW), 1, 1)
    inner = jnp.sum(probs * grad_probs, axis=0, keepdims=True)
    grad_scores = (probs * (grad_probs - inner)).astype(LOW)
    grad_queries = dot(keys, grad_scores) * SCORE_SCALE
    grad_keys = dot(queries, grad_scores, 1, 1)
    for i, grad in enumerate((grad_queries, grad_keys, grad_values)):
        out_ref[part((i * step + start) // HEAD_DIM + head, HEAD_DIM), :] = grad.astype(LOW)


def expand_back_kernel(
    count, places, back_ref, hat_ref, inv_ref, sums_ref, hidden_ref, packed_ref, lse_ref, doc_row, doc_col, *refs
):
    pieces, ups, refs = refs[:count], refs[count : 2 * count], refs[2 * count :]
    (
        first_out, low_out, mixed_back_out, grads_out, grad_packed_out, weight_out, weight_up, total, sems_out, sems_up
    ) = refs
    length, width = hat_ref.shape

    def fetch(c):
        return piece_copies(ups, places, weight_up, sems_up.at[c], part(c, width), part(c, width))

    for c in range(4):
        start_all(fetch(c))
    copies_out = start_all(piece_copies(pieces, places, weight_out, sems_out, pl.ds(3 * width, width)))
    total[...] = back_ref[...]

    @pl.loop(0, 4)
    def _(c):
        wait_all(fetch(c))
        total[...] += dot(hidden_ref[:, part(c, width)], weight_up[:, part(c, width)], 1, 1)

    grads_out[...] = jnp.zeros_like(grads_out)

    @functools.partial(by_rows, length)
    def _(rows):
        gradient, hat = total[rows, :], hat_ref[rows, :]
        grads_out[0:1, :] += column_sum(gradient * hat)
        grads_out[1:2, :] += column_sum(gradient)
        first = normalize_back(gradient * sums_ref[4:5, :], hat, inv_ref[rows, :])
        first_out[rows, :] = first
        low_out[rows, :] = first.astype(LOW)

    wait_all(copies_out)
    mixed_back_out[...] = dot(weight_out[...], low_out[...], 1, 1).astype(LOW)
    same = doc_col[...] == doc_row[...]
    heads = grad_packed_out.shape[0] // (3 * HEAD_DIM)

    @pl.loop(0, heads, unroll=3)
    def _(head):
        mixed_back = mixed_back_out[part(head, HEAD_DIM), :]
        attend_back_head(head, 0, packed_ref, mixed_back, lse_ref, same, grad_packed_out, heads * HEAD_DIM, 0)


def attend_back_kernel(
    count, tokens, places, packed_ref, mixed_back_ref, lse_ref, doc_row, doc_col, projected_ref, sums_ref, first_ref,
    done_ref, *refs
):
    pieces = refs[:count]
    grad_packed_out, embedded_out, grads_out, weight, sems = refs[count:]
    length, width = projected_ref.shape
    copies = start_all(piece_copies(pieces, places, weight, sems, pl.ds(0, 3 * width)))
    same = doc_col[...] == doc_row[...]
    done = done_ref.shape[0] // 3

    @pl.loop(0, (width - done) // HEAD_DIM, unroll=3)
    def _(head):
        mixed_back = mixed_back_ref[part(head + done // HEAD_DIM, HEAD_DIM), :]
        attend_back_head(head, done // HEAD_DIM, packed_ref, mixed_back, lse_ref, same, grad_packed_out, width, done)

    for i in range(3):
        grad_packed_out[i * width : i * width + done, :] = done_ref[i * done : (i + 1) * done, :]
    wait_all(copies)
    mean, _, inv = batch_scale(sums_ref, tokens)
    for n in range(width // TILE):
        cols = slice(n * TILE, (n + 1) * TILE)
        values = first_ref[:, cols] + dot(weight[cols, :], grad_packed_out[...]).T
        embedded_out[:, cols] = values
        normed = (projected_ref[:, cols] - mean[:, cols]) * inv[:, cols]
        grads_out[0:1, cols] = column_sum(values)
        grads_out[1:2, cols] = column_sum(values * normed)


def packed_gradient_kernel(tokens, places, grad_packed_ref, projected_ref, sums_ref, *refs):
    halves, (low, work) = refs[:-2], refs[-2:]
    length, width = projected_ref.shape

    @functools.partial(by_rows, length)
    def _(rows):
        low[:, rows] = embed(projected_ref, sums_ref, tokens, rows).T.astype(LOW)

    @pl.loop(0, 3)
    def _(c):
        for n in range(width // TILE):
            cols = part(c * (width // TILE) + n, TILE)
            put_blocks(halves, places, dot(low[...], grad_packed_ref[cols, :], 1, 1), cols, work.at[n % 2])


def project_back_kernel(tokens, places, embedded_ref, projected_ref, sums_ref, grads_ref, mixed_ref, low_ref, x_ref, *refs):
    halves, (low_out, work) = refs[:-2], refs[-2:]
    mean, _, inv = batch_scale(sums_ref, tokens)
    roi_rows = x_ref.shape[1] * halves[0].shape[1] // (x_ref.shape[1] + low_ref.shape[1])

    @functools.partial(by_rows, projected_ref.shape[0])
    def _(rows):
        normed = (projected_ref[rows, :] - mean) * inv
        shift = grads_ref[0:1, :] * (1.0 / tokens) + normed * (grads_ref[1:2, :] * (1.0 / tokens))
        low_out[rows, :] = (sums_ref[2:3, :] * inv * (embedded_ref[rows, :] - shift)).astype(LOW)

    row_blocks(halves, places, lambda at, n: dot(x_ref[:, lanes(at, n)], low_out[...], 0, 0), roi_rows)
    work[...] = dot(mixed_ref[...], low_ref[...]).astype(LOW)
    if len(halves) == 1:
        halves[0][0, roi_rows:, :] = work[...]
    else:
        rows = halves[0].shape[1] - roi_rows
        for rel in range(8):
            halves[rel & 1][rel >> 1, roi_rows:, :] = work[part(places[rel], rows), :]


def input_gradient_kernel(count, places, low_ref, *refs):
    pieces, (out_ref, weight, sems) = refs[:count], refs[count:]
    wait_all(start_all(piece_copies(pieces, places, weight, sems)))

    @pl.loop(0, weight.shape[0] // 512)
    def _(i):
        out_ref[:, part(i, 512)] = dot(low_ref[...], weight[part(i, 512), :], 1, 1)


def sides(own):
    return [swap(own, ACROSS), swap(own, ALONG)]


def corner_halves(across, along):
    half = across.shape[0] // 2
    return [swap(along[:half], ACROSS), swap(across[half:], ALONG)]


def with_cores(chips):
    pieces = []
    for shard in chips:
        pieces += [shard, swap(shard, CORE)]
    return pieces


def per_device(
    roi_features, doc_ids, w_roi, bn_gain, bn_beta, w_qkv, w_out, ln1_gain, ln1_beta,
    w_up, w_down, ln2_gain, ln2_beta, cotangent,
):
    _, length, roi_width = roi_features.shape
    width, hidden = w_roi.shape[1], w_up.shape[1]
    devices = lax.axis_size("dp") * lax.axis_size("shard")
    tokens = length * devices
    me = lax.axis_index("shard")
    direct = direct_mesh()
    shards, rows = 8 if direct else 1, w_up.shape[0]
    cores, chips = (2, 4) if direct else (1, 1)
    places = (me ^ jnp.arange(8)).astype(jnp.int32) if direct else jnp.zeros((8,), jnp.int32)

    x = roi_features.reshape(length, roi_width)
    doc_row, doc_col = doc_ids.reshape(1, length), doc_ids.reshape(length, 1)
    own_params = jnp.stack([bn_gain, bn_beta, ln1_gain, ln1_beta, ln2_gain, ln2_beta]).astype(F32)
    own_params = jnp.where(lax.axis_index("dp") == 0, own_params, 0.0)
    own_start = me * bn_gain.shape[0]
    params = lax.dynamic_update_slice(jnp.zeros((8, width), F32), own_params, (2, own_start))

    gather = functools.partial(lax.all_gather, axis_name="shard", axis=0, tiled=True)
    wide = jnp.concatenate([w_qkv, w_out], axis=1)
    if direct:
        roi_chips = [w_roi, *sides(w_roi), swap(w_roi, ACROSS | ALONG)]
        wide = tie(wide, params)
        wide_chips = [wide, *sides(wide), swap(wide, ACROSS | ALONG)]
        roi_pieces = with_cores(tie(roi_chips, wide))
    else:
        roi_pieces = [gather(w_roi)]
    count = len(roi_pieces)

    def blocks(r, c):
        return [shape((chips, r, c), LOW)] * cores

    def low(r, c):
        return pltpu.VMEM((r, c), LOW)

    projected, sums = call(
        functools.partial(project_kernel, count),
        [places, x, params, *roi_pieces],
        [shape((length, width)), shape((8, width))],
        [low(roi_width, width)],
        "project",
        out_near=(0,),
        far=range(3, 100),
        sems=((8,),),
    )
    if direct:
        sums = sums + swap(sums, CORE)
        sums = sums + swap(sums, 1, "dp")
        sums = sums + swap(sums, 2, "dp")
        around = [swap(sums, ACROSS), swap(sums, ALONG), swap(sums, ACROSS | ALONG)]
        wide_chips = tie(wide_chips, sums)
        around = tie(around, wide_chips)
        sums = (sums + around[0]) + (around[1] + around[2])
        wide_pieces = with_cores(wide_chips)
        up_sides = sides(tie(w_up, sums))
    else:
        sums = lax.psum(sums, ("dp", "shard"))
        wide_pieces = [gather(wide)]

    heads = width // HEAD_DIM
    part_width = heads // 2 * HEAD_DIM
    packed_qkv, mixed, lse = call(
        functools.partial(attend_kernel, count, tokens),
        [places, projected, sums, doc_row, doc_col, *wide_pieces],
        [shape((3 * width, length), LOW), shape((width, length), LOW), shape((heads, length))],
        [low(width, 3 * width), low(length, width)],
        "attend",
        near=(1,), out_near=(0, 1, 2),
        far=range(5, 100),
        sems=((3, 8),),
    )
    if direct:
        up_sides = tie(up_sides, mixed)
        up_corner = jnp.concatenate(corner_halves(*up_sides))
        down_sides = sides(tie(w_down, up_sides))
        up_pieces = with_cores([w_up, *up_sides, up_corner])
    else:
        up_pieces, down_parts = [gather(w_up)], [gather(w_down)]
    hat, inv, active, slope = call(
        functools.partial(expand_kernel, count, tokens),
        [places, projected, sums, mixed, *wide_pieces, *up_pieces],
        [shape((length, width)), shape((length, 1)), shape((length, hidden), LOW), shape((length, hidden), LOW)],
        [low(width, width), low(width, hidden), low(length, width)],
        "expand",
        near=(1, 3), out_near=(0, 1, 2, 3),
        far=range(4, 100),
        sems=((8,), (4, 8)),
    )
    if direct:
        down_sides = tie(down_sides, active)
        down_parts = with_cores([w_down, *down_sides, jnp.concatenate(corner_halves(*down_sides))])
    *down_halves, layer_out, back, grads_two = call(
        functools.partial(contract_kernel, count),
        [places, hat, sums, cotangent.reshape(length, width), active, *down_parts],
        blocks(hidden // shards, width) + [shape((length, width), LOW), shape((length, width)), shape((2, width))],
        [low(hidden, width), pltpu.VMEM((length, width), F32), low(length, width)],
        "contract",
        near=(1, 4), out_near=(cores + 1,),
        far=range(5, 100),
        sems=((8,),),
    )
    down = OwnedSum(down_halves)
    *up_halves, grad_hidden = call(
        functools.partial(hidden_back_kernel, count),
        [places, back, hat, sums, slope, *down_parts],
        blocks(hidden // shards, width) + [shape((length, hidden), LOW)],
        [low(hidden, width), low(length, width), low(width, length), pltpu.VMEM((2, width, TILE), LOW)],
        "hidden_back",
        near=(1, 2, 4), out_near=(cores,),
        far=range(5, 100),
        sems=((8,),),
    )
    up = OwnedSum(up_halves)
    sent = down.plane_one(grad_hidden)
    first, low_first, mixed_back, grads_one, grad_part = call(
        functools.partial(expand_back_kernel, count),
        [
            tie(places, sent), back, hat, inv, sums, grad_hidden, packed_qkv, lse, doc_row, doc_col,
            *wide_pieces, *up_pieces,
        ],
        [
            shape((length, width)), shape((length, width), LOW), shape((width, length), LOW), shape((2, width)),
            shape((3 * part_width, length), LOW),
        ],
        [low(width, width), low(width, hidden), pltpu.VMEM((length, width), F32)],
        "expand_back",
        near=(1, 2, 3, 5, 6, 7), out_near=(0, 1, 2, 4),
        far=range(10, 100),
        sems=((8,), (4, 8)),
    )
    sent = down.plane_two(first)
    sent = up.plane_one(sent)
    grad_packed, grad_embedded, grads_bn = call(
        functools.partial(attend_back_kernel, count, tokens),
        [
            tie(places, sent), packed_qkv, mixed_back, lse, doc_row, doc_col, projected, sums, first, grad_part,
            *wide_pieces,
        ],
        [shape((3 * width, length), LOW), shape((length, width)), shape((2, width))],
        [low(width, 3 * width)],
        "attend_back",
        near=(1, 2, 3, 6, 8, 9), out_near=(0, 1),
        far=range(10, 100),
        sems=((8,),),
    )
    second = jnp.concatenate([grads_bn, grads_one, grads_two, jnp.zeros((2, width), F32)])
    if direct:
        second = second + swap(tie(second, down.back), CORE)
        second = second + swap(second, 1, "dp")
        second = second + swap(second, 2, "dp")
        second = tie(second, up.came)
        around = [swap(second, ACROSS), swap(second, ALONG), swap(second, ACROSS | ALONG)]
        sent = up.plane_two(second)
        down_sum = LineSum(down.plane_done(sent))
        around = tie(around, sent, down_sum.step())
        second = (second + around[0]) + (around[1] + around[2])
    else:
        second = lax.psum(second, ("dp", "shard"))
    roi_rows, out_rows = roi_width // shards, width // shards
    *roi_halves, low_projected = call(
        functools.partial(project_back_kernel, tokens),
        [places, grad_embedded, projected, sums, second, mixed, low_first, x],
        blocks(roi_rows + out_rows, width) + [shape((length, width), LOW)],
        [low(width, width)],
        "project_back",
        near=(1, 2, 5, 6), out_near=(cores,),
    )
    roi = OwnedSum(roi_halves)
    start_packed = tie(places, low_projected)
    qkv_halves = call(
        functools.partial(packed_gradient_kernel, tokens),
        [start_packed, grad_packed, projected, sums],
        blocks(width // shards, 3 * width),
        [low(width, length), pltpu.VMEM((2, width, TILE), LOW)],
        "packed_gradient",
        near=(1, 2),
    )
    qkv = OwnedSum(qkv_halves)
    sent = roi.plane_one(qkv_halves)
    if direct:
        up_sum = LineSum(up.plane_done(sent))
        sent = up_sum.step()
    (roi_grad,) = call(
        functools.partial(input_gradient_kernel, count),
        [tie(places, sent), low_projected, *roi_pieces],
        [shape((length, roi_width))],
        [low(roi_width, width)],
        "input_gradient",
        near=(1,),
        far=range(2, 100),
        sems=((8,),),
    )
    if direct:
        sent = roi.plane_two(down_sum.step(roi_grad))
        sent = qkv.plane_one(sent)
        sent = down_sum.step(up_sum.step(sent))
        roi_sum = LineSum(roi.plane_done(sent))
        sent = roi_sum.step()
        sent = qkv.plane_two(sent)
        sent = up_sum.step(sent)
        sent = roi_sum.step(sent)
        qkv_sum = LineSum(qkv.plane_done(sent))
        sent = qkv_sum.step()
        sent = roi_sum.step(sent)
        sent = qkv_sum.step(sent)
        sent = qkv_sum.step(sent)
        sum_roi, sum_down, sum_up, sum_qkv = [g.total() for g in (roi_sum, down_sum, up_sum, qkv_sum)]
        sum_roi, sum_out = sum_roi[:roi_rows], sum_roi[roi_rows:]
        sum_up = jnp.concatenate([sum_up[i * rows : (i + 1) * rows] for i in range(4)], axis=1)
    else:
        grads = [roi_halves[0][0, :roi_rows], roi_halves[0][0, roi_rows:], down_halves[0][0], qkv_halves[0][0]]
        grads.append(up_halves[0][0].reshape(4, width, width).swapaxes(0, 1).reshape(width, hidden))
        sum_roi, sum_out, sum_down, sum_qkv, sum_up = [
            lax.psum(lax.psum_scatter(grad, "shard", scatter_dimension=0, tiled=True), "dp").astype(F32) for grad in grads
        ]
    own = lax.dynamic_slice_in_dim(second, own_start, bn_gain.shape[0], 1)
    mean = sums[0] / tokens
    return (
        layer_out[None], roi_grad[None], sum_roi, own[1], own[0], sum_qkv, sum_out, own[2], own[3],
        sum_up, sum_down, own[4], own[5], mean, sums[1] / tokens - mean * mean,
    )


def solution(mesh):
    rows3, rows2, split2, split1 = P(("dp", "shard"), None, None), P(("dp", "shard"), None), P("shard", None), P("shard")
    return jax.shard_map(
        per_device,
        mesh=mesh,
        in_specs=(
            rows3, rows2, split2, split1, split1, split2, split2, split1, split1, split2, split2, split1, split1, rows3,
        ),
        out_specs=(
            rows3, rows3, split2, split1, split1, split2, split2, split1, split1, split2, split2, split1, split1, P(), P(),
        ),
        check_vma=False,
    )
```

profile of v0, /device:TPU:0, one launch (start us, length us, event | category | flops | bytes accessed | tf_op | source)
XLA Modules:
  0.0 300.4 jit_solution(4504780860617324752)
XLA Ops:
  0.7 3.0 collective-permute-start
  7.6 6.2 %collective-permute-done.refs_2_ = bf16[256,768]{1,0:T(8,128)(2,1)S(1)} collective-permute-done((bf16[256,768]{1,0:T(8,128)(2,1)}, bf16[256,768]{1,0:T(8,128)(2,1)S(1)}, u32[]{:S(2)}, u32[]{:S(2)}) %collective-permute-start) | collective-permute-done | bytes 393248 | tf_op jit(solution)/shard_map/ppermute | solution.py:38
  13.8 9.1 %collective-permute-done.1.refs_4_ = bf16[256,768]{1,0:T(8,128)(2,1)S(1)} collective-permute-done((bf16[256,768]{1,0:T(8,128)(2,1)}, bf16[256,768]{1,0:T(8,128)(2,1)S(1)}, u32[]{:S(2)}, u32[]{:S(2)}) %collective-permute-start.1) | collective-permute-done | bytes 393248 | tf_op jit(solution)/shard_map/ppermute | solution.py:38
  31.6 4.6 %project.1 = (f32[512,768]{1,0:T(8,128)S(1)}, f32[8,768]{1,0:T(8,128)S(1)}) custom-call(s32[8]{0:T(128)S(1)} %iota_xor_fusion.places, bf16[512,2048]{1,0:T(8,128)(2,1)S(1)} %bitcast.71, f32[8,768]{1,0:T(8,128)S(1)} %dynamic_update_slice.3.params_ref, bf16[256,768]{1,0:T(8,128)(2,1)} %refs_0_.5, bf16[256,768]{1,0:T(8,128)(2,1)} %copy-done.30, ...), custom_call_target="tpu_custom_call" | custom-call | flops 1024 | bytes 1024 | tf_op jit(solution)/shard_map/project/pallas_call | solution.py:245
  39.1 2.2 collective-permute-done.8
  41.4 2.6 collective-permute-start.9
  44.0 2.1 collective-permute-done.9
  46.1 4.6 %collective-permute-done.14.refs_4_ = bf16[96,3072]{1,0:T(8,128)(2,1)} collective-permute-done((bf16[96,3072]{1,0:T(8,128)(2,1)S(1)}, bf16[96,3072]{1,0:T(8,128)(2,1)}, u32[]{:S(2)}, u32[]{:S(2)}) %collective-permute-start.14) | collective-permute-done | bytes 589856 | tf_op jit(solution)/shard_map/ppermute | solution.py:38
  57.2 2.4 collective-permute-done.12
  61.6 11.9 %attend.1 = (bf16[2304,512]{1,0:T(8,128)(2,1)S(1)}, bf16[768,512]{1,0:T(8,128)(2,1)S(1)}, f32[12,512]{1,0:T(8,128)S(1)}) custom-call(s32[8]{0:T(128)S(1)} %iota_xor_fusion.places, f32[512,768]{1,0:T(8,128)S(1)} %get-tuple-element.141.projected_ref, f32[8,768]{1,0:T(8,128)S(1)} %add_add_fusion.1.sums_ref, s32[1,512]{1,0:T(1,128)S(1)} %copy-done.8, ...), custom_call_target="tpu_custom_call" | custom-call | flops 1024 | bytes 1024 | tf_op jit(solution)/shard_map/attend/pallas_call | solution.py:245
  79.3 2.7 collective-permute-done.25
  82.1 5.7 %collective-permute-done.26 = bf16[48,3072]{1,0:T(8,128)(2,1)S(1)} collective-permute-done((bf16[48,3072]{1,0:T(8,128)(2,1)S(1)}, bf16[48,3072]{1,0:T(8,128)(2,1)S(1)}, u32[]{:S(2)}, u32[]{:S(2)}) %collective-permute-start.26) | collective-permute-done | bytes 294944 | tf_op jit(solution)/shard_map/ppermute | solution.py:38
  91.6 14.7 %expand.1 = (f32[512,768]{1,0:T(8,128)S(1)}, f32[512,1]{1,0:T(8,128)S(1)}, bf16[512,3072]{1,0:T(8,128)(2,1)S(1)}, bf16[512,3072]{1,0:T(8,128)(2,1)S(1)}) custom-call(s32[8]{0:T(128)S(1)} %iota_xor_fusion.places, f32[512,768]{1,0:T(8,128)S(1)} %get-tuple-element.141.projected_ref, f32[8,768]{1,0:T(8,128)S(1)} %add_add_fusion.1.sums_ref, ...), custom_call_target="tpu_custom_call" | custom-call | flops 1024 | bytes 1024 | tf_op jit(solution)/shard_map/expand/pallas_call | solution.py:245
  109.4 5.9 %collective-permute-done.33 = bf16[192,768]{1,0:T(8,128)(2,1)S(1)} collective-permute-done((bf16[192,768]{1,0:T(8,128)(2,1)S(1)}, bf16[192,768]{1,0:T(8,128)(2,1)S(1)}, u32[]{:S(2)}, u32[]{:S(2)}) %collective-permute-start.33) | collective-permute-done | bytes 294944 | tf_op jit(solution)/shard_map/ppermute | solution.py:38
  119.2 11.0 %contract.1 = (bf16[4,384,768]{2,1,0:T(8,128)(2,1)S(1)}, bf16[4,384,768]{2,1,0:T(8,128)(2,1)S(1)}, bf16[512,768]{1,0:T(8,128)(2,1)}, f32[512,768]{1,0:T(8,128)S(1)}, f32[2,768]{1,0:T(2,128)S(1)}) custom-call(s32[8]{0:T(128)S(1)} %iota_xor_fusion.places, f32[512,768]{1,0:T(8,128)S(1)} %get-tuple-element.154.hat_ref, f32[8,768]{1,0:T(8,128)S(1)} %add_add_fusion.1.sums_ref, ...), custom_call_target="tpu_custom_call" | custom-call | flops 1024 | bytes 1024 | tf_op jit(solution)/shard_map/contract/pallas_call | solution.py:245
  130.4 12.4 %hidden_back.1 = (bf16[4,384,768]{2,1,0:T(8,128)(2,1)S(1)}, bf16[4,384,768]{2,1,0:T(8,128)(2,1)S(1)}, bf16[512,3072]{1,0:T(8,128)(2,1)S(1)}) custom-call(s32[8]{0:T(128)S(1)} %iota_xor_fusion.places, f32[512,768]{1,0:T(8,128)S(1)} %get-tuple-element.160.back_ref, f32[512,768]{1,0:T(8,128)S(1)} %get-tuple-element.154.hat_ref, ...), custom_call_target="tpu_custom_call" | custom-call | flops 1024 | bytes 1024 | tf_op jit(solution)/shard_map/hidden_back/pallas_call | solution.py:245
  145.4 12.7 %expand_back.1 = (f32[512,768]{1,0:T(8,128)S(1)}, bf16[512,768]{1,0:T(8,128)(2,1)S(1)}, bf16[768,512]{1,0:T(8,128)(2,1)S(1)}, f32[2,768]{1,0:T(2,128)S(1)}, bf16[1152,512]{1,0:T(8,128)(2,1)S(1)}) custom-call(s32[8]{0:T(128)S(1)} %iota_xor_fusion.places, f32[512,768]{1,0:T(8,128)S(1)} %get-tuple-element.160.back_ref, ...), custom_call_target="tpu_custom_call" | custom-call | flops 1024 | bytes 1024 | tf_op jit(solution)/shard_map/expand_back/pallas_call | solution.py:245
  164.9 8.2 %attend_back.1 = (bf16[2304,512]{1,0:T(8,128)(2,1)S(1)}, f32[512,768]{1,0:T(8,128)S(1)}, f32[2,768]{1,0:T(2,128)S(1)}) custom-call(s32[8]{0:T(128)S(1)} %iota_xor_fusion.places, bf16[2304,512]{1,0:T(8,128)(2,1)S(1)} %get-tuple-element.171.packed_ref, bf16[768,512]{1,0:T(8,128)(2,1)S(1)} %get-tuple-element.181.mixed_back_ref, ...), custom_call_target="tpu_custom_call" | custom-call | flops 1024 | bytes 1024 | tf_op jit(solution)/shard_map/attend_back/pallas_call | solution.py:245
  176.1 2.2 collective-permute-done.45
  178.4 2.6 collective-permute-start.46
  180.9 2.1 collective-permute-done.46
  189.7 5.9 %project_back.1 = (bf16[4,352,768]{2,1,0:T(8,128)(2,1)S(1)}, bf16[4,352,768]{2,1,0:T(8,128)(2,1)}, bf16[512,768]{1,0:T(8,128)(2,1)S(1)}) custom-call(s32[8]{0:T(128)S(1)} %iota_xor_fusion.places, f32[512,768]{1,0:T(8,128)S(1)} %get-tuple-element.192.embedded_ref, f32[512,768]{1,0:T(8,128)S(1)} %get-tuple-element.141.projected_ref, ...), custom_call_target="tpu_custom_call" | custom-call | flops 1024 | bytes 1024 | tf_op jit(solution)/shard_map/project_back/pallas_call | solution.py:245
  199.9 3.5 %collective-permute-start.55 = (bf16[384,768]{1,0:T(8,128)(2,1)S(1)}, bf16[384,768]{1,0:T(8,128)(2,1)S(1)}, u32[]{:S(2)}, u32[]{:S(2)}) collective-permute-start(bf16[384,768]{1,0:T(8,128)(2,1)S(1)} %pad_maximum_fusion.2), channel_id=1, source_target_pairs={{0,8},{24,16},{1,9},{25,17},{2,10},{26,18},{3,11},{27,19},{4,12},{... | collective-permute-start | bytes 1769480 | tf_op jit(solution)/shard_map/ppermute | solution.py:115
  205.1 3.9 %packed_gradient.1 = (bf16[4,96,2304]{2,1,0:T(8,128)(2,1)S(1)}, bf16[4,96,2304]{2,1,0:T(8,128)(2,1)S(1)}) custom-call(s32[8]{0:T(128)S(1)} %iota_xor_fusion.places, bf16[2304,512]{1,0:T(8,128)(2,1)S(1)} %copy-done.4, f32[512,768]{1,0:T(8,128)S(1)} %get-tuple-element.141.projected_ref, f32[8,768]{1,0:T(8,128)S(1)} %add_add_fusion.1.sums_ref), custom_call_target="tpu_custom_call" | custom-call | flops 1024 | bytes 1024 | tf_op jit(solution)/shard_map/packed_gradient/pallas_call | solution.py:245
  217.0 6.9 %input_gradient.1 = f32[512,2048]{1,0:T(8,128)} custom-call(s32[8]{0:T(128)S(1)} %iota_xor_fusion.places, bf16[512,768]{1,0:T(8,128)(2,1)S(1)} %get-tuple-element.205.low_ref, bf16[256,768]{1,0:T(8,128)(2,1)} %refs_0_.5, bf16[256,768]{1,0:T(8,128)(2,1)} %copy-done.30, bf16[256,768]{1,0:T(8,128)(2,1)} %copy-done.27, bf16[256,768]{1,0:T(8,128)(2,1)} %copy-done.31, ...), custom_call_target="tpu_custom_call" | custom-call | flops 1024 | bytes 1024 | tf_op jit(solution)/shard_map/input_gradient/pallas_call | solution.py:245
  234.4 4.1 %collective-permute-done.56 = bf16[176,768]{1,0:T(8,128)(2,1)S(1)} collective-permute-done((bf16[176,768]{1,0:T(8,128)(2,1)S(1)}, bf16[176,768]{1,0:T(8,128)(2,1)S(1)}, u32[]{:S(2)}, u32[]{:S(2)}) %collective-permute-start.56) | collective-permute-done | bytes 270368 | tf_op jit(solution)/shard_map/ppermute | solution.py:38
  241.2 7.5 %collective-permute-start.61 = (bf16[352,768]{1,0:T(8,128)(2,1)S(1)}, bf16[352,768]{1,0:T(8,128)(2,1)S(1)}, u32[]{:S(2)}, u32[]{:S(2)}) collective-permute-start(bf16[352,768]{1,0:T(8,128)(2,1)S(1)} %pad_maximum_fusion.4), channel_id=1, source_target_pairs={{0,8},{24,16},{1,9},{25,17},{2,10},{26,18},{3,11},{27,19},{4,12},{... | collective-permute-start | bytes 1622024 | tf_op jit(solution)/shard_map/ppermute | solution.py:115
  252.8 6.4 %collective-permute-done.61 = bf16[352,768]{1,0:T(8,128)(2,1)S(1)} collective-permute-done((bf16[352,768]{1,0:T(8,128)(2,1)S(1)}, bf16[352,768]{1,0:T(8,128)(2,1)S(1)}, u32[]{:S(2)}, u32[]{:S(2)}) %collective-permute-start.61) | collective-permute-done | bytes 540704 | tf_op jit(solution)/shard_map/ppermute | solution.py:115
  260.3 6.1 %collective-permute-start.69 = (bf16[96,2304]{1,0:T(8,128)(2,1)S(1)}, bf16[96,2304]{1,0:T(8,128)(2,1)S(1)}, u32[]{:S(2)}, u32[]{:S(2)}) collective-permute-start(bf16[96,2304]{1,0:T(8,128)(2,1)S(1)} %pad_maximum_fusion.5), channel_id=1, source_target_pairs={{0,8},{24,16},{1,9},{25,17},{2,10},{26,18},{3,11},{27,19},{4,12},{... | collective-permute-start | bytes 1327112 | tf_op jit(solution)/shard_map/ppermute | solution.py:115
  267.7 5.9 %collective-permute-done.69 = bf16[96,2304]{1,0:T(8,128)(2,1)S(1)} collective-permute-done((bf16[96,2304]{1,0:T(8,128)(2,1)S(1)}, bf16[96,2304]{1,0:T(8,128)(2,1)S(1)}, u32[]{:S(2)}, u32[]{:S(2)}) %collective-permute-start.69) | collective-permute-done | bytes 442400 | tf_op jit(solution)/shard_map/ppermute | solution.py:115
  278.4 15.9 %collective-permute-done.68 = bf16[352,768]{1,0:T(8,128)(2,1)S(1)} collective-permute-done((bf16[352,768]{1,0:T(8,128)(2,1)S(1)}, bf16[352,768]{1,0:T(8,128)(2,1)S(1)}, u32[]{:S(2)}, u32[]{:S(2)}) %collective-permute-start.68) | collective-permute-done | bytes 540704 | tf_op jit(solution)/shard_map/ppermute | solution.py:115
  296.1 3.4 %collective-permute-done.71 = bf16[96,2304]{1,0:T(8,128)(2,1)S(1)} collective-permute-done((bf16[96,2304]{1,0:T(8,128)(2,1)S(1)}, bf16[96,2304]{1,0:T(8,128)(2,1)S(1)}, u32[]{:S(2)}, u32[]{:S(2)}) %collective-permute-start.71) | collective-permute-done | bytes 442400 | tf_op jit(solution)/shard_map/ppermute | solution.py:115
  (277 shorter events, 100.1 us)
Async XLA Ops:
  0.7 13.2 %collective-permute-start = (bf16[256,768]{1,0:T(8,128)(2,1)}, bf16[256,768]{1,0:T(8,128)(2,1)S(1)}, u32[]{:S(2)}, u32[]{:S(2)}) collective-permute-start(bf16[256,768]{1,0:T(8,128)(2,1)} %refs_0_.5), channel_id=1, source_target_pairs={{0,2},{1,3},{2,0},{3,1},{4,6},{5,7},{6,4},{7,5},{8,10},{9,11},{10,... | collective-permute-start | bytes 1179656 | tf_op jit(solution)/shard_map/ppermute | solution.py:38
  3.7 19.2 %collective-permute-start.1 = (bf16[256,768]{1,0:T(8,128)(2,1)}, bf16[256,768]{1,0:T(8,128)(2,1)S(1)}, u32[]{:S(2)}, u32[]{:S(2)}) collective-permute-start(bf16[256,768]{1,0:T(8,128)(2,1)} %refs_0_.5), channel_id=1, source_target_pairs={{0,4},{1,5},{2,6},{3,7},{4,0},{5,1},{6,2},{7,3},{8,12},{9,13},{10,... | collective-permute-start | bytes 1179656 | tf_op jit(solution)/shard_map/ppermute | solution.py:38
  5.2 17.7 %collective-permute-start.2 = (bf16[256,768]{1,0:T(8,128)(2,1)}, bf16[256,768]{1,0:T(8,128)(2,1)S(1)}, u32[]{:S(2)}, u32[]{:S(2)}) collective-permute-start(bf16[256,768]{1,0:T(8,128)(2,1)} %refs_0_.5), channel_id=1, source_target_pairs={{0,6},{1,7},{2,4},{3,5},{4,2},{5,3},{6,0},{7,1},{8,14},{9,15},{10,... | collective-permute-start | bytes 1179656 | tf_op jit(solution)/shard_map/ppermute | solution.py:38
  23.5 22.6 %collective-permute-start.13 = (bf16[96,3072]{1,0:T(8,128)(2,1)S(1)}, bf16[96,3072]{1,0:T(8,128)(2,1)S(1)}, u32[]{:S(2)}, u32[]{:S(2)}) collective-permute-start(bf16[96,3072]{1,0:T(8,128)(2,1)S(1)} %pad_maximum_fusion.1.refs_0_), channel_id=1, source_target_pairs={{0,2},{1,3},{2,0},{3,1},{4,6},{5,7},{6,4},{7,5},{8,10},{9,11},{10,... | collective-permute-start | bytes 1769480 | tf_op jit(solution)/shard_map/ppermute | solution.py:38
  24.6 26.1 %collective-permute-start.14 = (bf16[96,3072]{1,0:T(8,128)(2,1)S(1)}, bf16[96,3072]{1,0:T(8,128)(2,1)}, u32[]{:S(2)}, u32[]{:S(2)}) collective-permute-start(bf16[96,3072]{1,0:T(8,128)(2,1)S(1)} %pad_maximum_fusion.1.refs_0_), channel_id=1, source_target_pairs={{0,4},{1,5},{2,6},{3,7},{4,0},{5,1},{6,2},{7,3},{8,12},{9,13},{10,... | collective-permute-start | bytes 1769480 | tf_op jit(solution)/shard_map/ppermute | solution.py:38
  25.5 27.0 %collective-permute-start.15 = (bf16[96,3072]{1,0:T(8,128)(2,1)S(1)}, bf16[96,3072]{1,0:T(8,128)(2,1)}, u32[]{:S(2)}, u32[]{:S(2)}) collective-permute-start(bf16[96,3072]{1,0:T(8,128)(2,1)S(1)} %pad_maximum_fusion.1.refs_0_), channel_id=1, source_target_pairs={{0,6},{1,7},{2,4},{3,5},{4,2},{5,3},{6,0},{7,1},{8,14},{9,15},{10,... | collective-permute-start | bytes 1769480 | tf_op jit(solution)/shard_map/ppermute | solution.py:38
  59.6 14.3 %collective-permute-start.21 = (bf16[96,3072]{1,0:T(8,128)(2,1)}, bf16[96,3072]{1,0:T(8,128)(2,1)}, u32[]{:S(2)}, u32[]{:S(2)}) collective-permute-start(bf16[96,3072]{1,0:T(8,128)(2,1)} %refs_8_.3), channel_id=1, source_target_pairs={{0,2},{1,3},{2,0},{3,1},{4,6},{5,7},{6,4},{7,5},{8,10},{9,11},{10,... | collective-permute-start | bytes 1769480 | tf_op jit(solution)/shard_map/ppermute | solution.py:38
  60.2 14.0 %collective-permute-start.22 = (bf16[96,3072]{1,0:T(8,128)(2,1)}, bf16[96,3072]{1,0:T(8,128)(2,1)}, u32[]{:S(2)}, u32[]{:S(2)}) collective-permute-start(bf16[96,3072]{1,0:T(8,128)(2,1)} %refs_8_.3), channel_id=1, source_target_pairs={{0,4},{1,5},{2,6},{3,7},{4,0},{5,1},{6,2},{7,3},{8,12},{9,13},{10,... | collective-permute-start | bytes 1769480 | tf_op jit(solution)/shard_map/ppermute | solution.py:38
  87.9 18.4 %collective-permute-start.29 = (bf16[384,768]{1,0:T(8,128)(2,1)S(1)}, bf16[384,768]{1,0:T(8,128)(2,1)S(1)}, u32[]{:S(2)}, u32[]{:S(2)}) collective-permute-start(bf16[384,768]{1,0:T(8,128)(2,1)S(1)} %copy-done.16), channel_id=1, source_target_pairs={{0,2},{1,3},{2,0},{3,1},{4,6},{5,7},{6,4},{7,5},{8,10},{9,11},{10,... | collective-permute-start | bytes 1769480 | tf_op jit(solution)/shard_map/ppermute | solution.py:38
  88.5 17.8 %collective-permute-start.30 = (bf16[384,768]{1,0:T(8,128)(2,1)S(1)}, bf16[384,768]{1,0:T(8,128)(2,1)S(1)}, u32[]{:S(2)}, u32[]{:S(2)}) collective-permute-start(bf16[384,768]{1,0:T(8,128)(2,1)S(1)} %copy-done.16), channel_id=1, source_target_pairs={{0,4},{1,5},{2,6},{3,7},{4,0},{5,1},{6,2},{7,3},{8,12},{9,13},{10,... | collective-permute-start | bytes 1769480 | tf_op jit(solution)/shard_map/ppermute | solution.py:38
  130.2 13.0 %collective-permute-start.37 = (bf16[4,384,768]{2,1,0:T(8,128)(2,1)S(1)}, bf16[4,384,768]{2,1,0:T(8,128)(2,1)S(1)}, u32[]{:S(2)}, u32[]{:S(2)}) collective-permute-start(bf16[4,384,768]{2,1,0:T(8,128)(2,1)S(1)} %get-tuple-element.165), channel_id=1, source_target_pairs={{0,1},{1,0},{2,3},{3,2},{4,5},{5,4},{6,7},{7,6},{8,9},{9,8},{10,11... | collective-permute-start | bytes 7077896 | tf_op jit(solution)/shard_map/ppermute | solution.py:38
  142.8 17.4 %collective-permute-start.36 = (bf16[4,384,768]{2,1,0:T(8,128)(2,1)S(1)}, bf16[4,384,768]{2,1,0:T(8,128)(2,1)S(1)}, u32[]{:S(2)}, u32[]{:S(2)}) collective-permute-start(bf16[4,384,768]{2,1,0:T(8,128)(2,1)S(1)} %get-tuple-element.163), channel_id=1, source_target_pairs={{0,1},{1,0},{2,3},{3,2},{4,5},{5,4},{6,7},{7,6},{8,9},{9,8},{10,11... | collective-permute-start | bytes 7077896 | tf_op jit(solution)/shard_map/ppermute | solution.py:38
  143.4 15.4 %collective-permute-start.39 = (bf16[2,192,768]{2,1,0:T(8,128)(2,1)S(1)}, bf16[2,192,768]{2,1,0:T(8,128)(2,1)S(1)}, u32[]{:S(2)}, u32[]{:S(2)}) collective-permute-start(bf16[2,192,768]{2,1,0:T(8,128)(2,1)S(1)} %add_convert_fusion.6), channel_id=1, source_target_pairs={{0,4},{1,5},{2,6},{3,7},{4,0},{5,1},{6,2},{7,3},{8,12},{9,13},{10,... | collective-permute-start | bytes 1769480 | tf_op jit(solution)/shard_map/ppermute | solution.py:38
  144.8 15.1 %collective-permute-start.38 = (bf16[2,192,768]{2,1,0:T(8,128)(2,1)S(1)}, bf16[2,192,768]{2,1,0:T(8,128)(2,1)S(1)}, u32[]{:S(2)}, u32[]{:S(2)}) collective-permute-start(bf16[2,192,768]{2,1,0:T(8,128)(2,1)S(1)} %add_convert_fusion.7), channel_id=1, source_target_pairs={{0,2},{1,3},{2,0},{3,1},{4,6},{5,7},{6,4},{7,5},{8,10},{9,11},{10,... | collective-permute-start | bytes 1769480 | tf_op jit(solution)/shard_map/ppermute | solution.py:38
  162.3 20.8 %collective-permute-start.41 = (bf16[2,192,768]{2,1,0:T(8,128)(2,1)S(1)}, bf16[2,192,768]{2,1,0:T(8,128)(2,1)S(1)}, u32[]{:S(2)}, u32[]{:S(2)}) collective-permute-start(bf16[2,192,768]{2,1,0:T(8,128)(2,1)S(1)} %add_convert_fusion.4), channel_id=1, source_target_pairs={{0,4},{1,5},{2,6},{3,7},{4,0},{5,1},{6,2},{7,3},{8,12},{9,13},{10,... | collective-permute-start | bytes 1769480 | tf_op jit(solution)/shard_map/ppermute | solution.py:38
  163.2 19.9 %collective-permute-start.40 = (bf16[2,192,768]{2,1,0:T(8,128)(2,1)S(1)}, bf16[2,192,768]{2,1,0:T(8,128)(2,1)S(1)}, u32[]{:S(2)}, u32[]{:S(2)}) collective-permute-start(bf16[2,192,768]{2,1,0:T(8,128)(2,1)S(1)} %add_convert_fusion.5), channel_id=1, source_target_pairs={{0,2},{1,3},{2,0},{3,1},{4,6},{5,7},{6,4},{7,5},{8,10},{9,11},{10,... | collective-permute-start | bytes 1769480 | tf_op jit(solution)/shard_map/ppermute | solution.py:38
  197.6 15.5 %collective-permute-start.47 = (bf16[192,768]{1,0:T(8,128)(2,1)}, bf16[192,768]{1,0:T(8,128)(2,1)S(1)}, u32[]{:S(2)}, u32[]{:S(2)}) collective-permute-start(bf16[192,768]{1,0:T(8,128)(2,1)} %get-tuple-element.264), channel_id=1, source_target_pairs={{0,4},{1,5},{2,6},{3,7},{4,0},{5,1},{6,2},{7,3},{8,12},{9,13},{10,... | collective-permute-start | bytes 884744 | tf_op jit(solution)/shard_map/ppermute | solution.py:38
  198.4 15.7 %collective-permute-start.48 = (bf16[192,768]{1,0:T(8,128)(2,1)S(1)}, bf16[192,768]{1,0:T(8,128)(2,1)S(1)}, u32[]{:S(2)}, u32[]{:S(2)}) collective-permute-start(bf16[192,768]{1,0:T(8,128)(2,1)S(1)} %get-tuple-element.263), channel_id=1, source_target_pairs={{0,2},{1,3},{2,0},{3,1},{4,6},{5,7},{6,4},{7,5},{8,10},{9,11},{10,... | collective-permute-start | bytes 884744 | tf_op jit(solution)/shard_map/ppermute | solution.py:38
  199.9 24.0 %collective-permute-start.55 = (bf16[384,768]{1,0:T(8,128)(2,1)S(1)}, bf16[384,768]{1,0:T(8,128)(2,1)S(1)}, u32[]{:S(2)}, u32[]{:S(2)}) collective-permute-start(bf16[384,768]{1,0:T(8,128)(2,1)S(1)} %pad_maximum_fusion.2), channel_id=1, source_target_pairs={{0,8},{24,16},{1,9},{25,17},{2,10},{26,18},{3,11},{27,19},{4,12},{... | collective-permute-start | bytes 1769480 | tf_op jit(solution)/shard_map/ppermute | solution.py:115
  209.0 19.8 %collective-permute-start.60 = (bf16[4,96,2304]{2,1,0:T(8,128)(2,1)S(1)}, bf16[4,96,2304]{2,1,0:T(8,128)(2,1)S(1)}, u32[]{:S(2)}, u32[]{:S(2)}) collective-permute-start(bf16[4,96,2304]{2,1,0:T(8,128)(2,1)S(1)} %get-tuple-element.209), channel_id=1, source_target_pairs={{0,1},{1,0},{2,3},{3,2},{4,5},{5,4},{6,7},{7,6},{8,9},{9,8},{10,11... | collective-permute-start | bytes 5308424 | tf_op jit(solution)/shard_map/ppermute | solution.py:38
  212.1 14.7 %collective-permute-start.54 = (bf16[2,176,768]{2,1,0:T(8,128)(2,1)S(1)}, bf16[2,176,768]{2,1,0:T(8,128)(2,1)S(1)}, u32[]{:S(2)}, u32[]{:S(2)}) collective-permute-start(bf16[2,176,768]{2,1,0:T(8,128)(2,1)S(1)} %add_convert_fusion.10), channel_id=1, source_target_pairs={{0,4},{1,5},{2,6},{3,7},{4,0},{5,1},{6,2},{7,3},{8,12},{9,13},{10,... | collective-permute-start | bytes 1622024 | tf_op jit(solution)/shard_map/ppermute | solution.py:38
  213.2 14.5 %collective-permute-start.53 = (bf16[2,176,768]{2,1,0:T(8,128)(2,1)S(1)}, bf16[2,176,768]{2,1,0:T(8,128)(2,1)S(1)}, u32[]{:S(2)}, u32[]{:S(2)}) collective-permute-start(bf16[2,176,768]{2,1,0:T(8,128)(2,1)S(1)} %add_convert_fusion.11), channel_id=1, source_target_pairs={{0,2},{1,3},{2,0},{3,1},{4,6},{5,7},{6,4},{7,5},{8,10},{9,11},{10,... | collective-permute-start | bytes 1622024 | tf_op jit(solution)/shard_map/ppermute | solution.py:38
  215.7 16.4 %collective-permute-start.59 = (bf16[384,768]{1,0:T(8,128)(2,1)S(1)}, bf16[384,768]{1,0:T(8,128)(2,1)S(1)}, u32[]{:S(2)}, u32[]{:S(2)}) collective-permute-start(bf16[384,768]{1,0:T(8,128)(2,1)S(1)} %pad_maximum_fusion.3), channel_id=1, source_target_pairs={{0,8},{24,16},{1,9},{25,17},{2,10},{26,18},{3,11},{27,19},{4,12},{... | collective-permute-start | bytes 1769480 | tf_op jit(solution)/shard_map/ppermute | solution.py:115
  230.8 17.9 %collective-permute-start.64 = (bf16[2,48,2304]{2,1,0:T(8,128)(2,1)S(1)}, bf16[2,48,2304]{2,1,0:T(8,128)(2,1)S(1)}, u32[]{:S(2)}, u32[]{:S(2)}) collective-permute-start(bf16[2,48,2304]{2,1,0:T(8,128)(2,1)S(1)} %add_convert_fusion.14), channel_id=1, source_target_pairs={{0,4},{1,5},{2,6},{3,7},{4,0},{5,1},{6,2},{7,3},{8,12},{9,13},{10,... | collective-permute-start | bytes 1327112 | tf_op jit(solution)/shard_map/ppermute | solution.py:38
  232.2 16.6 %collective-permute-start.63 = (bf16[2,48,2304]{2,1,0:T(8,128)(2,1)S(1)}, bf16[2,48,2304]{2,1,0:T(8,128)(2,1)S(1)}, u32[]{:S(2)}, u32[]{:S(2)}) collective-permute-start(bf16[2,48,2304]{2,1,0:T(8,128)(2,1)S(1)} %add_convert_fusion.15), channel_id=1, source_target_pairs={{0,2},{1,3},{2,0},{3,1},{4,6},{5,7},{6,4},{7,5},{8,10},{9,11},{10,... | collective-permute-start | bytes 1327112 | tf_op jit(solution)/shard_map/ppermute | solution.py:38
  233.5 17.8 %collective-permute-start.62 = (bf16[384,768]{1,0:T(8,128)(2,1)S(1)}, bf16[384,768]{1,0:T(8,128)(2,1)S(1)}, u32[]{:S(2)}, u32[]{:S(2)}) collective-permute-start(bf16[384,768]{1,0:T(8,128)(2,1)S(1)} %add_convert_fusion.2), channel_id=1, source_target_pairs={{8,16},{16,8},{9,17},{17,9},{10,18},{18,10},{11,19},{19,11},{12,20... | collective-permute-start | bytes 1769480 | tf_op jit(solution)/shard_map/ppermute | solution.py:115
  238.6 27.9 %collective-permute-start.73 = (bf16[384,768]{1,0:T(8,128)(2,1)S(1)}, bf16[384,768]{1,0:T(8,128)(2,1)S(1)}, u32[]{:S(2)}, u32[]{:S(2)}) collective-permute-start(bf16[384,768]{1,0:T(8,128)(2,1)S(1)} %add_convert_fusion.1), channel_id=1, source_target_pairs={{8,0},{16,24},{9,1},{17,25},{10,2},{18,26},{11,3},{19,27},{12,4},{... | collective-permute-start | bytes 1769480 | tf_op jit(solution)/shard_map/ppermute | solution.py:115
  241.2 18.0 %collective-permute-start.61 = (bf16[352,768]{1,0:T(8,128)(2,1)S(1)}, bf16[352,768]{1,0:T(8,128)(2,1)S(1)}, u32[]{:S(2)}, u32[]{:S(2)}) collective-permute-start(bf16[352,768]{1,0:T(8,128)(2,1)S(1)} %pad_maximum_fusion.4), channel_id=1, source_target_pairs={{0,8},{24,16},{1,9},{25,17},{2,10},{26,18},{3,11},{27,19},{4,12},{... | collective-permute-start | bytes 1622024 | tf_op jit(solution)/shard_map/ppermute | solution.py:115
  251.5 22.9 %collective-permute-start.72 = (bf16[384,768]{1,0:T(8,128)(2,1)S(1)}, bf16[384,768]{1,0:T(8,128)(2,1)S(1)}, u32[]{:S(2)}, u32[]{:S(2)}) collective-permute-start(bf16[384,768]{1,0:T(8,128)(2,1)S(1)} %add_convert_fusion), channel_id=1, source_target_pairs={{8,0},{16,24},{9,1},{17,25},{10,2},{18,26},{11,3},{19,27},{12,4},{... | collective-permute-start | bytes 1769480 | tf_op jit(solution)/shard_map/ppermute | solution.py:115
  260.3 13.2 %collective-permute-start.69 = (bf16[96,2304]{1,0:T(8,128)(2,1)S(1)}, bf16[96,2304]{1,0:T(8,128)(2,1)S(1)}, u32[]{:S(2)}, u32[]{:S(2)}) collective-permute-start(bf16[96,2304]{1,0:T(8,128)(2,1)S(1)} %pad_maximum_fusion.5), channel_id=1, source_target_pairs={{0,8},{24,16},{1,9},{25,17},{2,10},{26,18},{3,11},{27,19},{4,12},{... | collective-permute-start | bytes 1327112 | tf_op jit(solution)/shard_map/ppermute | solution.py:115
  274.6 19.7 %collective-permute-start.68 = (bf16[352,768]{1,0:T(8,128)(2,1)S(1)}, bf16[352,768]{1,0:T(8,128)(2,1)S(1)}, u32[]{:S(2)}, u32[]{:S(2)}) collective-permute-start(bf16[352,768]{1,0:T(8,128)(2,1)S(1)} %add_convert_fusion.8), channel_id=1, source_target_pairs={{8,0},{16,24},{9,1},{17,25},{10,2},{18,26},{11,3},{19,27},{12,4},{... | collective-permute-start | bytes 1622024 | tf_op jit(solution)/shard_map/ppermute | solution.py:115
  276.0 23.4 %collective-permute-start.71 = (bf16[96,2304]{1,0:T(8,128)(2,1)S(1)}, bf16[96,2304]{1,0:T(8,128)(2,1)S(1)}, u32[]{:S(2)}, u32[]{:S(2)}) collective-permute-start(bf16[96,2304]{1,0:T(8,128)(2,1)S(1)} %add_convert_fusion.12), channel_id=1, source_target_pairs={{8,0},{16,24},{9,1},{17,25},{10,2},{18,26},{11,3},{19,27},{12,4},{... | collective-permute-start | bytes 1327112 | tf_op jit(solution)/shard_map/ppermute | solution.py:115
  (81 other events, 604.8 us)
where the time goes:
time: 301 us; the launch traced here: 300 us
  waiting for transfers between devices  98.2 us (33%)
  Pallas kernels  92.1 us (31%)
  starting transfers between devices  78.5 us (26%)
  local copies, waits for them, and re-layouts  15.3 us (5%)
  other arithmetic  14.6 us (5%)
    pallas_call x10, Pallas kernels, call(): pl.pallas_call(kernel, in_specs=[pl.BlockSpec(memory_space=space) for spa...  92.1 us
    ppermute x62, waiting for transfers between devices, swap(): return lax.ppermute(values, axis, [(i, i ^ step) for i in range(size)])  66.6 us
    ppermute x62, starting transfers between devices, swap(): return lax.ppermute(values, axis, [(i, i ^ step) for i in range(size)])  52.1 us
    ppermute x12, waiting for transfers between devices, step(): self.came = lax.ppermute(self.part, 'dp', self.pairs[self.number])  31.6 us
    ppermute x12, starting transfers between devices, step(): self.came = lax.ppermute(self.part, 'dp', self.pairs[self.number])  26.4 us
    convert_element_type x24, other arithmetic, add_low(): return total.astype(LOW)  9.14 us
    unnamed x80, local copies, waits for them, and re-layouts  8.04 us
  transfers between devices with their start and end apart: 74, of which 33 were waited for; matrix products, arithmetic and copies ran while one was open for 7% of the time, Pallas kernels for 25%

commit v1 on v0

--- a/solution.py
+++ b/solution.py
@@ -160,6 +160,16 @@
     return copies
 
 
+def wait_chunk(count, copies, places, target, sems, c):
+    if count == 1:
+        return c
+    rows = target.shape[0] // 8
+    for k in range(2):
+        at = target.at[part(places[2 * c + k], rows)]
+        pltpu.make_async_copy(at, at, sems.at[2 * c + k]).wait()
+    return places[2 * c] >> 1
+
+
 def put_blocks(halves, places, values, columns, work, section=0):
     if len(halves) == 1:
         halves[0][0, part(section, values.shape[0]), columns] = values.astype(LOW)
@@ -233,13 +243,15 @@
     return math.prod(array.shape) * jnp.dtype(array.dtype).itemsize
 
 
-def call(kernel, args, outs, scratch, name, spare=6, far=(), near=(), out_near=(), sems=()):
-    spaces = [pltpu.HBM if i in far else pltpu.VMEM for i in range(len(args))]
+def call(kernel, args, outs, scratch, name, spare=6, far=(), loose=(), near=(), out_near=(), sems=()):
+    spaces = [pl.ANY if i in loose else pltpu.HBM if i in far else pltpu.VMEM for i in range(len(args))]
     spaces[0] = pltpu.SMEM
     held = [a for i, a in enumerate(args) if i and i not in far and i not in near]
     held += [a for i, a in enumerate(outs) if i not in out_near] + list(scratch)
     args = [
-        pltpu.with_memory_space_constraint(a, pltpu.HBM if i in far else pltpu.VMEM) if i in far or i in near else a
+        pltpu.with_memory_space_constraint(a, pltpu.HBM if i in far else pltpu.VMEM)
+        if (i in far and i not in loose) or i in near
+        else a
         for i, a in enumerate(args)
     ]
     return pl.pallas_call(
@@ -263,14 +275,15 @@
 
 
 def project_kernel(count, places, x_ref, params_ref, *refs):
-    pieces, (out_ref, sums_ref, weight, sems) = refs[:count], refs[count:]
-    wait_all(start_all(piece_copies(pieces, places, weight, sems)))
+    pieces, (out_ref, sums_ref, weight, x, sems, sems_x) = refs[:count], refs[count:]
+    copies = start_all([pltpu.make_async_copy(x_ref, x, sems_x.at[0])])
+    wait_all(start_all(piece_copies(pieces, places, weight, sems)) + copies)
     sums_ref[...] = params_ref[...]
 
     @pl.loop(0, out_ref.shape[1] // TILE)
     def _(n):
         cols = part(n, TILE)
-        values = dot(x_ref[...], weight[:, cols])
+        values = dot(x[...], weight[:, cols])
         out_ref[:, cols] = values
         sums_ref[0:1, cols] = column_sum(values)
         sums_ref[1:2, cols] = column_sum(values * values)
@@ -316,10 +329,10 @@
 
 
 def expand_kernel(count, tokens, places, projected_ref, sums_ref, mixed_ref, *refs):
-    pieces, ups, refs = refs[:count], refs[count : 2 * count], refs[2 * count :]
+    ups, refs = refs[:count], refs[count:]
     hat_out, inv_out, active_out, slope_out, weight_out, weight_up, low_one, sems_out, sems_up = refs
     length, width = projected_ref.shape
-    copies_out = start_all(piece_copies(pieces, places, weight_out, sems_out, pl.ds(3 * width, width)))
+    copies_out = start_all(piece_copies(ups, places, weight_out, sems_out, pl.ds(4 * width, width)))
 
     def fetch(c):
         return piece_copies(ups, places, weight_up, sems_up.at[c], part(c, width), part(c, width))
@@ -346,29 +359,33 @@
             slope_out[:, cols] = slope.astype(LOW)
 
 
-def contract_kernel(count, places, hat_ref, sums_ref, grad_ref, active_ref, *refs):
+def contract_kernel(count, places, hat_ref, sums_ref, active_ref, grad_ref, *refs):
     pieces, refs = refs[:count], refs[count:]
-    halves, (layer_out, back_out, grads_out, weight, branch, low_back, sems) = refs[:-7], refs[-7:]
+    halves, refs = refs[:-9], refs[-9:]
+    layer_out, back_out, grads_out, weight, branch, low_back, grad, sems, sems_grad = refs
     length, width = hat_ref.shape
     copies = start_all(piece_copies(pieces, places, weight, sems))
+    grad_copy = start_all([pltpu.make_async_copy(grad_ref, grad, sems_grad.at[0])])
+    if count == 1:
+        wait_all(copies)
 
     @functools.partial(by_rows, length)
     def _(rows):
         branch[rows, :] = hat_ref[rows, :] * sums_ref[4:5, :] + sums_ref[5:6, :]
 
-    wait_all(copies)
-
     @pl.loop(0, 4)
-    def _(c):
+    def _(i):
+        c = wait_chunk(count, copies, places, weight, sems, i)
         branch[...] += dot(active_ref[:, part(c, width)], weight[part(c, width), :])
 
+    wait_all(grad_copy)
     grads_out[...] = jnp.zeros_like(grads_out)
 
     @functools.partial(by_rows, length)
     def _(rows):
         hat, inv = normalize(branch[rows, :])
         layer_out[rows, :] = (hat * sums_ref[6:7, :] + sums_ref[7:8, :]).astype(LOW)
-        gradient = grad_ref[rows, :].astype(F32)
+        gradient = grad[rows, :].astype(F32)
         grads_out[0:1, :] += column_sum(gradient * hat)
         grads_out[1:2, :] += column_sum(gradient)
         back = normalize_back(gradient * sums_ref[6:7, :], hat, inv)
@@ -389,10 +406,12 @@
         low_back[rows, :] = back_ref[rows, :].astype(LOW)
         low_one[:, rows] = (hat_ref[rows, :] * sums_ref[4:5, :] + sums_ref[5:6, :]).T.astype(LOW)
 
-    wait_all(copies)
+    if count == 1:
+        wait_all(copies)
 
     @pl.loop(0, 4)
-    def _(c):
+    def _(i):
+        c = wait_chunk(count, copies, places, weight, sems, i)
         for n in range(width // TILE):
             cols = part(c * (width // TILE) + n, TILE)
             values = (dot(low_back[...], weight[cols, :], 1, 1) * slope_ref[:, cols].astype(F32)).astype(LOW)
@@ -423,7 +442,7 @@
 def expand_back_kernel(
     count, places, back_ref, hat_ref, inv_ref, sums_ref, hidden_ref, packed_ref, lse_ref, doc_row, doc_col, *refs
 ):
-    pieces, ups, refs = refs[:count], refs[count : 2 * count], refs[2 * count :]
+    ups, refs = refs[:count], refs[count:]
     (
         first_out, low_out, mixed_back_out, grads_out, grad_packed_out, weight_out, weight_up, total, sems_out, sems_up
     ) = refs
@@ -434,7 +453,7 @@
 
     for c in range(4):
         start_all(fetch(c))
-    copies_out = start_all(piece_copies(pieces, places, weight_out, sems_out, pl.ds(3 * width, width)))
+    copies_out = start_all(piece_copies(ups, places, weight_out, sems_out, pl.ds(4 * width, width)))
     total[...] = back_ref[...]
 
     @pl.loop(0, 4)
@@ -493,9 +512,15 @@
         grads_out[1:2, cols] = column_sum(values * normed)
 
 
-def packed_gradient_kernel(tokens, places, grad_packed_ref, projected_ref, sums_ref, *refs):
-    halves, (low, work) = refs[:-2], refs[-2:]
+def packed_gradient_kernel(tokens, places, projected_ref, sums_ref, grad_packed_ref, *refs):
+    halves, (low, work, grad_packed, sems) = refs[:-4], refs[-4:]
     length, width = projected_ref.shape
+
+    def fetch(c):
+        return pltpu.make_async_copy(grad_packed_ref.at[part(c, width)], grad_packed.at[part(c, width)], sems.at[c])
+
+    for c in range(3):
+        fetch(c).start()
 
     @functools.partial(by_rows, length)
     def _(rows):
@@ -503,13 +528,15 @@
 
     @pl.loop(0, 3)
     def _(c):
+        fetch(c).wait()
         for n in range(width // TILE):
             cols = part(c * (width // TILE) + n, TILE)
-            put_blocks(halves, places, dot(low[...], grad_packed_ref[cols, :], 1, 1), cols, work.at[n % 2])
+            put_blocks(halves, places, dot(low[...], grad_packed[cols, :], 1, 1), cols, work.at[n % 2])
 
 
 def project_back_kernel(tokens, places, embedded_ref, projected_ref, sums_ref, grads_ref, mixed_ref, low_ref, x_ref, *refs):
-    halves, (low_out, work) = refs[:-2], refs[-2:]
+    halves, (low_out, work, x, sems) = refs[:-4], refs[-4:]
+    copies = start_all([pltpu.make_async_copy(x_ref, x, sems.at[0])])
     mean, _, inv = batch_scale(sums_ref, tokens)
     roi_rows = x_ref.shape[1] * halves[0].shape[1] // (x_ref.shape[1] + low_ref.shape[1])
 
@@ -519,7 +546,8 @@
         shift = grads_ref[0:1, :] * (1.0 / tokens) + normed * (grads_ref[1:2, :] * (1.0 / tokens))
         low_out[rows, :] = (sums_ref[2:3, :] * inv * (embedded_ref[rows, :] - shift)).astype(LOW)
 
-    row_blocks(halves, places, lambda at, n: dot(x_ref[:, lanes(at, n)], low_out[...], 0, 0), roi_rows)
+    wait_all(copies)
+    row_blocks(halves, places, lambda at, n: dot(x[:, lanes(at, n)], low_out[...], 0, 0), roi_rows)
     work[...] = dot(mixed_ref[...], low_ref[...]).astype(LOW)
     if len(halves) == 1:
         halves[0][0, roi_rows:, :] = work[...]
@@ -576,12 +604,12 @@
     params = lax.dynamic_update_slice(jnp.zeros((8, width), F32), own_params, (2, own_start))
 
     gather = functools.partial(lax.all_gather, axis_name="shard", axis=0, tiled=True)
-    wide = jnp.concatenate([w_qkv, w_out], axis=1)
+    wide_up = jnp.concatenate([w_up, w_out], axis=1)
     if direct:
         roi_chips = [w_roi, *sides(w_roi), swap(w_roi, ACROSS | ALONG)]
-        wide = tie(wide, params)
-        wide_chips = [wide, *sides(wide), swap(wide, ACROSS | ALONG)]
-        roi_pieces = with_cores(tie(roi_chips, wide))
+        w_qkv = tie(w_qkv, params, wide_up)
+        qkv_chips = [w_qkv, *sides(w_qkv), swap(w_qkv, ACROSS | ALONG)]
+        roi_pieces = with_cores(tie(roi_chips, w_qkv))
     else:
         roi_pieces = [gather(w_roi)]
     count = len(roi_pieces)
@@ -596,67 +624,71 @@
         functools.partial(project_kernel, count),
         [places, x, params, *roi_pieces],
         [shape((length, width)), shape((8, width))],
-        [low(roi_width, width)],
+        [low(roi_width, width), low(length, roi_width)],
         "project",
         out_near=(0,),
-        far=range(3, 100),
-        sems=((8,),),
+        far=(1, *range(3, 100)),
+        sems=((8,), (1,)),
+        loose=(2 + count,),
     )
     if direct:
         sums = sums + swap(sums, CORE)
         sums = sums + swap(sums, 1, "dp")
         sums = sums + swap(sums, 2, "dp")
         around = [swap(sums, ACROSS), swap(sums, ALONG), swap(sums, ACROSS | ALONG)]
-        wide_chips = tie(wide_chips, sums)
-        around = tie(around, wide_chips)
+        qkv_chips = tie(qkv_chips, sums)
+        around = tie(around, qkv_chips)
         sums = (sums + around[0]) + (around[1] + around[2])
-        wide_pieces = with_cores(wide_chips)
-        up_sides = sides(tie(w_up, sums))
+        qkv_pieces = with_cores(qkv_chips)
+        up_sides = sides(tie(wide_up, sums))
     else:
         sums = lax.psum(sums, ("dp", "shard"))
-        wide_pieces = [gather(wide)]
+        qkv_pieces = [gather(w_qkv)]
 
     heads = width // HEAD_DIM
     part_width = heads // 2 * HEAD_DIM
     packed_qkv, mixed, lse = call(
         functools.partial(attend_kernel, count, tokens),
-        [places, projected, sums, doc_row, doc_col, *wide_pieces],
+        [places, projected, sums, doc_row, doc_col, *qkv_pieces],
         [shape((3 * width, length), LOW), shape((width, length), LOW), shape((heads, length))],
         [low(width, 3 * width), low(length, width)],
         "attend",
         near=(1,), out_near=(0, 1, 2),
         far=range(5, 100),
         sems=((3, 8),),
+        loose=(4 + count,),
     )
     if direct:
         up_sides = tie(up_sides, mixed)
         up_corner = jnp.concatenate(corner_halves(*up_sides))
         down_sides = sides(tie(w_down, up_sides))
-        up_pieces = with_cores([w_up, *up_sides, up_corner])
+        up_pieces = with_cores([wide_up, *up_sides, up_corner])
     else:
-        up_pieces, down_parts = [gather(w_up)], [gather(w_down)]
+        up_pieces, down_parts = [gather(wide_up)], [gather(w_down)]
     hat, inv, active, slope = call(
         functools.partial(expand_kernel, count, tokens),
-        [places, projected, sums, mixed, *wide_pieces, *up_pieces],
+        [places, projected, sums, mixed, *up_pieces],
         [shape((length, width)), shape((length, 1)), shape((length, hidden), LOW), shape((length, hidden), LOW)],
         [low(width, width), low(width, hidden), low(length, width)],
         "expand",
         near=(1, 3), out_near=(0, 1, 2, 3),
         far=range(4, 100),
         sems=((8,), (4, 8)),
+        loose=(3 + count,),
     )
     if direct:
         down_sides = tie(down_sides, active)
         down_parts = with_cores([w_down, *down_sides, jnp.concatenate(corner_halves(*down_sides))])
     *down_halves, layer_out, back, grads_two = call(
         functools.partial(contract_kernel, count),
-        [places, hat, sums, cotangent.reshape(length, width), active, *down_parts],
+        [places, hat, sums, active, cotangent.reshape(length, width), *down_parts],
         blocks(hidden // shards, width) + [shape((length, width), LOW), shape((length, width)), shape((2, width))],
-        [low(hidden, width), pltpu.VMEM((length, width), F32), low(length, width)],
+        [low(hidden, width), pltpu.VMEM((length, width), F32), low(length, width), low(length, width)],
         "contract",
-        near=(1, 4), out_near=(cores + 1,),
-        far=range(5, 100),
-        sems=((8,),),
+        near=(1, 3), out_near=(cores + 1,),
+        far=range(4, 100),
+        sems=((8,), (1,)),
+        loose=(4 + count,),
     )
     down = OwnedSum(down_halves)
     *up_halves, grad_hidden = call(
@@ -674,8 +706,7 @@
     first, low_first, mixed_back, grads_one, grad_part = call(
         functools.partial(expand_back_kernel, count),
         [
-            tie(places, sent), back, hat, inv, sums, grad_hidden, packed_qkv, lse, doc_row, doc_col,
-            *wide_pieces, *up_pieces,
+            tie(places, sent), back, hat, inv, sums, grad_hidden, packed_qkv, lse, doc_row, doc_col, *up_pieces,
         ],
         [
             shape((length, width)), shape((length, width), LOW), shape((width, length), LOW), shape((2, width)),
@@ -693,7 +724,7 @@
         functools.partial(attend_back_kernel, count, tokens),
         [
             tie(places, sent), packed_qkv, mixed_back, lse, doc_row, doc_col, projected, sums, first, grad_part,
-            *wide_pieces,
+            *qkv_pieces,
         ],
         [shape((3 * width, length), LOW), shape((length, width)), shape((2, width))],
         [low(width, 3 * width)],
@@ -720,19 +751,23 @@
         functools.partial(project_back_kernel, tokens),
         [places, grad_embedded, projected, sums, second, mixed, low_first, x],
         blocks(roi_rows + out_rows, width) + [shape((length, width), LOW)],
-        [low(width, width)],
+        [low(width, width), low(length, roi_width)],
         "project_back",
         near=(1, 2, 5, 6), out_near=(cores,),
+        far=(8,),
+        sems=((1,),),
     )
     roi = OwnedSum(roi_halves)
     start_packed = tie(places, low_projected)
     qkv_halves = call(
         functools.partial(packed_gradient_kernel, tokens),
-        [start_packed, grad_packed, projected, sums],
+        [start_packed, projected, sums, grad_packed],
         blocks(width // shards, 3 * width),
-        [low(width, length), pltpu.VMEM((2, width, TILE), LOW)],
+        [low(width, length), pltpu.VMEM((2, width, TILE), LOW), low(3 * width, length)],
         "packed_gradient",
-        near=(1, 2),
+        near=(1,),
+        far=(3,),
+        sems=((3,),),
     )
     qkv = OwnedSum(qkv_halves)
     sent = roi.plane_one(qkv_halves)

time: 301 us -> 290 us (0.963)
  waiting for transfers between devices: 98.2 us -> 93.2 us
    ppermute x62, waiting for transfers between devices: 66.6 us -> 61 us  [swap(): return lax.ppermute(values, axis, [(i, i ^ step) for i in range(size)])]
    unnamed x80 -> x79, local copies, waits for them, and re-layouts: 8.04 us -> 5.16 us
  transfers between devices with their start and end apart: 74 -> 74, of which waited for: 33 -> 29; matrix products, arithmetic and copies ran while one was open for 7% -> 7% of each run, Pallas kernels for 25% -> 26%
where the time goes in v1:
time: 290 us
  waiting for transfers between devices  93.2 us (32%)
  Pallas kernels  89.9 us (31%)
  starting transfers between devices  78.9 us (27%)
  other arithmetic  13.5 us (5%)
  local copies, waits for them, and re-layouts  12.4 us (4%)
    pallas_call x10, Pallas kernels, call(): pl.pallas_call(kernel, in_specs=[pl.BlockSpec(memory_space=space) for spa...  89.9 us
    ppermute x62, waiting for transfers between devices, swap(): return lax.ppermute(values, axis, [(i, i ^ step) for i in range(size)])  61 us
    ppermute x62, starting transfers between devices, swap(): return lax.ppermute(values, axis, [(i, i ^ step) for i in range(size)])  52 us
    ppermute x12, waiting for transfers between devices, step(): self.came = lax.ppermute(self.part, 'dp', self.pairs[self.number])  32.2 us
    ppermute x12, starting transfers between devices, step(): self.came = lax.ppermute(self.part, 'dp', self.pairs[self.number])  26.9 us
    convert_element_type x24, other arithmetic, add_low(): return total.astype(LOW)  9.14 us
  transfers between devices with their start and end apart: 74, of which 29 were waited for; matrix products, arithmetic and copies ran while one was open for 7% of the time, Pallas kernels for 26%

profile of v1, /device:TPU:0, one launch (start us, length us, event | category | flops | bytes accessed | tf_op | source)
XLA Modules:
  0.0 289.5 jit_solution(3940864406388017555)
XLA Ops:
  0.7 3.0 %collective-permute-start = (bf16[256,768]{1,0:T(8,128)(2,1)}, bf16[256,768]{1,0:T(8,128)(2,1)S(1)}, u32[]{:S(2)}, u32[]{:S(2)}) collective-permute-start(bf16[256,768]{1,0:T(8,128)(2,1)} %refs_0_.7), channel_id=1, source_target_pairs={{0,2},{1,3},{2,0},{3,1},{4,6},{5,7},{6,4},{7,5},{8,10},{9,11},{10,... | collective-permute-start | bytes 1179656 | tf_op jit(solution)/shard_map/ppermute | solution.py:38
  7.6 6.2 %collective-permute-done.refs_2_ = bf16[256,768]{1,0:T(8,128)(2,1)S(1)} collective-permute-done((bf16[256,768]{1,0:T(8,128)(2,1)}, bf16[256,768]{1,0:T(8,128)(2,1)S(1)}, u32[]{:S(2)}, u32[]{:S(2)}) %collective-permute-start) | collective-permute-done | bytes 393248 | tf_op jit(solution)/shard_map/ppermute | solution.py:38
  13.8 9.1 %collective-permute-done.1.refs_4_ = bf16[256,768]{1,0:T(8,128)(2,1)S(1)} collective-permute-done((bf16[256,768]{1,0:T(8,128)(2,1)}, bf16[256,768]{1,0:T(8,128)(2,1)S(1)}, u32[]{:S(2)}, u32[]{:S(2)}) %collective-permute-start.1) | collective-permute-done | bytes 393248 | tf_op jit(solution)/shard_map/ppermute | solution.py:38
  28.3 5.2 %project.1 = (f32[512,768]{1,0:T(8,128)S(1)}, f32[8,768]{1,0:T(8,128)S(1)}) custom-call(s32[8]{0:T(128)S(1)} %iota_xor_fusion.places, bf16[512,2048]{1,0:T(8,128)(2,1)} %bitcast.71, f32[8,768]{1,0:T(8,128)S(1)} %dynamic_update_slice.3.params_ref, bf16[256,768]{1,0:T(8,128)(2,1)} %refs_0_.7, bf16[256,768]{1,0:T(8,128)(2,1)} %copy-done.29, ...), custom_call_target="tpu_custom_call" | custom-call | flops 1024 | bytes 1024 | tf_op jit(solution)/shard_map/project/pallas_call | solution.py:257
  36.3 2.2 collective-permute-done.8
  38.6 2.6 collective-permute-start.9
  41.2 2.1 collective-permute-done.9
  48.3 2.0 collective-permute-done.12
  55.6 11.8 %attend.1 = (bf16[2304,512]{1,0:T(8,128)(2,1)S(1)}, bf16[768,512]{1,0:T(8,128)(2,1)S(1)}, f32[12,512]{1,0:T(8,128)S(1)}) custom-call(s32[8]{0:T(128)S(1)} %iota_xor_fusion.places, f32[512,768]{1,0:T(8,128)S(1)} %get-tuple-element.141.projected_ref, f32[8,768]{1,0:T(8,128)S(1)} %add_add_fusion.1.sums_ref, s32[1,512]{1,0:T(1,128)S(1)} %copy-done.9, ...), custom_call_target="tpu_custom_call" | custom-call | flops 1024 | bytes 1024 | tf_op jit(solution)/shard_map/attend/pallas_call | solution.py:257
  72.4 6.7 %collective-permute-done.25 = bf16[48,3840]{1,0:T(8,128)(2,1)S(1)} collective-permute-done((bf16[48,3840]{1,0:T(8,128)(2,1)S(1)}, bf16[48,3840]{1,0:T(8,128)(2,1)S(1)}, u32[]{:S(2)}, u32[]{:S(2)}) %collective-permute-start.25) | collective-permute-done | bytes 368672 | tf_op jit(solution)/shard_map/ppermute | solution.py:38
  79.2 3.1 %collective-permute-done.26 = bf16[48,3840]{1,0:T(8,128)(2,1)S(1)} collective-permute-done((bf16[48,3840]{1,0:T(8,128)(2,1)S(1)}, bf16[48,3840]{1,0:T(8,128)(2,1)S(1)}, u32[]{:S(2)}, u32[]{:S(2)}) %collective-permute-start.26) | collective-permute-done | bytes 368672 | tf_op jit(solution)/shard_map/ppermute | solution.py:38
  86.0 13.3 %expand.1 = (f32[512,768]{1,0:T(8,128)S(1)}, f32[512,1]{1,0:T(8,128)S(1)}, bf16[512,3072]{1,0:T(8,128)(2,1)S(1)}, bf16[512,3072]{1,0:T(8,128)(2,1)S(1)}) custom-call(s32[8]{0:T(128)S(1)} %iota_xor_fusion.places, f32[512,768]{1,0:T(8,128)S(1)} %get-tuple-element.141.projected_ref, f32[8,768]{1,0:T(8,128)S(1)} %add_add_fusion.1.sums_ref, ...), custom_call_target="tpu_custom_call" | custom-call | flops 1024 | bytes 1024 | tf_op jit(solution)/shard_map/expand/pallas_call | solution.py:257
  101.7 6.5 %collective-permute-done.33 = bf16[192,768]{1,0:T(8,128)(2,1)S(1)} collective-permute-done((bf16[192,768]{1,0:T(8,128)(2,1)S(1)}, bf16[192,768]{1,0:T(8,128)(2,1)S(1)}, u32[]{:S(2)}, u32[]{:S(2)}) %collective-permute-start.33) | collective-permute-done | bytes 294944 | tf_op jit(solution)/shard_map/ppermute | solution.py:38
  110.9 10.0 %contract.1 = (bf16[4,384,768]{2,1,0:T(8,128)(2,1)S(1)}, bf16[4,384,768]{2,1,0:T(8,128)(2,1)S(1)}, bf16[512,768]{1,0:T(8,128)(2,1)}, f32[512,768]{1,0:T(8,128)S(1)}, f32[2,768]{1,0:T(2,128)S(1)}) custom-call(s32[8]{0:T(128)S(1)} %iota_xor_fusion.places, f32[512,768]{1,0:T(8,128)S(1)} %get-tuple-element.154.hat_ref, f32[8,768]{1,0:T(8,128)S(1)} %add_add_fusion.1.sums_ref, ...), custom_call_target="tpu_custom_call" | custom-call | flops 1024 | bytes 1024 | tf_op jit(solution)/shard_map/contract/pallas_call | solution.py:257
  121.0 11.3 %hidden_back.1 = (bf16[4,384,768]{2,1,0:T(8,128)(2,1)S(1)}, bf16[4,384,768]{2,1,0:T(8,128)(2,1)S(1)}, bf16[512,3072]{1,0:T(8,128)(2,1)S(1)}) custom-call(s32[8]{0:T(128)S(1)} %iota_xor_fusion.places, f32[512,768]{1,0:T(8,128)S(1)} %get-tuple-element.160.back_ref, f32[512,768]{1,0:T(8,128)S(1)} %get-tuple-element.154.hat_ref, ...), custom_call_target="tpu_custom_call" | custom-call | flops 1024 | bytes 1024 | tf_op jit(solution)/shard_map/hidden_back/pallas_call | solution.py:257
  135.2 12.7 %expand_back.1 = (f32[512,768]{1,0:T(8,128)S(1)}, bf16[512,768]{1,0:T(8,128)(2,1)S(1)}, bf16[768,512]{1,0:T(8,128)(2,1)S(1)}, f32[2,768]{1,0:T(2,128)S(1)}, bf16[1152,512]{1,0:T(8,128)(2,1)S(1)}) custom-call(s32[8]{0:T(128)S(1)} %iota_xor_fusion.places, f32[512,768]{1,0:T(8,128)S(1)} %get-tuple-element.160.back_ref, ...), custom_call_target="tpu_custom_call" | custom-call | flops 1024 | bytes 1024 | tf_op jit(solution)/shard_map/expand_back/pallas_call | solution.py:257
  154.3 8.2 %attend_back.1 = (bf16[2304,512]{1,0:T(8,128)(2,1)S(1)}, f32[512,768]{1,0:T(8,128)S(1)}, f32[2,768]{1,0:T(2,128)S(1)}) custom-call(s32[8]{0:T(128)S(1)} %iota_xor_fusion.places, bf16[2304,512]{1,0:T(8,128)(2,1)S(1)} %get-tuple-element.171.packed_ref, bf16[768,512]{1,0:T(8,128)(2,1)S(1)} %get-tuple-element.181.mixed_back_ref, ...), custom_call_target="tpu_custom_call" | custom-call | flops 1024 | bytes 1024 | tf_op jit(solution)/shard_map/attend_back/pallas_call | solution.py:257
  165.5 2.2 collective-permute-done.45
  167.8 2.6 collective-permute-start.46
  170.4 2.1 collective-permute-done.46
  177.4 2.3 collective-permute-done.51
  179.7 6.0 %project_back.1 = (bf16[4,352,768]{2,1,0:T(8,128)(2,1)S(1)}, bf16[4,352,768]{2,1,0:T(8,128)(2,1)}, bf16[512,768]{1,0:T(8,128)(2,1)S(1)}) custom-call(s32[8]{0:T(128)S(1)} %iota_xor_fusion.places, f32[512,768]{1,0:T(8,128)S(1)} %get-tuple-element.192.embedded_ref, f32[512,768]{1,0:T(8,128)S(1)} %get-tuple-element.141.projected_ref, ...), custom_call_target="tpu_custom_call" | custom-call | flops 1024 | bytes 1024 | tf_op jit(solution)/shard_map/project_back/pallas_call | solution.py:257
  189.5 3.5 %collective-permute-start.55 = (bf16[384,768]{1,0:T(8,128)(2,1)S(1)}, bf16[384,768]{1,0:T(8,128)(2,1)S(1)}, u32[]{:S(2)}, u32[]{:S(2)}) collective-permute-start(bf16[384,768]{1,0:T(8,128)(2,1)S(1)} %pad_maximum_fusion.1), channel_id=1, source_target_pairs={{0,8},{24,16},{1,9},{25,17},{2,10},{26,18},{3,11},{27,19},{4,12},{... | collective-permute-start | bytes 1769480 | tf_op jit(solution)/shard_map/ppermute | solution.py:115
  193.0 4.5 %packed_gradient.1 = (bf16[4,96,2304]{2,1,0:T(8,128)(2,1)S(1)}, bf16[4,96,2304]{2,1,0:T(8,128)(2,1)S(1)}) custom-call(s32[8]{0:T(128)S(1)} %iota_xor_fusion.places, f32[512,768]{1,0:T(8,128)S(1)} %get-tuple-element.141.projected_ref, f32[8,768]{1,0:T(8,128)S(1)} %add_add_fusion.1.sums_ref, bf16[2304,512]{1,0:T(8,128)(2,1)} %copy-done.4), custom_call_target="tpu_custom_call" | custom-call | flops 1024 | bytes 1024 | tf_op jit(solution)/shard_map/packed_gradient/pallas_call | solution.py:257
  206.2 6.9 %input_gradient.1 = f32[512,2048]{1,0:T(8,128)} custom-call(s32[8]{0:T(128)S(1)} %iota_xor_fusion.places, bf16[512,768]{1,0:T(8,128)(2,1)S(1)} %get-tuple-element.205.low_ref, bf16[256,768]{1,0:T(8,128)(2,1)} %refs_0_.7, bf16[256,768]{1,0:T(8,128)(2,1)} %copy-done.29, bf16[256,768]{1,0:T(8,128)(2,1)} %copy-done.26, bf16[256,768]{1,0:T(8,128)(2,1)} %copy-done.30, ...), custom_call_target="tpu_custom_call" | custom-call | flops 1024 | bytes 1024 | tf_op jit(solution)/shard_map/input_gradient/pallas_call | solution.py:257
  223.1 4.1 %collective-permute-done.56 = bf16[176,768]{1,0:T(8,128)(2,1)S(1)} collective-permute-done((bf16[176,768]{1,0:T(8,128)(2,1)S(1)}, bf16[176,768]{1,0:T(8,128)(2,1)S(1)}, u32[]{:S(2)}, u32[]{:S(2)}) %collective-permute-start.56) | collective-permute-done | bytes 270368 | tf_op jit(solution)/shard_map/ppermute | solution.py:38
  229.9 8.0 %collective-permute-start.61 = (bf16[352,768]{1,0:T(8,128)(2,1)S(1)}, bf16[352,768]{1,0:T(8,128)(2,1)S(1)}, u32[]{:S(2)}, u32[]{:S(2)}) collective-permute-start(bf16[352,768]{1,0:T(8,128)(2,1)S(1)} %pad_maximum_fusion.3), channel_id=1, source_target_pairs={{0,8},{24,16},{1,9},{25,17},{2,10},{26,18},{3,11},{27,19},{4,12},{... | collective-permute-start | bytes 1622024 | tf_op jit(solution)/shard_map/ppermute | solution.py:115
  241.3 7.0 %collective-permute-done.61 = bf16[352,768]{1,0:T(8,128)(2,1)S(1)} collective-permute-done((bf16[352,768]{1,0:T(8,128)(2,1)S(1)}, bf16[352,768]{1,0:T(8,128)(2,1)S(1)}, u32[]{:S(2)}, u32[]{:S(2)}) %collective-permute-start.61) | collective-permute-done | bytes 540704 | tf_op jit(solution)/shard_map/ppermute | solution.py:115
  249.5 6.1 %collective-permute-start.69 = (bf16[96,2304]{1,0:T(8,128)(2,1)S(1)}, bf16[96,2304]{1,0:T(8,128)(2,1)S(1)}, u32[]{:S(2)}, u32[]{:S(2)}) collective-permute-start(bf16[96,2304]{1,0:T(8,128)(2,1)S(1)} %pad_maximum_fusion.4), channel_id=1, source_target_pairs={{0,8},{24,16},{1,9},{25,17},{2,10},{26,18},{3,11},{27,19},{4,12},{... | collective-permute-start | bytes 1327112 | tf_op jit(solution)/shard_map/ppermute | solution.py:115
  256.8 5.9 %collective-permute-done.69 = bf16[96,2304]{1,0:T(8,128)(2,1)S(1)} collective-permute-done((bf16[96,2304]{1,0:T(8,128)(2,1)S(1)}, bf16[96,2304]{1,0:T(8,128)(2,1)S(1)}, u32[]{:S(2)}, u32[]{:S(2)}) %collective-permute-start.69) | collective-permute-done | bytes 442400 | tf_op jit(solution)/shard_map/ppermute | solution.py:115
  267.6 15.9 %collective-permute-done.68 = bf16[352,768]{1,0:T(8,128)(2,1)S(1)} collective-permute-done((bf16[352,768]{1,0:T(8,128)(2,1)S(1)}, bf16[352,768]{1,0:T(8,128)(2,1)S(1)}, u32[]{:S(2)}, u32[]{:S(2)}) %collective-permute-start.68) | collective-permute-done | bytes 540704 | tf_op jit(solution)/shard_map/ppermute | solution.py:115
  285.2 3.4 %collective-permute-done.71 = bf16[96,2304]{1,0:T(8,128)(2,1)S(1)} collective-permute-done((bf16[96,2304]{1,0:T(8,128)(2,1)S(1)}, bf16[96,2304]{1,0:T(8,128)(2,1)S(1)}, u32[]{:S(2)}, u32[]{:S(2)}) %collective-permute-start.71) | collective-permute-done | bytes 442400 | tf_op jit(solution)/shard_map/ppermute | solution.py:115
  (276 shorter events, 91.1 us)
Async XLA Ops:
  3.7 19.2 %collective-permute-start.1 = (bf16[256,768]{1,0:T(8,128)(2,1)}, bf16[256,768]{1,0:T(8,128)(2,1)S(1)}, u32[]{:S(2)}, u32[]{:S(2)}) collective-permute-start(bf16[256,768]{1,0:T(8,128)(2,1)} %refs_0_.7), channel_id=1, source_target_pairs={{0,4},{1,5},{2,6},{3,7},{4,0},{5,1},{6,2},{7,3},{8,12},{9,13},{10,... | collective-permute-start | bytes 1179656 | tf_op jit(solution)/shard_map/ppermute | solution.py:38
  5.2 17.7 %collective-permute-start.2 = (bf16[256,768]{1,0:T(8,128)(2,1)}, bf16[256,768]{1,0:T(8,128)(2,1)S(1)}, u32[]{:S(2)}, u32[]{:S(2)}) collective-permute-start(bf16[256,768]{1,0:T(8,128)(2,1)} %refs_0_.7), channel_id=1, source_target_pairs={{0,6},{1,7},{2,4},{3,5},{4,2},{5,3},{6,0},{7,1},{8,14},{9,15},{10,... | collective-permute-start | bytes 1179656 | tf_op jit(solution)/shard_map/ppermute | solution.py:38
  24.0 21.5 %collective-permute-start.13 = (bf16[96,2304]{1,0:T(8,128)(2,1)S(1)}, bf16[96,2304]{1,0:T(8,128)(2,1)}, u32[]{:S(2)}, u32[]{:S(2)}) collective-permute-start(bf16[96,2304]{1,0:T(8,128)(2,1)S(1)} %copy-done.23), channel_id=1, source_target_pairs={{0,2},{1,3},{2,0},{3,1},{4,6},{5,7},{6,4},{7,5},{8,10},{9,11},{10,... | collective-permute-start | bytes 1327112 | tf_op jit(solution)/shard_map/ppermute | solution.py:38
  25.2 21.6 %collective-permute-start.14 = (bf16[96,2304]{1,0:T(8,128)(2,1)S(1)}, bf16[96,2304]{1,0:T(8,128)(2,1)}, u32[]{:S(2)}, u32[]{:S(2)}) collective-permute-start(bf16[96,2304]{1,0:T(8,128)(2,1)S(1)} %copy-done.23), channel_id=1, source_target_pairs={{0,4},{1,5},{2,6},{3,7},{4,0},{5,1},{6,2},{7,3},{8,12},{9,13},{10,... | collective-permute-start | bytes 1327112 | tf_op jit(solution)/shard_map/ppermute | solution.py:38
  26.2 20.7 %collective-permute-start.15 = (bf16[96,2304]{1,0:T(8,128)(2,1)S(1)}, bf16[96,2304]{1,0:T(8,128)(2,1)}, u32[]{:S(2)}, u32[]{:S(2)}) collective-permute-start(bf16[96,2304]{1,0:T(8,128)(2,1)S(1)} %copy-done.23), channel_id=1, source_target_pairs={{0,6},{1,7},{2,4},{3,5},{4,2},{5,3},{6,0},{7,1},{8,14},{9,15},{10,... | collective-permute-start | bytes 1327112 | tf_op jit(solution)/shard_map/ppermute | solution.py:38
  50.2 17.2 %collective-permute-start.21 = (bf16[96,3840]{1,0:T(8,128)(2,1)S(1)}, bf16[96,3840]{1,0:T(8,128)(2,1)}, u32[]{:S(2)}, u32[]{:S(2)}) collective-permute-start(bf16[96,3840]{1,0:T(8,128)(2,1)S(1)} %constant_dynamic-update-slice_fusion.refs_0_), channel_id=1, source_target_pairs={{0,2},{1,3},{2,0},{3,1},{4,6},{5,7},{6,4},{7,5},{8,10},{9,11},{10,... | collective-permute-start | bytes 2211848 | tf_op jit(solution)/shard_map/ppermute | solution.py:38
  51.7 15.8 %collective-permute-start.22 = (bf16[96,3840]{1,0:T(8,128)(2,1)S(1)}, bf16[96,3840]{1,0:T(8,128)(2,1)}, u32[]{:S(2)}, u32[]{:S(2)}) collective-permute-start(bf16[96,3840]{1,0:T(8,128)(2,1)S(1)} %constant_dynamic-update-slice_fusion.refs_0_), channel_id=1, source_target_pairs={{0,4},{1,5},{2,6},{3,7},{4,0},{5,1},{6,2},{7,3},{8,12},{9,13},{10,... | collective-permute-start | bytes 2211848 | tf_op jit(solution)/shard_map/ppermute | solution.py:38
  69.7 13.7 %collective-permute-start.20 = (bf16[96,3840]{1,0:T(8,128)(2,1)S(1)}, bf16[96,3840]{1,0:T(8,128)(2,1)S(1)}, u32[]{:S(2)}, u32[]{:S(2)}) collective-permute-start(bf16[96,3840]{1,0:T(8,128)(2,1)S(1)} %constant_dynamic-update-slice_fusion.refs_0_), channel_id=1, source_target_pairs={{0,1},{1,0},{2,3},{3,2},{4,5},{5,4},{6,7},{7,6},{8,9},{9,8},{10,11... | collective-permute-start | bytes 2211848 | tf_op jit(solution)/shard_map/ppermute | solution.py:38
  70.7 14.2 %collective-permute-start.23 = (bf16[96,3840]{1,0:T(8,128)(2,1)}, bf16[96,3840]{1,0:T(8,128)(2,1)S(1)}, u32[]{:S(2)}, u32[]{:S(2)}) collective-permute-start(bf16[96,3840]{1,0:T(8,128)(2,1)} %collective-permute-done.21.refs_2_), channel_id=1, source_target_pairs={{0,1},{1,0},{2,3},{3,2},{4,5},{5,4},{6,7},{7,6},{8,9},{9,8},{10,11... | collective-permute-start | bytes 2211848 | tf_op jit(solution)/shard_map/ppermute | solution.py:38
  71.2 13.6 %collective-permute-start.24 = (bf16[96,3840]{1,0:T(8,128)(2,1)}, bf16[96,3840]{1,0:T(8,128)(2,1)S(1)}, u32[]{:S(2)}, u32[]{:S(2)}) collective-permute-start(bf16[96,3840]{1,0:T(8,128)(2,1)} %collective-permute-done.22.refs_4_), channel_id=1, source_target_pairs={{0,1},{1,0},{2,3},{3,2},{4,5},{5,4},{6,7},{7,6},{8,9},{9,8},{10,11... | collective-permute-start | bytes 2211848 | tf_op jit(solution)/shard_map/ppermute | solution.py:38
  82.4 16.9 %collective-permute-start.29 = (bf16[384,768]{1,0:T(8,128)(2,1)S(1)}, bf16[384,768]{1,0:T(8,128)(2,1)S(1)}, u32[]{:S(2)}, u32[]{:S(2)}) collective-permute-start(bf16[384,768]{1,0:T(8,128)(2,1)S(1)} %copy-done.18), channel_id=1, source_target_pairs={{0,2},{1,3},{2,0},{3,1},{4,6},{5,7},{6,4},{7,5},{8,10},{9,11},{10,... | collective-permute-start | bytes 1769480 | tf_op jit(solution)/shard_map/ppermute | solution.py:38
  83.4 15.9 %collective-permute-start.30 = (bf16[384,768]{1,0:T(8,128)(2,1)S(1)}, bf16[384,768]{1,0:T(8,128)(2,1)S(1)}, u32[]{:S(2)}, u32[]{:S(2)}) collective-permute-start(bf16[384,768]{1,0:T(8,128)(2,1)S(1)} %copy-done.18), channel_id=1, source_target_pairs={{0,4},{1,5},{2,6},{3,7},{4,0},{5,1},{6,2},{7,3},{8,12},{9,13},{10,... | collective-permute-start | bytes 1769480 | tf_op jit(solution)/shard_map/ppermute | solution.py:38
  132.4 17.3 %collective-permute-start.36 = (bf16[4,384,768]{2,1,0:T(8,128)(2,1)S(1)}, bf16[4,384,768]{2,1,0:T(8,128)(2,1)S(1)}, u32[]{:S(2)}, u32[]{:S(2)}) collective-permute-start(bf16[4,384,768]{2,1,0:T(8,128)(2,1)S(1)} %get-tuple-element.163), channel_id=1, source_target_pairs={{0,1},{1,0},{2,3},{3,2},{4,5},{5,4},{6,7},{7,6},{8,9},{9,8},{10,11... | collective-permute-start | bytes 7077896 | tf_op jit(solution)/shard_map/ppermute | solution.py:38
  133.0 15.4 %collective-permute-start.39 = (bf16[2,192,768]{2,1,0:T(8,128)(2,1)S(1)}, bf16[2,192,768]{2,1,0:T(8,128)(2,1)S(1)}, u32[]{:S(2)}, u32[]{:S(2)}) collective-permute-start(bf16[2,192,768]{2,1,0:T(8,128)(2,1)S(1)} %add_convert_fusion.6), channel_id=1, source_target_pairs={{0,4},{1,5},{2,6},{3,7},{4,0},{5,1},{6,2},{7,3},{8,12},{9,13},{10,... | collective-permute-start | bytes 1769480 | tf_op jit(solution)/shard_map/ppermute | solution.py:38
  134.2 15.2 %collective-permute-start.38 = (bf16[2,192,768]{2,1,0:T(8,128)(2,1)S(1)}, bf16[2,192,768]{2,1,0:T(8,128)(2,1)S(1)}, u32[]{:S(2)}, u32[]{:S(2)}) collective-permute-start(bf16[2,192,768]{2,1,0:T(8,128)(2,1)S(1)} %add_convert_fusion.7), channel_id=1, source_target_pairs={{0,2},{1,3},{2,0},{3,1},{4,6},{5,7},{6,4},{7,5},{8,10},{9,11},{10,... | collective-permute-start | bytes 1769480 | tf_op jit(solution)/shard_map/ppermute | solution.py:38
  152.3 20.2 %collective-permute-start.41 = (bf16[2,192,768]{2,1,0:T(8,128)(2,1)S(1)}, bf16[2,192,768]{2,1,0:T(8,128)(2,1)S(1)}, u32[]{:S(2)}, u32[]{:S(2)}) collective-permute-start(bf16[2,192,768]{2,1,0:T(8,128)(2,1)S(1)} %add_convert_fusion.4), channel_id=1, source_target_pairs={{0,4},{1,5},{2,6},{3,7},{4,0},{5,1},{6,2},{7,3},{8,12},{9,13},{10,... | collective-permute-start | bytes 1769480 | tf_op jit(solution)/shard_map/ppermute | solution.py:38
  153.0 19.5 %collective-permute-start.40 = (bf16[2,192,768]{2,1,0:T(8,128)(2,1)S(1)}, bf16[2,192,768]{2,1,0:T(8,128)(2,1)S(1)}, u32[]{:S(2)}, u32[]{:S(2)}) collective-permute-start(bf16[2,192,768]{2,1,0:T(8,128)(2,1)S(1)} %add_convert_fusion.5), channel_id=1, source_target_pairs={{0,2},{1,3},{2,0},{3,1},{4,6},{5,7},{6,4},{7,5},{8,10},{9,11},{10,... | collective-permute-start | bytes 1769480 | tf_op jit(solution)/shard_map/ppermute | solution.py:38
  187.8 14.0 %collective-permute-start.47 = (bf16[192,768]{1,0:T(8,128)(2,1)}, bf16[192,768]{1,0:T(8,128)(2,1)S(1)}, u32[]{:S(2)}, u32[]{:S(2)}) collective-permute-start(bf16[192,768]{1,0:T(8,128)(2,1)} %get-tuple-element.264), channel_id=1, source_target_pairs={{0,4},{1,5},{2,6},{3,7},{4,0},{5,1},{6,2},{7,3},{8,12},{9,13},{10,... | collective-permute-start | bytes 884744 | tf_op jit(solution)/shard_map/ppermute | solution.py:38
  188.3 15.0 %collective-permute-start.48 = (bf16[192,768]{1,0:T(8,128)(2,1)S(1)}, bf16[192,768]{1,0:T(8,128)(2,1)S(1)}, u32[]{:S(2)}, u32[]{:S(2)}) collective-permute-start(bf16[192,768]{1,0:T(8,128)(2,1)S(1)} %get-tuple-element.263), channel_id=1, source_target_pairs={{0,2},{1,3},{2,0},{3,1},{4,6},{5,7},{6,4},{7,5},{8,10},{9,11},{10,... | collective-permute-start | bytes 884744 | tf_op jit(solution)/shard_map/ppermute | solution.py:38
  189.5 23.6 %collective-permute-start.55 = (bf16[384,768]{1,0:T(8,128)(2,1)S(1)}, bf16[384,768]{1,0:T(8,128)(2,1)S(1)}, u32[]{:S(2)}, u32[]{:S(2)}) collective-permute-start(bf16[384,768]{1,0:T(8,128)(2,1)S(1)} %pad_maximum_fusion.1), channel_id=1, source_target_pairs={{0,8},{24,16},{1,9},{25,17},{2,10},{26,18},{3,11},{27,19},{4,12},{... | collective-permute-start | bytes 1769480 | tf_op jit(solution)/shard_map/ppermute | solution.py:115
  197.6 20.0 %collective-permute-start.60 = (bf16[4,96,2304]{2,1,0:T(8,128)(2,1)S(1)}, bf16[4,96,2304]{2,1,0:T(8,128)(2,1)S(1)}, u32[]{:S(2)}, u32[]{:S(2)}) collective-permute-start(bf16[4,96,2304]{2,1,0:T(8,128)(2,1)S(1)} %get-tuple-element.209), channel_id=1, source_target_pairs={{0,1},{1,0},{2,3},{3,2},{4,5},{5,4},{6,7},{7,6},{8,9},{9,8},{10,11... | collective-permute-start | bytes 5308424 | tf_op jit(solution)/shard_map/ppermute | solution.py:38
  200.6 14.7 %collective-permute-start.54 = (bf16[2,176,768]{2,1,0:T(8,128)(2,1)S(1)}, bf16[2,176,768]{2,1,0:T(8,128)(2,1)S(1)}, u32[]{:S(2)}, u32[]{:S(2)}) collective-permute-start(bf16[2,176,768]{2,1,0:T(8,128)(2,1)S(1)} %add_convert_fusion.10), channel_id=1, source_target_pairs={{0,4},{1,5},{2,6},{3,7},{4,0},{5,1},{6,2},{7,3},{8,12},{9,13},{10,... | collective-permute-start | bytes 1622024 | tf_op jit(solution)/shard_map/ppermute | solution.py:38
  201.9 14.5 %collective-permute-start.53 = (bf16[2,176,768]{2,1,0:T(8,128)(2,1)S(1)}, bf16[2,176,768]{2,1,0:T(8,128)(2,1)S(1)}, u32[]{:S(2)}, u32[]{:S(2)}) collective-permute-start(bf16[2,176,768]{2,1,0:T(8,128)(2,1)S(1)} %add_convert_fusion.11), channel_id=1, source_target_pairs={{0,2},{1,3},{2,0},{3,1},{4,6},{5,7},{6,4},{7,5},{8,10},{9,11},{10,... | collective-permute-start | bytes 1622024 | tf_op jit(solution)/shard_map/ppermute | solution.py:38
  204.9 16.5 %collective-permute-start.59 = (bf16[384,768]{1,0:T(8,128)(2,1)S(1)}, bf16[384,768]{1,0:T(8,128)(2,1)S(1)}, u32[]{:S(2)}, u32[]{:S(2)}) collective-permute-start(bf16[384,768]{1,0:T(8,128)(2,1)S(1)} %pad_maximum_fusion.2), channel_id=1, source_target_pairs={{0,8},{24,16},{1,9},{25,17},{2,10},{26,18},{3,11},{27,19},{4,12},{... | collective-permute-start | bytes 1769480 | tf_op jit(solution)/shard_map/ppermute | solution.py:115
  219.7 18.2 %collective-permute-start.64 = (bf16[2,48,2304]{2,1,0:T(8,128)(2,1)S(1)}, bf16[2,48,2304]{2,1,0:T(8,128)(2,1)S(1)}, u32[]{:S(2)}, u32[]{:S(2)}) collective-permute-start(bf16[2,48,2304]{2,1,0:T(8,128)(2,1)S(1)} %add_convert_fusion.14), channel_id=1, source_target_pairs={{0,4},{1,5},{2,6},{3,7},{4,0},{5,1},{6,2},{7,3},{8,12},{9,13},{10,... | collective-permute-start | bytes 1327112 | tf_op jit(solution)/shard_map/ppermute | solution.py:38
  221.4 16.6 %collective-permute-start.63 = (bf16[2,48,2304]{2,1,0:T(8,128)(2,1)S(1)}, bf16[2,48,2304]{2,1,0:T(8,128)(2,1)S(1)}, u32[]{:S(2)}, u32[]{:S(2)}) collective-permute-start(bf16[2,48,2304]{2,1,0:T(8,128)(2,1)S(1)} %add_convert_fusion.15), channel_id=1, source_target_pairs={{0,2},{1,3},{2,0},{3,1},{4,6},{5,7},{6,4},{7,5},{8,10},{9,11},{10,... | collective-permute-start | bytes 1327112 | tf_op jit(solution)/shard_map/ppermute | solution.py:38
  222.2 17.6 %collective-permute-start.62 = (bf16[384,768]{1,0:T(8,128)(2,1)S(1)}, bf16[384,768]{1,0:T(8,128)(2,1)S(1)}, u32[]{:S(2)}, u32[]{:S(2)}) collective-permute-start(bf16[384,768]{1,0:T(8,128)(2,1)S(1)} %add_convert_fusion.2), channel_id=1, source_target_pairs={{8,16},{16,8},{9,17},{17,9},{10,18},{18,10},{11,19},{19,11},{12,20... | collective-permute-start | bytes 1769480 | tf_op jit(solution)/shard_map/ppermute | solution.py:115
  227.2 28.4 %collective-permute-start.73 = (bf16[384,768]{1,0:T(8,128)(2,1)S(1)}, bf16[384,768]{1,0:T(8,128)(2,1)S(1)}, u32[]{:S(2)}, u32[]{:S(2)}) collective-permute-start(bf16[384,768]{1,0:T(8,128)(2,1)S(1)} %add_convert_fusion.1), channel_id=1, source_target_pairs={{8,0},{16,24},{9,1},{17,25},{10,2},{18,26},{11,3},{19,27},{12,4},{... | collective-permute-start | bytes 1769480 | tf_op jit(solution)/shard_map/ppermute | solution.py:115
  229.9 18.5 %collective-permute-start.61 = (bf16[352,768]{1,0:T(8,128)(2,1)S(1)}, bf16[352,768]{1,0:T(8,128)(2,1)S(1)}, u32[]{:S(2)}, u32[]{:S(2)}) collective-permute-start(bf16[352,768]{1,0:T(8,128)(2,1)S(1)} %pad_maximum_fusion.3), channel_id=1, source_target_pairs={{0,8},{24,16},{1,9},{25,17},{2,10},{26,18},{3,11},{27,19},{4,12},{... | collective-permute-start | bytes 1622024 | tf_op jit(solution)/shard_map/ppermute | solution.py:115
  240.0 23.5 %collective-permute-start.72 = (bf16[384,768]{1,0:T(8,128)(2,1)S(1)}, bf16[384,768]{1,0:T(8,128)(2,1)S(1)}, u32[]{:S(2)}, u32[]{:S(2)}) collective-permute-start(bf16[384,768]{1,0:T(8,128)(2,1)S(1)} %add_convert_fusion), channel_id=1, source_target_pairs={{8,0},{16,24},{9,1},{17,25},{10,2},{18,26},{11,3},{19,27},{12,4},{... | collective-permute-start | bytes 1769480 | tf_op jit(solution)/shard_map/ppermute | solution.py:115
  263.7 19.7 %collective-permute-start.68 = (bf16[352,768]{1,0:T(8,128)(2,1)S(1)}, bf16[352,768]{1,0:T(8,128)(2,1)S(1)}, u32[]{:S(2)}, u32[]{:S(2)}) collective-permute-start(bf16[352,768]{1,0:T(8,128)(2,1)S(1)} %add_convert_fusion.8), channel_id=1, source_target_pairs={{8,0},{16,24},{9,1},{17,25},{10,2},{18,26},{11,3},{19,27},{12,4},{... | collective-permute-start | bytes 1622024 | tf_op jit(solution)/shard_map/ppermute | solution.py:115
  265.2 23.4 %collective-permute-start.71 = (bf16[96,2304]{1,0:T(8,128)(2,1)S(1)}, bf16[96,2304]{1,0:T(8,128)(2,1)S(1)}, u32[]{:S(2)}, u32[]{:S(2)}) collective-permute-start(bf16[96,2304]{1,0:T(8,128)(2,1)S(1)} %add_convert_fusion.12), channel_id=1, source_target_pairs={{8,0},{16,24},{9,1},{17,25},{10,2},{18,26},{11,3},{19,27},{12,4},{... | collective-permute-start | bytes 1327112 | tf_op jit(solution)/shard_map/ppermute | solution.py:115
  (80 other events, 649.5 us)

commit v2 on v1

--- a/solution.py
+++ b/solution.py
@@ -774,18 +774,22 @@
     if direct:
         up_sum = LineSum(up.plane_done(sent))
         sent = up_sum.step()
-    (roi_grad,) = call(
-        functools.partial(input_gradient_kernel, count),
-        [tie(places, sent), low_projected, *roi_pieces],
-        [shape((length, roi_width))],
-        [low(roi_width, width)],
-        "input_gradient",
-        near=(1,),
-        far=range(2, 100),
-        sems=((8,),),
-    )
+    def input_gradient(*sent):
+        return call(
+            functools.partial(input_gradient_kernel, count),
+            [tie(places, *sent), low_projected, *roi_pieces],
+            [shape((length, roi_width))],
+            [low(roi_width, width)],
+            "input_gradient",
+            near=(1,),
+            far=range(2, 100),
+            sems=((8,),),
+        )[0]
+
     if direct:
-        sent = roi.plane_two(down_sum.step(roi_grad))
+        sent = down_sum.step(sent)
+        sent = roi_grad = input_gradient(sent)
+        sent = roi.plane_two(sent)
         sent = qkv.plane_one(sent)
         sent = down_sum.step(up_sum.step(sent))
         roi_sum = LineSum(roi.plane_done(sent))
@@ -802,6 +806,7 @@
         sum_roi, sum_out = sum_roi[:roi_rows], sum_roi[roi_rows:]
         sum_up = jnp.concatenate([sum_up[i * rows : (i + 1) * rows] for i in range(4)], axis=1)
     else:
+        roi_grad = input_gradient()
         grads = [roi_halves[0][0, :roi_rows], roi_halves[0][0, roi_rows:], down_halves[0][0], qkv_halves[0][0]]
         grads.append(up_halves[0][0].reshape(4, width, width).swapaxes(0, 1).reshape(width, hidden))
         sum_roi, sum_out, sum_down, sum_qkv, sum_up = [

time: 290 us -> 282 us (0.972)
  waiting for transfers between devices: 93.2 us -> 86.3 us
    ppermute x12, waiting for transfers between devices: 32.2 us -> 24 us  [step(): self.came = lax.ppermute(self.part, 'dp', self.pairs[self.number])]
  transfers between devices with their start and end apart: 74 -> 74, of which waited for: 29 -> 31; matrix products, arithmetic and copies ran while one was open for 7% -> 7% of each run, Pallas kernels for 26% -> 26%
where the time goes in v2:
time: 282 us; the launch traced here: 281 us
  Pallas kernels  89.9 us (32%)
  waiting for transfers between devices  86.3 us (31%)
  starting transfers between devices  77.3 us (27%)
  other arithmetic  13.5 us (5%)
  local copies, waits for them, and re-layouts  12.4 us (4%)
    pallas_call x10, Pallas kernels, call(): pl.pallas_call(kernel, in_specs=[pl.BlockSpec(memory_space=space) for spa...  89.9 us
    ppermute x62, waiting for transfers between devices, swap(): return lax.ppermute(values, axis, [(i, i ^ step) for i in range(size)])  62.2 us
    ppermute x62, starting transfers between devices, swap(): return lax.ppermute(values, axis, [(i, i ^ step) for i in range(size)])  52.7 us
    ppermute x12, starting transfers between devices, step(): self.came = lax.ppermute(self.part, 'dp', self.pairs[self.number])  24.6 us
    ppermute x12, waiting for transfers between devices, step(): self.came = lax.ppermute(self.part, 'dp', self.pairs[self.number])  24 us
    convert_element_type x24, other arithmetic, add_low(): return total.astype(LOW)  9.14 us
  transfers between devices with their start and end apart: 74, of which 31 were waited for; matrix products, arithmetic and copies ran while one was open for 7% of the time, Pallas kernels for 26%

profile of v2, /device:TPU:0, one launch (start us, length us, event | category | flops | bytes accessed | tf_op | source)
XLA Modules:
  0.0 281.1 jit_solution(15399116836417609628)
XLA Ops:
  0.7 3.0 %collective-permute-start = (bf16[256,768]{1,0:T(8,128)(2,1)}, bf16[256,768]{1,0:T(8,128)(2,1)S(1)}, u32[]{:S(2)}, u32[]{:S(2)}) collective-permute-start(bf16[256,768]{1,0:T(8,128)(2,1)} %refs_0_.7), channel_id=1, source_target_pairs={{0,2},{1,3},{2,0},{3,1},{4,6},{5,7},{6,4},{7,5},{8,10},{9,11},{10,... | collective-permute-start | bytes 1179656 | tf_op jit(solution)/shard_map/ppermute | solution.py:38
  7.6 6.2 %collective-permute-done.refs_2_ = bf16[256,768]{1,0:T(8,128)(2,1)S(1)} collective-permute-done((bf16[256,768]{1,0:T(8,128)(2,1)}, bf16[256,768]{1,0:T(8,128)(2,1)S(1)}, u32[]{:S(2)}, u32[]{:S(2)}) %collective-permute-start) | collective-permute-done | bytes 393248 | tf_op jit(solution)/shard_map/ppermute | solution.py:38
  13.8 9.1 %collective-permute-done.1.refs_4_ = bf16[256,768]{1,0:T(8,128)(2,1)S(1)} collective-permute-done((bf16[256,768]{1,0:T(8,128)(2,1)}, bf16[256,768]{1,0:T(8,128)(2,1)S(1)}, u32[]{:S(2)}, u32[]{:S(2)}) %collective-permute-start.1) | collective-permute-done | bytes 393248 | tf_op jit(solution)/shard_map/ppermute | solution.py:38
  28.3 5.2 %project.1 = (f32[512,768]{1,0:T(8,128)S(1)}, f32[8,768]{1,0:T(8,128)S(1)}) custom-call(s32[8]{0:T(128)S(1)} %iota_xor_fusion.places, bf16[512,2048]{1,0:T(8,128)(2,1)} %bitcast.71, f32[8,768]{1,0:T(8,128)S(1)} %dynamic_update_slice.3.params_ref, bf16[256,768]{1,0:T(8,128)(2,1)} %refs_0_.7, bf16[256,768]{1,0:T(8,128)(2,1)} %copy-done.29, ...), custom_call_target="tpu_custom_call" | custom-call | flops 1024 | bytes 1024 | tf_op jit(solution)/shard_map/project/pallas_call | solution.py:257
  36.3 2.2 collective-permute-done.8
  38.6 2.6 collective-permute-start.9
  41.2 2.1 collective-permute-done.9
  48.3 2.0 collective-permute-done.12
  55.6 11.8 %attend.1 = (bf16[2304,512]{1,0:T(8,128)(2,1)S(1)}, bf16[768,512]{1,0:T(8,128)(2,1)S(1)}, f32[12,512]{1,0:T(8,128)S(1)}) custom-call(s32[8]{0:T(128)S(1)} %iota_xor_fusion.places, f32[512,768]{1,0:T(8,128)S(1)} %get-tuple-element.141.projected_ref, f32[8,768]{1,0:T(8,128)S(1)} %add_add_fusion.1.sums_ref, s32[1,512]{1,0:T(1,128)S(1)} %copy-done.9, ...), custom_call_target="tpu_custom_call" | custom-call | flops 1024 | bytes 1024 | tf_op jit(solution)/shard_map/attend/pallas_call | solution.py:257
  72.4 6.7 %collective-permute-done.25 = bf16[48,3840]{1,0:T(8,128)(2,1)S(1)} collective-permute-done((bf16[48,3840]{1,0:T(8,128)(2,1)S(1)}, bf16[48,3840]{1,0:T(8,128)(2,1)S(1)}, u32[]{:S(2)}, u32[]{:S(2)}) %collective-permute-start.25) | collective-permute-done | bytes 368672 | tf_op jit(solution)/shard_map/ppermute | solution.py:38
  79.2 3.1 %collective-permute-done.26 = bf16[48,3840]{1,0:T(8,128)(2,1)S(1)} collective-permute-done((bf16[48,3840]{1,0:T(8,128)(2,1)S(1)}, bf16[48,3840]{1,0:T(8,128)(2,1)S(1)}, u32[]{:S(2)}, u32[]{:S(2)}) %collective-permute-start.26) | collective-permute-done | bytes 368672 | tf_op jit(solution)/shard_map/ppermute | solution.py:38
  86.0 13.3 %expand.1 = (f32[512,768]{1,0:T(8,128)S(1)}, f32[512,1]{1,0:T(8,128)S(1)}, bf16[512,3072]{1,0:T(8,128)(2,1)S(1)}, bf16[512,3072]{1,0:T(8,128)(2,1)S(1)}) custom-call(s32[8]{0:T(128)S(1)} %iota_xor_fusion.places, f32[512,768]{1,0:T(8,128)S(1)} %get-tuple-element.141.projected_ref, f32[8,768]{1,0:T(8,128)S(1)} %add_add_fusion.1.sums_ref, ...), custom_call_target="tpu_custom_call" | custom-call | flops 1024 | bytes 1024 | tf_op jit(solution)/shard_map/expand/pallas_call | solution.py:257
  101.7 6.5 %collective-permute-done.33 = bf16[192,768]{1,0:T(8,128)(2,1)S(1)} collective-permute-done((bf16[192,768]{1,0:T(8,128)(2,1)S(1)}, bf16[192,768]{1,0:T(8,128)(2,1)S(1)}, u32[]{:S(2)}, u32[]{:S(2)}) %collective-permute-start.33) | collective-permute-done | bytes 294944 | tf_op jit(solution)/shard_map/ppermute | solution.py:38
  110.9 10.0 %contract.1 = (bf16[4,384,768]{2,1,0:T(8,128)(2,1)S(1)}, bf16[4,384,768]{2,1,0:T(8,128)(2,1)S(1)}, bf16[512,768]{1,0:T(8,128)(2,1)}, f32[512,768]{1,0:T(8,128)S(1)}, f32[2,768]{1,0:T(2,128)S(1)}) custom-call(s32[8]{0:T(128)S(1)} %iota_xor_fusion.places, f32[512,768]{1,0:T(8,128)S(1)} %get-tuple-element.154.hat_ref, f32[8,768]{1,0:T(8,128)S(1)} %add_add_fusion.1.sums_ref, ...), custom_call_target="tpu_custom_call" | custom-call | flops 1024 | bytes 1024 | tf_op jit(solution)/shard_map/contract/pallas_call | solution.py:257
  121.0 11.3 %hidden_back.1 = (bf16[4,384,768]{2,1,0:T(8,128)(2,1)S(1)}, bf16[4,384,768]{2,1,0:T(8,128)(2,1)S(1)}, bf16[512,3072]{1,0:T(8,128)(2,1)S(1)}) custom-call(s32[8]{0:T(128)S(1)} %iota_xor_fusion.places, f32[512,768]{1,0:T(8,128)S(1)} %get-tuple-element.162.back_ref, f32[512,768]{1,0:T(8,128)S(1)} %get-tuple-element.154.hat_ref, ...), custom_call_target="tpu_custom_call" | custom-call | flops 1024 | bytes 1024 | tf_op jit(solution)/shard_map/hidden_back/pallas_call | solution.py:257
  135.2 12.7 %expand_back.1 = (f32[512,768]{1,0:T(8,128)S(1)}, bf16[512,768]{1,0:T(8,128)(2,1)S(1)}, bf16[768,512]{1,0:T(8,128)(2,1)S(1)}, f32[2,768]{1,0:T(2,128)S(1)}, bf16[1152,512]{1,0:T(8,128)(2,1)S(1)}) custom-call(s32[8]{0:T(128)S(1)} %iota_xor_fusion.places, f32[512,768]{1,0:T(8,128)S(1)} %get-tuple-element.162.back_ref, ...), custom_call_target="tpu_custom_call" | custom-call | flops 1024 | bytes 1024 | tf_op jit(solution)/shard_map/expand_back/pallas_call | solution.py:257
  154.3 8.2 %attend_back.1 = (bf16[2304,512]{1,0:T(8,128)(2,1)S(1)}, f32[512,768]{1,0:T(8,128)S(1)}, f32[2,768]{1,0:T(2,128)S(1)}) custom-call(s32[8]{0:T(128)S(1)} %iota_xor_fusion.places, bf16[2304,512]{1,0:T(8,128)(2,1)S(1)} %get-tuple-element.169.packed_ref, bf16[768,512]{1,0:T(8,128)(2,1)S(1)} %get-tuple-element.181.mixed_back_ref, ...), custom_call_target="tpu_custom_call" | custom-call | flops 1024 | bytes 1024 | tf_op jit(solution)/shard_map/attend_back/pallas_call | solution.py:257
  165.5 2.2 collective-permute-done.45
  167.8 2.6 collective-permute-start.46
  170.4 2.1 collective-permute-done.46
  177.4 2.3 collective-permute-done.52
  179.7 6.0 %project_back.1 = (bf16[4,352,768]{2,1,0:T(8,128)(2,1)S(1)}, bf16[4,352,768]{2,1,0:T(8,128)(2,1)}, bf16[512,768]{1,0:T(8,128)(2,1)S(1)}) custom-call(s32[8]{0:T(128)S(1)} %iota_xor_fusion.places, f32[512,768]{1,0:T(8,128)S(1)} %get-tuple-element.198.embedded_ref, f32[512,768]{1,0:T(8,128)S(1)} %get-tuple-element.141.projected_ref, ...), custom_call_target="tpu_custom_call" | custom-call | flops 1024 | bytes 1024 | tf_op jit(solution)/shard_map/project_back/pallas_call | solution.py:257
  189.5 3.5 %collective-permute-start.47 = (bf16[384,768]{1,0:T(8,128)(2,1)S(1)}, bf16[384,768]{1,0:T(8,128)(2,1)S(1)}, u32[]{:S(2)}, u32[]{:S(2)}) collective-permute-start(bf16[384,768]{1,0:T(8,128)(2,1)S(1)} %pad_maximum_fusion.1), channel_id=1, source_target_pairs={{0,8},{24,16},{1,9},{25,17},{2,10},{26,18},{3,11},{27,19},{4,12},{... | collective-permute-start | bytes 1769480 | tf_op jit(solution)/shard_map/ppermute | solution.py:115
  193.0 4.5 %packed_gradient.1 = (bf16[4,96,2304]{2,1,0:T(8,128)(2,1)S(1)}, bf16[4,96,2304]{2,1,0:T(8,128)(2,1)S(1)}) custom-call(s32[8]{0:T(128)S(1)} %iota_xor_fusion.places, f32[512,768]{1,0:T(8,128)S(1)} %get-tuple-element.141.projected_ref, f32[8,768]{1,0:T(8,128)S(1)} %add_add_fusion.1.sums_ref, bf16[2304,512]{1,0:T(8,128)(2,1)} %copy-done.4), custom_call_target="tpu_custom_call" | custom-call | flops 1024 | bytes 1024 | tf_op jit(solution)/shard_map/packed_gradient/pallas_call | solution.py:257
  207.1 6.9 %input_gradient.1 = f32[512,2048]{1,0:T(8,128)} custom-call(s32[8]{0:T(128)S(1)} %iota_xor_fusion.places, bf16[512,768]{1,0:T(8,128)(2,1)S(1)} %get-tuple-element.205.low_ref, bf16[256,768]{1,0:T(8,128)(2,1)} %refs_0_.7, bf16[256,768]{1,0:T(8,128)(2,1)} %copy-done.29, bf16[256,768]{1,0:T(8,128)(2,1)} %copy-done.26, bf16[256,768]{1,0:T(8,128)(2,1)} %copy-done.30, ...), custom_call_target="tpu_custom_call" | custom-call | flops 1024 | bytes 1024 | tf_op jit(solution)/shard_map/input_gradient/pallas_call | solution.py:257
  223.1 4.1 %collective-permute-done.56 = bf16[176,768]{1,0:T(8,128)(2,1)S(1)} collective-permute-done((bf16[176,768]{1,0:T(8,128)(2,1)S(1)}, bf16[176,768]{1,0:T(8,128)(2,1)S(1)}, u32[]{:S(2)}, u32[]{:S(2)}) %collective-permute-start.56) | collective-permute-done | bytes 270368 | tf_op jit(solution)/shard_map/ppermute | solution.py:38
  229.9 4.6 %collective-permute-start.61 = (bf16[352,768]{1,0:T(8,128)(2,1)S(1)}, bf16[352,768]{1,0:T(8,128)(2,1)S(1)}, u32[]{:S(2)}, u32[]{:S(2)}) collective-permute-start(bf16[352,768]{1,0:T(8,128)(2,1)S(1)} %pad_maximum_fusion.3), channel_id=1, source_target_pairs={{0,8},{24,16},{1,9},{25,17},{2,10},{26,18},{3,11},{27,19},{4,12},{... | collective-permute-start | bytes 1622024 | tf_op jit(solution)/shard_map/ppermute | solution.py:115
  239.9 2.8 %collective-permute-done.61 = bf16[352,768]{1,0:T(8,128)(2,1)S(1)} collective-permute-done((bf16[352,768]{1,0:T(8,128)(2,1)S(1)}, bf16[352,768]{1,0:T(8,128)(2,1)S(1)}, u32[]{:S(2)}, u32[]{:S(2)}) %collective-permute-start.61) | collective-permute-done | bytes 540704 | tf_op jit(solution)/shard_map/ppermute | solution.py:115
  243.8 7.2 %collective-permute-start.69 = (bf16[96,2304]{1,0:T(8,128)(2,1)S(1)}, bf16[96,2304]{1,0:T(8,128)(2,1)S(1)}, u32[]{:S(2)}, u32[]{:S(2)}) collective-permute-start(bf16[96,2304]{1,0:T(8,128)(2,1)S(1)} %pad_maximum_fusion.4), channel_id=1, source_target_pairs={{0,8},{24,16},{1,9},{25,17},{2,10},{26,18},{3,11},{27,19},{4,12},{... | collective-permute-start | bytes 1327112 | tf_op jit(solution)/shard_map/ppermute | solution.py:115
  252.3 4.5 %collective-permute-done.69 = bf16[96,2304]{1,0:T(8,128)(2,1)S(1)} collective-permute-done((bf16[96,2304]{1,0:T(8,128)(2,1)S(1)}, bf16[96,2304]{1,0:T(8,128)(2,1)S(1)}, u32[]{:S(2)}, u32[]{:S(2)}) %collective-permute-start.69) | collective-permute-done | bytes 442400 | tf_op jit(solution)/shard_map/ppermute | solution.py:115
  261.7 13.6 %collective-permute-done.68 = bf16[352,768]{1,0:T(8,128)(2,1)S(1)} collective-permute-done((bf16[352,768]{1,0:T(8,128)(2,1)S(1)}, bf16[352,768]{1,0:T(8,128)(2,1)S(1)}, u32[]{:S(2)}, u32[]{:S(2)}) %collective-permute-start.68) | collective-permute-done | bytes 540704 | tf_op jit(solution)/shard_map/ppermute | solution.py:115
  277.1 3.0 %collective-permute-done.71 = bf16[96,2304]{1,0:T(8,128)(2,1)S(1)} collective-permute-done((bf16[96,2304]{1,0:T(8,128)(2,1)S(1)}, bf16[96,2304]{1,0:T(8,128)(2,1)S(1)}, u32[]{:S(2)}, u32[]{:S(2)}) %collective-permute-start.71) | collective-permute-done | bytes 442400 | tf_op jit(solution)/shard_map/ppermute | solution.py:115
  (276 shorter events, 93.1 us)
Async XLA Ops:
  3.7 19.2 %collective-permute-start.1 = (bf16[256,768]{1,0:T(8,128)(2,1)}, bf16[256,768]{1,0:T(8,128)(2,1)S(1)}, u32[]{:S(2)}, u32[]{:S(2)}) collective-permute-start(bf16[256,768]{1,0:T(8,128)(2,1)} %refs_0_.7), channel_id=1, source_target_pairs={{0,4},{1,5},{2,6},{3,7},{4,0},{5,1},{6,2},{7,3},{8,12},{9,13},{10,... | collective-permute-start | bytes 1179656 | tf_op jit(solution)/shard_map/ppermute | solution.py:38
  5.2 17.7 %collective-permute-start.2 = (bf16[256,768]{1,0:T(8,128)(2,1)}, bf16[256,768]{1,0:T(8,128)(2,1)S(1)}, u32[]{:S(2)}, u32[]{:S(2)}) collective-permute-start(bf16[256,768]{1,0:T(8,128)(2,1)} %refs_0_.7), channel_id=1, source_target_pairs={{0,6},{1,7},{2,4},{3,5},{4,2},{5,3},{6,0},{7,1},{8,14},{9,15},{10,... | collective-permute-start | bytes 1179656 | tf_op jit(solution)/shard_map/ppermute | solution.py:38
  24.0 21.5 %collective-permute-start.13 = (bf16[96,2304]{1,0:T(8,128)(2,1)S(1)}, bf16[96,2304]{1,0:T(8,128)(2,1)}, u32[]{:S(2)}, u32[]{:S(2)}) collective-permute-start(bf16[96,2304]{1,0:T(8,128)(2,1)S(1)} %copy-done.23), channel_id=1, source_target_pairs={{0,2},{1,3},{2,0},{3,1},{4,6},{5,7},{6,4},{7,5},{8,10},{9,11},{10,... | collective-permute-start | bytes 1327112 | tf_op jit(solution)/shard_map/ppermute | solution.py:38
  25.2 21.6 %collective-permute-start.14 = (bf16[96,2304]{1,0:T(8,128)(2,1)S(1)}, bf16[96,2304]{1,0:T(8,128)(2,1)}, u32[]{:S(2)}, u32[]{:S(2)}) collective-permute-start(bf16[96,2304]{1,0:T(8,128)(2,1)S(1)} %copy-done.23), channel_id=1, source_target_pairs={{0,4},{1,5},{2,6},{3,7},{4,0},{5,1},{6,2},{7,3},{8,12},{9,13},{10,... | collective-permute-start | bytes 1327112 | tf_op jit(solution)/shard_map/ppermute | solution.py:38
  26.2 20.7 %collective-permute-start.15 = (bf16[96,2304]{1,0:T(8,128)(2,1)S(1)}, bf16[96,2304]{1,0:T(8,128)(2,1)}, u32[]{:S(2)}, u32[]{:S(2)}) collective-permute-start(bf16[96,2304]{1,0:T(8,128)(2,1)S(1)} %copy-done.23), channel_id=1, source_target_pairs={{0,6},{1,7},{2,4},{3,5},{4,2},{5,3},{6,0},{7,1},{8,14},{9,15},{10,... | collective-permute-start | bytes 1327112 | tf_op jit(solution)/shard_map/ppermute | solution.py:38
  50.2 17.2 %collective-permute-start.21 = (bf16[96,3840]{1,0:T(8,128)(2,1)S(1)}, bf16[96,3840]{1,0:T(8,128)(2,1)}, u32[]{:S(2)}, u32[]{:S(2)}) collective-permute-start(bf16[96,3840]{1,0:T(8,128)(2,1)S(1)} %constant_dynamic-update-slice_fusion.refs_0_), channel_id=1, source_target_pairs={{0,2},{1,3},{2,0},{3,1},{4,6},{5,7},{6,4},{7,5},{8,10},{9,11},{10,... | collective-permute-start | bytes 2211848 | tf_op jit(solution)/shard_map/ppermute | solution.py:38
  51.7 15.8 %collective-permute-start.22 = (bf16[96,3840]{1,0:T(8,128)(2,1)S(1)}, bf16[96,3840]{1,0:T(8,128)(2,1)}, u32[]{:S(2)}, u32[]{:S(2)}) collective-permute-start(bf16[96,3840]{1,0:T(8,128)(2,1)S(1)} %constant_dynamic-update-slice_fusion.refs_0_), channel_id=1, source_target_pairs={{0,4},{1,5},{2,6},{3,7},{4,0},{5,1},{6,2},{7,3},{8,12},{9,13},{10,... | collective-permute-start | bytes 2211848 | tf_op jit(solution)/shard_map/ppermute | solution.py:38
  69.7 13.7 %collective-permute-start.20 = (bf16[96,3840]{1,0:T(8,128)(2,1)S(1)}, bf16[96,3840]{1,0:T(8,128)(2,1)S(1)}, u32[]{:S(2)}, u32[]{:S(2)}) collective-permute-start(bf16[96,3840]{1,0:T(8,128)(2,1)S(1)} %constant_dynamic-update-slice_fusion.refs_0_), channel_id=1, source_target_pairs={{0,1},{1,0},{2,3},{3,2},{4,5},{5,4},{6,7},{7,6},{8,9},{9,8},{10,11... | collective-permute-start | bytes 2211848 | tf_op jit(solution)/shard_map/ppermute | solution.py:38
  70.7 14.2 %collective-permute-start.23 = (bf16[96,3840]{1,0:T(8,128)(2,1)}, bf16[96,3840]{1,0:T(8,128)(2,1)S(1)}, u32[]{:S(2)}, u32[]{:S(2)}) collective-permute-start(bf16[96,3840]{1,0:T(8,128)(2,1)} %collective-permute-done.21.refs_2_), channel_id=1, source_target_pairs={{0,1},{1,0},{2,3},{3,2},{4,5},{5,4},{6,7},{7,6},{8,9},{9,8},{10,11... | collective-permute-start | bytes 2211848 | tf_op jit(solution)/shard_map/ppermute | solution.py:38
  71.2 13.6 %collective-permute-start.24 = (bf16[96,3840]{1,0:T(8,128)(2,1)}, bf16[96,3840]{1,0:T(8,128)(2,1)S(1)}, u32[]{:S(2)}, u32[]{:S(2)}) collective-permute-start(bf16[96,3840]{1,0:T(8,128)(2,1)} %collective-permute-done.22.refs_4_), channel_id=1, source_target_pairs={{0,1},{1,0},{2,3},{3,2},{4,5},{5,4},{6,7},{7,6},{8,9},{9,8},{10,11... | collective-permute-start | bytes 2211848 | tf_op jit(solution)/shard_map/ppermute | solution.py:38
  82.4 16.9 %collective-permute-start.29 = (bf16[384,768]{1,0:T(8,128)(2,1)S(1)}, bf16[384,768]{1,0:T(8,128)(2,1)S(1)}, u32[]{:S(2)}, u32[]{:S(2)}) collective-permute-start(bf16[384,768]{1,0:T(8,128)(2,1)S(1)} %copy-done.18), channel_id=1, source_target_pairs={{0,2},{1,3},{2,0},{3,1},{4,6},{5,7},{6,4},{7,5},{8,10},{9,11},{10,... | collective-permute-start | bytes 1769480 | tf_op jit(solution)/shard_map/ppermute | solution.py:38
  83.4 15.9 %collective-permute-start.30 = (bf16[384,768]{1,0:T(8,128)(2,1)S(1)}, bf16[384,768]{1,0:T(8,128)(2,1)S(1)}, u32[]{:S(2)}, u32[]{:S(2)}) collective-permute-start(bf16[384,768]{1,0:T(8,128)(2,1)S(1)} %copy-done.18), channel_id=1, source_target_pairs={{0,4},{1,5},{2,6},{3,7},{4,0},{5,1},{6,2},{7,3},{8,12},{9,13},{10,... | collective-permute-start | bytes 1769480 | tf_op jit(solution)/shard_map/ppermute | solution.py:38
  132.4 17.3 %collective-permute-start.41 = (bf16[4,384,768]{2,1,0:T(8,128)(2,1)S(1)}, bf16[4,384,768]{2,1,0:T(8,128)(2,1)S(1)}, u32[]{:S(2)}, u32[]{:S(2)}) collective-permute-start(bf16[4,384,768]{2,1,0:T(8,128)(2,1)S(1)} %get-tuple-element.177), channel_id=1, source_target_pairs={{0,1},{1,0},{2,3},{3,2},{4,5},{5,4},{6,7},{7,6},{8,9},{9,8},{10,11... | collective-permute-start | bytes 7077896 | tf_op jit(solution)/shard_map/ppermute | solution.py:38
  133.0 15.4 %collective-permute-start.38 = (bf16[2,192,768]{2,1,0:T(8,128)(2,1)S(1)}, bf16[2,192,768]{2,1,0:T(8,128)(2,1)S(1)}, u32[]{:S(2)}, u32[]{:S(2)}) collective-permute-start(bf16[2,192,768]{2,1,0:T(8,128)(2,1)S(1)} %add_convert_fusion.6), channel_id=1, source_target_pairs={{0,4},{1,5},{2,6},{3,7},{4,0},{5,1},{6,2},{7,3},{8,12},{9,13},{10,... | collective-permute-start | bytes 1769480 | tf_op jit(solution)/shard_map/ppermute | solution.py:38
  134.2 15.2 %collective-permute-start.37 = (bf16[2,192,768]{2,1,0:T(8,128)(2,1)S(1)}, bf16[2,192,768]{2,1,0:T(8,128)(2,1)S(1)}, u32[]{:S(2)}, u32[]{:S(2)}) collective-permute-start(bf16[2,192,768]{2,1,0:T(8,128)(2,1)S(1)} %add_convert_fusion.7), channel_id=1, source_target_pairs={{0,2},{1,3},{2,0},{3,1},{4,6},{5,7},{6,4},{7,5},{8,10},{9,11},{10,... | collective-permute-start | bytes 1769480 | tf_op jit(solution)/shard_map/ppermute | solution.py:38
  152.3 20.2 %collective-permute-start.43 = (bf16[2,192,768]{2,1,0:T(8,128)(2,1)S(1)}, bf16[2,192,768]{2,1,0:T(8,128)(2,1)S(1)}, u32[]{:S(2)}, u32[]{:S(2)}) collective-permute-start(bf16[2,192,768]{2,1,0:T(8,128)(2,1)S(1)} %add_convert_fusion.4), channel_id=1, source_target_pairs={{0,4},{1,5},{2,6},{3,7},{4,0},{5,1},{6,2},{7,3},{8,12},{9,13},{10,... | collective-permute-start | bytes 1769480 | tf_op jit(solution)/shard_map/ppermute | solution.py:38
  153.0 19.5 %collective-permute-start.42 = (bf16[2,192,768]{2,1,0:T(8,128)(2,1)S(1)}, bf16[2,192,768]{2,1,0:T(8,128)(2,1)S(1)}, u32[]{:S(2)}, u32[]{:S(2)}) collective-permute-start(bf16[2,192,768]{2,1,0:T(8,128)(2,1)S(1)} %add_convert_fusion.5), channel_id=1, source_target_pairs={{0,2},{1,3},{2,0},{3,1},{4,6},{5,7},{6,4},{7,5},{8,10},{9,11},{10,... | collective-permute-start | bytes 1769480 | tf_op jit(solution)/shard_map/ppermute | solution.py:38
  187.8 14.0 %collective-permute-start.48 = (bf16[192,768]{1,0:T(8,128)(2,1)}, bf16[192,768]{1,0:T(8,128)(2,1)S(1)}, u32[]{:S(2)}, u32[]{:S(2)}) collective-permute-start(bf16[192,768]{1,0:T(8,128)(2,1)} %get-tuple-element.264), channel_id=1, source_target_pairs={{0,4},{1,5},{2,6},{3,7},{4,0},{5,1},{6,2},{7,3},{8,12},{9,13},{10,... | collective-permute-start | bytes 884744 | tf_op jit(solution)/shard_map/ppermute | solution.py:38
  188.3 15.0 %collective-permute-start.49 = (bf16[192,768]{1,0:T(8,128)(2,1)S(1)}, bf16[192,768]{1,0:T(8,128)(2,1)S(1)}, u32[]{:S(2)}, u32[]{:S(2)}) collective-permute-start(bf16[192,768]{1,0:T(8,128)(2,1)S(1)} %get-tuple-element.263), channel_id=1, source_target_pairs={{0,2},{1,3},{2,0},{3,1},{4,6},{5,7},{6,4},{7,5},{8,10},{9,11},{10,... | collective-permute-start | bytes 884744 | tf_op jit(solution)/shard_map/ppermute | solution.py:38
  189.5 16.7 %collective-permute-start.47 = (bf16[384,768]{1,0:T(8,128)(2,1)S(1)}, bf16[384,768]{1,0:T(8,128)(2,1)S(1)}, u32[]{:S(2)}, u32[]{:S(2)}) collective-permute-start(bf16[384,768]{1,0:T(8,128)(2,1)S(1)} %pad_maximum_fusion.1), channel_id=1, source_target_pairs={{0,8},{24,16},{1,9},{25,17},{2,10},{26,18},{3,11},{27,19},{4,12},{... | collective-permute-start | bytes 1769480 | tf_op jit(solution)/shard_map/ppermute | solution.py:115
  197.6 20.0 %collective-permute-start.60 = (bf16[4,96,2304]{2,1,0:T(8,128)(2,1)S(1)}, bf16[4,96,2304]{2,1,0:T(8,128)(2,1)S(1)}, u32[]{:S(2)}, u32[]{:S(2)}) collective-permute-start(bf16[4,96,2304]{2,1,0:T(8,128)(2,1)S(1)} %get-tuple-element.209), channel_id=1, source_target_pairs={{0,1},{1,0},{2,3},{3,2},{4,5},{5,4},{6,7},{7,6},{8,9},{9,8},{10,11... | collective-permute-start | bytes 5308424 | tf_op jit(solution)/shard_map/ppermute | solution.py:38
  200.6 14.7 %collective-permute-start.55 = (bf16[2,176,768]{2,1,0:T(8,128)(2,1)S(1)}, bf16[2,176,768]{2,1,0:T(8,128)(2,1)S(1)}, u32[]{:S(2)}, u32[]{:S(2)}) collective-permute-start(bf16[2,176,768]{2,1,0:T(8,128)(2,1)S(1)} %add_convert_fusion.10), channel_id=1, source_target_pairs={{0,4},{1,5},{2,6},{3,7},{4,0},{5,1},{6,2},{7,3},{8,12},{9,13},{10,... | collective-permute-start | bytes 1622024 | tf_op jit(solution)/shard_map/ppermute | solution.py:38
  201.9 14.5 %collective-permute-start.54 = (bf16[2,176,768]{2,1,0:T(8,128)(2,1)S(1)}, bf16[2,176,768]{2,1,0:T(8,128)(2,1)S(1)}, u32[]{:S(2)}, u32[]{:S(2)}) collective-permute-start(bf16[2,176,768]{2,1,0:T(8,128)(2,1)S(1)} %add_convert_fusion.11), channel_id=1, source_target_pairs={{0,2},{1,3},{2,0},{3,1},{4,6},{5,7},{6,4},{7,5},{8,10},{9,11},{10,... | collective-permute-start | bytes 1622024 | tf_op jit(solution)/shard_map/ppermute | solution.py:38
  204.9 16.5 %collective-permute-start.59 = (bf16[384,768]{1,0:T(8,128)(2,1)S(1)}, bf16[384,768]{1,0:T(8,128)(2,1)S(1)}, u32[]{:S(2)}, u32[]{:S(2)}) collective-permute-start(bf16[384,768]{1,0:T(8,128)(2,1)S(1)} %pad_maximum_fusion.2), channel_id=1, source_target_pairs={{0,8},{24,16},{1,9},{25,17},{2,10},{26,18},{3,11},{27,19},{4,12},{... | collective-permute-start | bytes 1769480 | tf_op jit(solution)/shard_map/ppermute | solution.py:115
  206.4 15.8 %collective-permute-start.58 = (bf16[384,768]{1,0:T(8,128)(2,1)S(1)}, bf16[384,768]{1,0:T(8,128)(2,1)S(1)}, u32[]{:S(2)}, u32[]{:S(2)}) collective-permute-start(bf16[384,768]{1,0:T(8,128)(2,1)S(1)} %add_convert_fusion.3), channel_id=1, source_target_pairs={{8,16},{16,8},{9,17},{17,9},{10,18},{18,10},{11,19},{19,11},{12,20... | collective-permute-start | bytes 1769480 | tf_op jit(solution)/shard_map/ppermute | solution.py:115
  219.7 15.4 %collective-permute-start.64 = (bf16[2,48,2304]{2,1,0:T(8,128)(2,1)S(1)}, bf16[2,48,2304]{2,1,0:T(8,128)(2,1)S(1)}, u32[]{:S(2)}, u32[]{:S(2)}) collective-permute-start(bf16[2,48,2304]{2,1,0:T(8,128)(2,1)S(1)} %add_convert_fusion.14), channel_id=1, source_target_pairs={{0,4},{1,5},{2,6},{3,7},{4,0},{5,1},{6,2},{7,3},{8,12},{9,13},{10,... | collective-permute-start | bytes 1327112 | tf_op jit(solution)/shard_map/ppermute | solution.py:38
  221.4 14.4 %collective-permute-start.63 = (bf16[2,48,2304]{2,1,0:T(8,128)(2,1)S(1)}, bf16[2,48,2304]{2,1,0:T(8,128)(2,1)S(1)}, u32[]{:S(2)}, u32[]{:S(2)}) collective-permute-start(bf16[2,48,2304]{2,1,0:T(8,128)(2,1)S(1)} %add_convert_fusion.15), channel_id=1, source_target_pairs={{0,2},{1,3},{2,0},{3,1},{4,6},{5,7},{6,4},{7,5},{8,10},{9,11},{10,... | collective-permute-start | bytes 1327112 | tf_op jit(solution)/shard_map/ppermute | solution.py:38
  222.2 16.2 %collective-permute-start.62 = (bf16[384,768]{1,0:T(8,128)(2,1)S(1)}, bf16[384,768]{1,0:T(8,128)(2,1)S(1)}, u32[]{:S(2)}, u32[]{:S(2)}) collective-permute-start(bf16[384,768]{1,0:T(8,128)(2,1)S(1)} %add_convert_fusion.2), channel_id=1, source_target_pairs={{8,16},{16,8},{9,17},{17,9},{10,18},{18,10},{11,19},{19,11},{12,20... | collective-permute-start | bytes 1769480 | tf_op jit(solution)/shard_map/ppermute | solution.py:115
  227.2 23.8 %collective-permute-start.73 = (bf16[384,768]{1,0:T(8,128)(2,1)S(1)}, bf16[384,768]{1,0:T(8,128)(2,1)S(1)}, u32[]{:S(2)}, u32[]{:S(2)}) collective-permute-start(bf16[384,768]{1,0:T(8,128)(2,1)S(1)} %add_convert_fusion.1), channel_id=1, source_target_pairs={{8,0},{16,24},{9,1},{17,25},{10,2},{18,26},{11,3},{19,27},{12,4},{... | collective-permute-start | bytes 1769480 | tf_op jit(solution)/shard_map/ppermute | solution.py:115
  238.6 19.1 %collective-permute-start.72 = (bf16[384,768]{1,0:T(8,128)(2,1)S(1)}, bf16[384,768]{1,0:T(8,128)(2,1)S(1)}, u32[]{:S(2)}, u32[]{:S(2)}) collective-permute-start(bf16[384,768]{1,0:T(8,128)(2,1)S(1)} %add_convert_fusion), channel_id=1, source_target_pairs={{8,0},{16,24},{9,1},{17,25},{10,2},{18,26},{11,3},{19,27},{12,4},{... | collective-permute-start | bytes 1769480 | tf_op jit(solution)/shard_map/ppermute | solution.py:115
  257.8 17.5 %collective-permute-start.68 = (bf16[352,768]{1,0:T(8,128)(2,1)S(1)}, bf16[352,768]{1,0:T(8,128)(2,1)S(1)}, u32[]{:S(2)}, u32[]{:S(2)}) collective-permute-start(bf16[352,768]{1,0:T(8,128)(2,1)S(1)} %add_convert_fusion.8), channel_id=1, source_target_pairs={{8,0},{16,24},{9,1},{17,25},{10,2},{18,26},{11,3},{19,27},{12,4},{... | collective-permute-start | bytes 1622024 | tf_op jit(solution)/shard_map/ppermute | solution.py:115
  259.3 20.8 %collective-permute-start.71 = (bf16[96,2304]{1,0:T(8,128)(2,1)S(1)}, bf16[96,2304]{1,0:T(8,128)(2,1)S(1)}, u32[]{:S(2)}, u32[]{:S(2)}) collective-permute-start(bf16[96,2304]{1,0:T(8,128)(2,1)S(1)} %add_convert_fusion.12), channel_id=1, source_target_pairs={{8,0},{16,24},{9,1},{17,25},{10,2},{18,26},{11,3},{19,27},{12,4},{... | collective-permute-start | bytes 1327112 | tf_op jit(solution)/shard_map/ppermute | solution.py:115
  (80 other events, 646.7 us)

commit v3 on v2

--- a/solution.py
+++ b/solution.py
@@ -68,15 +68,23 @@
             whole = halves[0].reshape(-1, halves[0].shape[-1])
             self.part = lax.psum_scatter(whole, "shard", scatter_dimension=0, tiled=True)
 
+    def sent(self):
+        mine, got = self.mine, self.got
+        return [
+            add_low(jnp.stack([mine[near, cut], mine[3, cut]]), jnp.stack([got[near, cut], got[3, cut]]))
+            for cut, near, _ in self.cuts
+        ]
+
+    def passed(self):
+        return [
+            add_low(self.mine[far, cut], self.got[far, cut], came[1]) for came, (cut, _, far) in zip(self.came, self.cuts)
+        ]
+
     def plane_one(self, *after):
         if not self.direct:
             return self.part
         self.mine, self.got = tie((self.mine, self.got), *after)
-        mine, got = self.mine, self.got
-        sent = [
-            add_low(jnp.stack([mine[near, cut], mine[3, cut]]), jnp.stack([got[near, cut], got[3, cut]]))
-            for cut, near, _ in self.cuts
-        ]
+        sent = self.sent()
         self.came = [swap(part, 2 * near) for part, (_, near, _) in zip(sent, self.cuts)]
         return sent
 
@@ -84,9 +92,7 @@
         if not self.direct:
             return self.part
         self.mine, self.got, self.came = tie((self.mine, self.got, self.came), *after)
-        passed = [
-            add_low(self.mine[far, cut], self.got[far, cut], came[1]) for came, (cut, _, far) in zip(self.came, self.cuts)
-        ]
+        passed = self.passed()
         self.back = [swap(part, 2 * far) for part, (_, _, far) in zip(passed, self.cuts)]
         return passed
 
@@ -97,6 +103,19 @@
         return jnp.concatenate(
             [add_low(mine[0, cut], got[0, cut], c[0], b) for c, b, (cut, _, _) in zip(came, back, self.cuts)]
         )
+
+
+def plane_together(older, newer, *after):
+    older.mine, older.got, older.came, newer.mine, newer.got = tie(
+        (older.mine, older.got, older.came, newer.mine, newer.got), *after
+    )
+    passed, sent = older.passed(), newer.sent()
+    parts, size = [jnp.concatenate([new.reshape(-1, new.shape[-1]), old]) for new, old in zip(sent, passed[::-1])], sent[0]
+    came = [swap(parts[0], ACROSS), swap(parts[1], ALONG)]
+    rows = size.shape[0] * size.shape[1]
+    newer.came = [part[:rows].reshape(size.shape) for part in came]
+    older.back = [part[rows:] for part in came[::-1]]
+    return parts
 
 
 class LineSum:
@@ -629,7 +648,7 @@
         out_near=(0,),
         far=(1, *range(3, 100)),
         sems=((8,), (1,)),
-        loose=(2 + count,),
+        loose=(4, 6, 8, 10),
     )
     if direct:
         sums = sums + swap(sums, CORE)
@@ -656,7 +675,7 @@
         near=(1,), out_near=(0, 1, 2),
         far=range(5, 100),
         sems=((3, 8),),
-        loose=(4 + count,),
+        loose=(6, 8, 10, 12),
     )
     if direct:
         up_sides = tie(up_sides, mixed)
@@ -674,7 +693,7 @@
         near=(1, 3), out_near=(0, 1, 2, 3),
         far=range(4, 100),
         sems=((8,), (4, 8)),
-        loose=(3 + count,),
+        loose=(5, 7, 9, 11),
     )
     if direct:
         down_sides = tie(down_sides, active)
@@ -688,7 +707,7 @@
         near=(1, 3), out_near=(cores + 1,),
         far=range(4, 100),
         sems=((8,), (1,)),
-        loose=(4 + count,),
+        loose=(6, 8, 10, 12),
     )
     down = OwnedSum(down_halves)
     *up_halves, grad_hidden = call(
@@ -718,8 +737,7 @@
         far=range(10, 100),
         sems=((8,), (4, 8)),
     )
-    sent = down.plane_two(first)
-    sent = up.plane_one(sent)
+    sent = plane_together(down, up, first) if direct else first
     grad_packed, grad_embedded, grads_bn = call(
         functools.partial(attend_back_kernel, count, tokens),
         [
@@ -735,7 +753,7 @@
     )
     second = jnp.concatenate([grads_bn, grads_one, grads_two, jnp.zeros((2, width), F32)])
     if direct:
-        second = second + swap(tie(second, down.back), CORE)
+        second = second + swap(second, CORE)
         second = second + swap(second, 1, "dp")
         second = second + swap(second, 2, "dp")
         second = tie(second, up.came)
@@ -788,7 +806,6 @@
 
     if direct:
         sent = down_sum.step(sent)
-        sent = roi_grad = input_gradient(sent)
         sent = roi.plane_two(sent)
         sent = qkv.plane_one(sent)
         sent = down_sum.step(up_sum.step(sent))
@@ -801,6 +818,7 @@
         sent = qkv_sum.step()
         sent = roi_sum.step(sent)
         sent = qkv_sum.step(sent)
+        sent = roi_grad = input_gradient(sent)
         sent = qkv_sum.step(sent)
         sum_roi, sum_down, sum_up, sum_qkv = [g.total() for g in (roi_sum, down_sum, up_sum, qkv_sum)]
         sum_roi, sum_out = sum_roi[:roi_rows], sum_roi[roi_rows:]

time: 282 us -> 280 us (level)
    ppermute x62 -> x60, waiting for transfers between devices: 62.2 us -> 69.3 us  [swap(): return lax.ppermute(values, axis, [(i, i ^ step) for i in range(size)])]
    ppermute x12, waiting for transfers between devices: 24 us -> 17.7 us  [step(): self.came = lax.ppermute(self.part, 'dp', self.pairs[self.number])]
    ppermute x62 -> x60, starting transfers between devices: 52.7 us -> 50.9 us  [swap(): return lax.ppermute(values, axis, [(i, i ^ step) for i in range(size)])]
  transfers between devices with their start and end apart: 74 -> 72, of which waited for: 31 -> 35; matrix products, arithmetic and copies ran while one was open for 7% -> 8% of each run, Pallas kernels for 26% -> 26%
where the time goes in v3:
time: 280 us
  Pallas kernels  89.4 us (32%)
  waiting for transfers between devices  86.9 us (31%)
  starting transfers between devices  75.6 us (27%)
  other arithmetic  13.6 us (5%)
  local copies, waits for them, and re-layouts  12.5 us (4%)
    pallas_call x10, Pallas kernels, call(): pl.pallas_call(kernel, in_specs=[pl.BlockSpec(memory_space=space) for spa...  89.4 us
    ppermute x60, waiting for transfers between devices, swap(): return lax.ppermute(values, axis, [(i, i ^ step) for i in range(size)])  69.3 us
    ppermute x60, starting transfers between devices, swap(): return lax.ppermute(values, axis, [(i, i ^ step) for i in range(size)])  50.9 us
    ppermute x12, starting transfers between devices, step(): self.came = lax.ppermute(self.part, 'dp', self.pairs[self.number])  24.6 us
    ppermute x12, waiting for transfers between devices, step(): self.came = lax.ppermute(self.part, 'dp', self.pairs[self.number])  17.7 us
    convert_element_type x24, other arithmetic, add_low(): return total.astype(LOW)  9.11 us
  transfers between devices with their start and end apart: 72, of which 35 were waited for; matrix products, arithmetic and copies ran while one was open for 8% of the time, Pallas kernels for 26%

profile of v3, /device:TPU:0, one launch (start us, length us, event | category | flops | bytes accessed | tf_op | source)
XLA Modules:
  0.0 279.7 jit_solution(5258261275192737634)
XLA Ops:
  0.6 3.0 %collective-permute-start = (bf16[256,768]{1,0:T(8,128)(2,1)}, bf16[256,768]{1,0:T(8,128)(2,1)S(1)}, u32[]{:S(2)}, u32[]{:S(2)}) collective-permute-start(bf16[256,768]{1,0:T(8,128)(2,1)} %refs_0_.7), channel_id=1, source_target_pairs={{0,2},{1,3},{2,0},{3,1},{4,6},{5,7},{6,4},{7,5},{8,10},{9,11},{10,... | collective-permute-start | bytes 1179656 | tf_op jit(solution)/shard_map/ppermute | solution.py:38
  9.9 3.9 %collective-permute-done.refs_2_ = bf16[256,768]{1,0:T(8,128)(2,1)S(1)} collective-permute-done((bf16[256,768]{1,0:T(8,128)(2,1)}, bf16[256,768]{1,0:T(8,128)(2,1)S(1)}, u32[]{:S(2)}, u32[]{:S(2)}) %collective-permute-start) | collective-permute-done | bytes 393248 | tf_op jit(solution)/shard_map/ppermute | solution.py:38
  13.8 9.1 %collective-permute-done.1.refs_4_ = bf16[256,768]{1,0:T(8,128)(2,1)S(1)} collective-permute-done((bf16[256,768]{1,0:T(8,128)(2,1)}, bf16[256,768]{1,0:T(8,128)(2,1)S(1)}, u32[]{:S(2)}, u32[]{:S(2)}) %collective-permute-start.1) | collective-permute-done | bytes 393248 | tf_op jit(solution)/shard_map/ppermute | solution.py:38
  28.1 5.0 %project.1 = (f32[512,768]{1,0:T(8,128)S(1)}, f32[8,768]{1,0:T(8,128)S(1)}) custom-call(s32[8]{0:T(128)S(1)} %iota_xor_fusion.places, bf16[512,2048]{1,0:T(8,128)(2,1)} %bitcast.75, f32[8,768]{1,0:T(8,128)S(1)} %dynamic_update_slice.3.params_ref, bf16[256,768]{1,0:T(8,128)(2,1)} %refs_0_.7, bf16[256,768]{1,0:T(8,128)(2,1)S(1)} %collective-permute-done.3.refs_1_, ...), custom_call_target="tpu_custom_call" | custom-call | flops 1024 | bytes 1024 | tf_op jit(solution)/shard_map/project/pallas_call | solution.py:276
  36.0 2.3 collective-permute-done.8
  38.2 2.6 collective-permute-start.9
  40.8 2.1 collective-permute-done.9
  47.6 2.0 collective-permute-done.12
  55.2 11.7 %attend.1 = (bf16[2304,512]{1,0:T(8,128)(2,1)S(1)}, bf16[768,512]{1,0:T(8,128)(2,1)S(1)}, f32[12,512]{1,0:T(8,128)S(1)}) custom-call(s32[8]{0:T(128)S(1)} %iota_xor_fusion.places, f32[512,768]{1,0:T(8,128)S(1)} %get-tuple-element.140.projected_ref, f32[8,768]{1,0:T(8,128)S(1)} %add_add_fusion.1.sums_ref, s32[1,512]{1,0:T(1,128)S(1)} %copy-done.20, ...), custom_call_target="tpu_custom_call" | custom-call | flops 1024 | bytes 1024 | tf_op jit(solution)/shard_map/attend/pallas_call | solution.py:276
  72.7 6.0 %collective-permute-done.25 = bf16[48,3840]{1,0:T(8,128)(2,1)S(1)} collective-permute-done((bf16[48,3840]{1,0:T(8,128)(2,1)S(1)}, bf16[48,3840]{1,0:T(8,128)(2,1)S(1)}, u32[]{:S(2)}, u32[]{:S(2)}) %collective-permute-start.25) | collective-permute-done | bytes 368672 | tf_op jit(solution)/shard_map/ppermute | solution.py:38
  78.8 3.4 %collective-permute-done.26 = bf16[48,3840]{1,0:T(8,128)(2,1)S(1)} collective-permute-done((bf16[48,3840]{1,0:T(8,128)(2,1)S(1)}, bf16[48,3840]{1,0:T(8,128)(2,1)S(1)}, u32[]{:S(2)}, u32[]{:S(2)}) %collective-permute-start.26) | collective-permute-done | bytes 368672 | tf_op jit(solution)/shard_map/ppermute | solution.py:38
  84.7 13.3 %expand.1 = (f32[512,768]{1,0:T(8,128)S(1)}, f32[512,1]{1,0:T(8,128)S(1)}, bf16[512,3072]{1,0:T(8,128)(2,1)S(1)}, bf16[512,3072]{1,0:T(8,128)(2,1)S(1)}) custom-call(s32[8]{0:T(128)S(1)} %iota_xor_fusion.places, f32[512,768]{1,0:T(8,128)S(1)} %get-tuple-element.140.projected_ref, f32[8,768]{1,0:T(8,128)S(1)} %add_add_fusion.1.sums_ref, ...), custom_call_target="tpu_custom_call" | custom-call | flops 1024 | bytes 1024 | tf_op jit(solution)/shard_map/expand/pallas_call | solution.py:276
  102.0 5.8 %collective-permute-done.33 = bf16[192,768]{1,0:T(8,128)(2,1)S(1)} collective-permute-done((bf16[192,768]{1,0:T(8,128)(2,1)S(1)}, bf16[192,768]{1,0:T(8,128)(2,1)S(1)}, u32[]{:S(2)}, u32[]{:S(2)}) %collective-permute-start.33) | collective-permute-done | bytes 294944 | tf_op jit(solution)/shard_map/ppermute | solution.py:38
  110.5 9.8 %contract.1 = (bf16[4,384,768]{2,1,0:T(8,128)(2,1)S(1)}, bf16[4,384,768]{2,1,0:T(8,128)(2,1)S(1)}, bf16[512,768]{1,0:T(8,128)(2,1)}, f32[512,768]{1,0:T(8,128)S(1)}, f32[2,768]{1,0:T(2,128)S(1)}) custom-call(s32[8]{0:T(128)S(1)} %iota_xor_fusion.places, f32[512,768]{1,0:T(8,128)S(1)} %get-tuple-element.153.hat_ref, f32[8,768]{1,0:T(8,128)S(1)} %add_add_fusion.1.sums_ref, ...), custom_call_target="tpu_custom_call" | custom-call | flops 1024 | bytes 1024 | tf_op jit(solution)/shard_map/contract/pallas_call | solution.py:276
  120.5 11.3 %hidden_back.1 = (bf16[4,384,768]{2,1,0:T(8,128)(2,1)S(1)}, bf16[4,384,768]{2,1,0:T(8,128)(2,1)S(1)}, bf16[512,3072]{1,0:T(8,128)(2,1)S(1)}) custom-call(s32[8]{0:T(128)S(1)} %iota_xor_fusion.places, f32[512,768]{1,0:T(8,128)S(1)} %get-tuple-element.161.back_ref, f32[512,768]{1,0:T(8,128)S(1)} %get-tuple-element.153.hat_ref, ...), custom_call_target="tpu_custom_call" | custom-call | flops 1024 | bytes 1024 | tf_op jit(solution)/shard_map/hidden_back/pallas_call | solution.py:276
  134.7 12.7 %expand_back.1 = (f32[512,768]{1,0:T(8,128)S(1)}, bf16[512,768]{1,0:T(8,128)(2,1)S(1)}, bf16[768,512]{1,0:T(8,128)(2,1)S(1)}, f32[2,768]{1,0:T(2,128)S(1)}, bf16[1152,512]{1,0:T(8,128)(2,1)S(1)}) custom-call(s32[8]{0:T(128)S(1)} %iota_xor_fusion.places, f32[512,768]{1,0:T(8,128)S(1)} %get-tuple-element.161.back_ref, ...), custom_call_target="tpu_custom_call" | custom-call | flops 1024 | bytes 1024 | tf_op jit(solution)/shard_map/expand_back/pallas_call | solution.py:276
  152.1 8.2 %attend_back.1 = (bf16[2304,512]{1,0:T(8,128)(2,1)S(1)}, f32[512,768]{1,0:T(8,128)S(1)}, f32[2,768]{1,0:T(2,128)S(1)}) custom-call(s32[8]{0:T(128)S(1)} %iota_xor_fusion.places, bf16[2304,512]{1,0:T(8,128)(2,1)S(1)} %get-tuple-element.170.packed_ref, bf16[768,512]{1,0:T(8,128)(2,1)S(1)} %get-tuple-element.180.mixed_back_ref, ...), custom_call_target="tpu_custom_call" | custom-call | flops 1024 | bytes 1024 | tf_op jit(solution)/shard_map/attend_back/pallas_call | solution.py:276
  163.3 2.2 collective-permute-done.41
  165.5 2.6 collective-permute-start.42
  168.1 2.1 collective-permute-done.42
  177.8 6.0 %project_back.1 = (bf16[4,352,768]{2,1,0:T(8,128)(2,1)S(1)}, bf16[4,352,768]{2,1,0:T(8,128)(2,1)}, bf16[512,768]{1,0:T(8,128)(2,1)S(1)}) custom-call(s32[8]{0:T(128)S(1)} %iota_xor_fusion.places, f32[512,768]{1,0:T(8,128)S(1)} %get-tuple-element.182.embedded_ref, f32[512,768]{1,0:T(8,128)S(1)} %get-tuple-element.140.projected_ref, ...), custom_call_target="tpu_custom_call" | custom-call | flops 1024 | bytes 1024 | tf_op jit(solution)/shard_map/project_back/pallas_call | solution.py:276
  188.0 3.5 %collective-permute-start.52 = (bf16[384,768]{1,0:T(8,128)(2,1)S(1)}, bf16[384,768]{1,0:T(8,128)(2,1)S(1)}, u32[]{:S(2)}, u32[]{:S(2)}) collective-permute-start(bf16[384,768]{1,0:T(8,128)(2,1)S(1)} %pad_maximum_fusion.3), channel_id=1, source_target_pairs={{0,8},{24,16},{1,9},{25,17},{2,10},{26,18},{3,11},{27,19},{4,12},{... | collective-permute-start | bytes 1769480 | tf_op jit(solution)/shard_map/ppermute | solution.py:134
  191.6 4.5 %packed_gradient.1 = (bf16[4,96,2304]{2,1,0:T(8,128)(2,1)S(1)}, bf16[4,96,2304]{2,1,0:T(8,128)(2,1)S(1)}) custom-call(s32[8]{0:T(128)S(1)} %iota_xor_fusion.places, f32[512,768]{1,0:T(8,128)S(1)} %get-tuple-element.140.projected_ref, f32[8,768]{1,0:T(8,128)S(1)} %add_add_fusion.1.sums_ref, bf16[2304,512]{1,0:T(8,128)(2,1)} %copy-done.10), custom_call_target="tpu_custom_call" | custom-call | flops 1024 | bytes 1024 | tf_op jit(solution)/shard_map/packed_gradient/pallas_call | solution.py:276
  205.1 8.8 %collective-permute-done.51 = bf16[2,176,768]{2,1,0:T(8,128)(2,1)S(1)} collective-permute-done((bf16[2,176,768]{2,1,0:T(8,128)(2,1)S(1)}, bf16[2,176,768]{2,1,0:T(8,128)(2,1)S(1)}, u32[]{:S(2)}, u32[]{:S(2)}) %collective-permute-start.51) | collective-permute-done | bytes 540704 | tf_op jit(solution)/shard_map/ppermute | solution.py:38
  221.7 4.2 %collective-permute-done.57 = bf16[176,768]{1,0:T(8,128)(2,1)S(1)} collective-permute-done((bf16[176,768]{1,0:T(8,128)(2,1)S(1)}, bf16[176,768]{1,0:T(8,128)(2,1)S(1)}, u32[]{:S(2)}, u32[]{:S(2)}) %collective-permute-start.57) | collective-permute-done | bytes 270368 | tf_op jit(solution)/shard_map/ppermute | solution.py:38
  228.5 4.6 %collective-permute-start.63 = (bf16[352,768]{1,0:T(8,128)(2,1)S(1)}, bf16[352,768]{1,0:T(8,128)(2,1)S(1)}, u32[]{:S(2)}, u32[]{:S(2)}) collective-permute-start(bf16[352,768]{1,0:T(8,128)(2,1)S(1)} %pad_maximum_fusion.5), channel_id=1, source_target_pairs={{0,8},{24,16},{1,9},{25,17},{2,10},{26,18},{3,11},{27,19},{4,12},{... | collective-permute-start | bytes 1622024 | tf_op jit(solution)/shard_map/ppermute | solution.py:134
  237.9 3.4 %collective-permute-done.63 = bf16[352,768]{1,0:T(8,128)(2,1)S(1)} collective-permute-done((bf16[352,768]{1,0:T(8,128)(2,1)S(1)}, bf16[352,768]{1,0:T(8,128)(2,1)S(1)}, u32[]{:S(2)}, u32[]{:S(2)}) %collective-permute-start.63) | collective-permute-done | bytes 540704 | tf_op jit(solution)/shard_map/ppermute | solution.py:134
  242.5 7.2 %collective-permute-start.65 = (bf16[96,2304]{1,0:T(8,128)(2,1)S(1)}, bf16[96,2304]{1,0:T(8,128)(2,1)S(1)}, u32[]{:S(2)}, u32[]{:S(2)}) collective-permute-start(bf16[96,2304]{1,0:T(8,128)(2,1)S(1)} %pad_maximum_fusion.6), channel_id=1, source_target_pairs={{0,8},{24,16},{1,9},{25,17},{2,10},{26,18},{3,11},{27,19},{4,12},{... | collective-permute-start | bytes 1327112 | tf_op jit(solution)/shard_map/ppermute | solution.py:134
  250.9 4.5 %collective-permute-done.65 = bf16[96,2304]{1,0:T(8,128)(2,1)S(1)} collective-permute-done((bf16[96,2304]{1,0:T(8,128)(2,1)S(1)}, bf16[96,2304]{1,0:T(8,128)(2,1)S(1)}, u32[]{:S(2)}, u32[]{:S(2)}) %collective-permute-start.65) | collective-permute-done | bytes 442400 | tf_op jit(solution)/shard_map/ppermute | solution.py:134
  257.8 6.9 %input_gradient.1 = f32[512,2048]{1,0:T(8,128)} custom-call(s32[8]{0:T(128)S(1)} %iota_xor_fusion.places, bf16[512,768]{1,0:T(8,128)(2,1)S(1)} %get-tuple-element.201.low_ref, bf16[256,768]{1,0:T(8,128)(2,1)} %refs_0_.7, bf16[256,768]{1,0:T(8,128)(2,1)} %copy-done.16, bf16[256,768]{1,0:T(8,128)(2,1)} %copy-done.32, bf16[256,768]{1,0:T(8,128)(2,1)} %copy-done.17, ...), custom_call_target="tpu_custom_call" | custom-call | flops 1024 | bytes 1024 | tf_op jit(solution)/shard_map/input_gradient/pallas_call | solution.py:276
  267.2 5.8 %collective-permute-done.67 = bf16[352,768]{1,0:T(8,128)(2,1)S(1)} collective-permute-done((bf16[352,768]{1,0:T(8,128)(2,1)S(1)}, bf16[352,768]{1,0:T(8,128)(2,1)S(1)}, u32[]{:S(2)}, u32[]{:S(2)}) %collective-permute-start.67) | collective-permute-done | bytes 540704 | tf_op jit(solution)/shard_map/ppermute | solution.py:134
  274.8 3.9 %collective-permute-done.69 = bf16[96,2304]{1,0:T(8,128)(2,1)S(1)} collective-permute-done((bf16[96,2304]{1,0:T(8,128)(2,1)S(1)}, bf16[96,2304]{1,0:T(8,128)(2,1)S(1)}, u32[]{:S(2)}, u32[]{:S(2)}) %collective-permute-start.69) | collective-permute-done | bytes 442400 | tf_op jit(solution)/shard_map/ppermute | solution.py:134
  (274 shorter events, 95.5 us)
Async XLA Ops:
  3.7 19.2 %collective-permute-start.1 = (bf16[256,768]{1,0:T(8,128)(2,1)}, bf16[256,768]{1,0:T(8,128)(2,1)S(1)}, u32[]{:S(2)}, u32[]{:S(2)}) collective-permute-start(bf16[256,768]{1,0:T(8,128)(2,1)} %refs_0_.7), channel_id=1, source_target_pairs={{0,4},{1,5},{2,6},{3,7},{4,0},{5,1},{6,2},{7,3},{8,12},{9,13},{10,... | collective-permute-start | bytes 1179656 | tf_op jit(solution)/shard_map/ppermute | solution.py:38
  5.2 17.7 %collective-permute-start.2 = (bf16[256,768]{1,0:T(8,128)(2,1)}, bf16[256,768]{1,0:T(8,128)(2,1)S(1)}, u32[]{:S(2)}, u32[]{:S(2)}) collective-permute-start(bf16[256,768]{1,0:T(8,128)(2,1)} %refs_0_.7), channel_id=1, source_target_pairs={{0,6},{1,7},{2,4},{3,5},{4,2},{5,3},{6,0},{7,1},{8,14},{9,15},{10,... | collective-permute-start | bytes 1179656 | tf_op jit(solution)/shard_map/ppermute | solution.py:38
  24.0 20.8 %collective-permute-start.13 = (bf16[96,2304]{1,0:T(8,128)(2,1)}, bf16[96,2304]{1,0:T(8,128)(2,1)}, u32[]{:S(2)}, u32[]{:S(2)}) collective-permute-start(bf16[96,2304]{1,0:T(8,128)(2,1)} %refs_0_.6), channel_id=1, source_target_pairs={{0,2},{1,3},{2,0},{3,1},{4,6},{5,7},{6,4},{7,5},{8,10},{9,11},{10,... | collective-permute-start | bytes 1327112 | tf_op jit(solution)/shard_map/ppermute | solution.py:38
  25.1 21.3 %collective-permute-start.14 = (bf16[96,2304]{1,0:T(8,128)(2,1)}, bf16[96,2304]{1,0:T(8,128)(2,1)}, u32[]{:S(2)}, u32[]{:S(2)}) collective-permute-start(bf16[96,2304]{1,0:T(8,128)(2,1)} %refs_0_.6), channel_id=1, source_target_pairs={{0,4},{1,5},{2,6},{3,7},{4,0},{5,1},{6,2},{7,3},{8,12},{9,13},{10,... | collective-permute-start | bytes 1327112 | tf_op jit(solution)/shard_map/ppermute | solution.py:38
  26.4 21.0 %collective-permute-start.15 = (bf16[96,2304]{1,0:T(8,128)(2,1)}, bf16[96,2304]{1,0:T(8,128)(2,1)}, u32[]{:S(2)}, u32[]{:S(2)}) collective-permute-start(bf16[96,2304]{1,0:T(8,128)(2,1)} %refs_0_.6), channel_id=1, source_target_pairs={{0,6},{1,7},{2,4},{3,5},{4,2},{5,3},{6,0},{7,1},{8,14},{9,15},{10,... | collective-permute-start | bytes 1327112 | tf_op jit(solution)/shard_map/ppermute | solution.py:38
  49.5 17.5 %collective-permute-start.21 = (bf16[96,3840]{1,0:T(8,128)(2,1)}, bf16[96,3840]{1,0:T(8,128)(2,1)}, u32[]{:S(2)}, u32[]{:S(2)}) collective-permute-start(bf16[96,3840]{1,0:T(8,128)(2,1)} %constant_dynamic-update-slice_fusion.refs_0_), channel_id=1, source_target_pairs={{0,2},{1,3},{2,0},{3,1},{4,6},{5,7},{6,4},{7,5},{8,10},{9,11},{10,... | collective-permute-start | bytes 2211848 | tf_op jit(solution)/shard_map/ppermute | solution.py:38
  50.7 17.4 %collective-permute-start.22 = (bf16[96,3840]{1,0:T(8,128)(2,1)}, bf16[96,3840]{1,0:T(8,128)(2,1)}, u32[]{:S(2)}, u32[]{:S(2)}) collective-permute-start(bf16[96,3840]{1,0:T(8,128)(2,1)} %constant_dynamic-update-slice_fusion.refs_0_), channel_id=1, source_target_pairs={{0,4},{1,5},{2,6},{3,7},{4,0},{5,1},{6,2},{7,3},{8,12},{9,13},{10,... | collective-permute-start | bytes 2211848 | tf_op jit(solution)/shard_map/ppermute | solution.py:38
  69.6 14.5 %collective-permute-start.20 = (bf16[96,3840]{1,0:T(8,128)(2,1)}, bf16[96,3840]{1,0:T(8,128)(2,1)S(1)}, u32[]{:S(2)}, u32[]{:S(2)}) collective-permute-start(bf16[96,3840]{1,0:T(8,128)(2,1)} %constant_dynamic-update-slice_fusion.refs_0_), channel_id=1, source_target_pairs={{0,1},{1,0},{2,3},{3,2},{4,5},{5,4},{6,7},{7,6},{8,9},{9,8},{10,11... | collective-permute-start | bytes 2211848 | tf_op jit(solution)/shard_map/ppermute | solution.py:38
  70.6 14.1 %collective-permute-start.23 = (bf16[96,3840]{1,0:T(8,128)(2,1)}, bf16[96,3840]{1,0:T(8,128)(2,1)S(1)}, u32[]{:S(2)}, u32[]{:S(2)}) collective-permute-start(bf16[96,3840]{1,0:T(8,128)(2,1)} %collective-permute-done.21.refs_2_), channel_id=1, source_target_pairs={{0,1},{1,0},{2,3},{3,2},{4,5},{5,4},{6,7},{7,6},{8,9},{9,8},{10,11... | collective-permute-start | bytes 2211848 | tf_op jit(solution)/shard_map/ppermute | solution.py:38
  71.2 13.5 %collective-permute-start.24 = (bf16[96,3840]{1,0:T(8,128)(2,1)}, bf16[96,3840]{1,0:T(8,128)(2,1)S(1)}, u32[]{:S(2)}, u32[]{:S(2)}) collective-permute-start(bf16[96,3840]{1,0:T(8,128)(2,1)} %collective-permute-done.22.refs_4_), channel_id=1, source_target_pairs={{0,1},{1,0},{2,3},{3,2},{4,5},{5,4},{6,7},{7,6},{8,9},{9,8},{10,11... | collective-permute-start | bytes 2211848 | tf_op jit(solution)/shard_map/ppermute | solution.py:38
  82.3 15.7 %collective-permute-start.29 = (bf16[384,768]{1,0:T(8,128)(2,1)S(1)}, bf16[384,768]{1,0:T(8,128)(2,1)S(1)}, u32[]{:S(2)}, u32[]{:S(2)}) collective-permute-start(bf16[384,768]{1,0:T(8,128)(2,1)S(1)} %copy-done.25), channel_id=1, source_target_pairs={{0,2},{1,3},{2,0},{3,1},{4,6},{5,7},{6,4},{7,5},{8,10},{9,11},{10,... | collective-permute-start | bytes 1769480 | tf_op jit(solution)/shard_map/ppermute | solution.py:38
  84.1 15.4 %collective-permute-start.30 = (bf16[384,768]{1,0:T(8,128)(2,1)S(1)}, bf16[384,768]{1,0:T(8,128)(2,1)S(1)}, u32[]{:S(2)}, u32[]{:S(2)}) collective-permute-start(bf16[384,768]{1,0:T(8,128)(2,1)S(1)} %copy-done.25), channel_id=1, source_target_pairs={{0,4},{1,5},{2,6},{3,7},{4,0},{5,1},{6,2},{7,3},{8,12},{9,13},{10,... | collective-permute-start | bytes 1769480 | tf_op jit(solution)/shard_map/ppermute | solution.py:38
  131.8 15.5 %collective-permute-start.39 = (bf16[4,384,768]{2,1,0:T(8,128)(2,1)S(1)}, bf16[4,384,768]{2,1,0:T(8,128)(2,1)S(1)}, u32[]{:S(2)}, u32[]{:S(2)}) collective-permute-start(bf16[4,384,768]{2,1,0:T(8,128)(2,1)S(1)} %get-tuple-element.167), channel_id=1, source_target_pairs={{0,1},{1,0},{2,3},{3,2},{4,5},{5,4},{6,7},{7,6},{8,9},{9,8},{10,11... | collective-permute-start | bytes 7077896 | tf_op jit(solution)/shard_map/ppermute | solution.py:38
  132.4 15.4 %collective-permute-start.38 = (bf16[2,192,768]{2,1,0:T(8,128)(2,1)S(1)}, bf16[2,192,768]{2,1,0:T(8,128)(2,1)S(1)}, u32[]{:S(2)}, u32[]{:S(2)}) collective-permute-start(bf16[2,192,768]{2,1,0:T(8,128)(2,1)S(1)} %add_convert_fusion.6), channel_id=1, source_target_pairs={{0,4},{1,5},{2,6},{3,7},{4,0},{5,1},{6,2},{7,3},{8,12},{9,13},{10,... | collective-permute-start | bytes 1769480 | tf_op jit(solution)/shard_map/ppermute | solution.py:38
  133.8 15.1 %collective-permute-start.37 = (bf16[2,192,768]{2,1,0:T(8,128)(2,1)S(1)}, bf16[2,192,768]{2,1,0:T(8,128)(2,1)S(1)}, u32[]{:S(2)}, u32[]{:S(2)}) collective-permute-start(bf16[2,192,768]{2,1,0:T(8,128)(2,1)S(1)} %add_convert_fusion.7), channel_id=1, source_target_pairs={{0,2},{1,3},{2,0},{3,1},{4,6},{5,7},{6,4},{7,5},{8,10},{9,11},{10,... | collective-permute-start | bytes 1769480 | tf_op jit(solution)/shard_map/ppermute | solution.py:38
  149.5 20.8 %collective-permute-start.44 = (bf16[576,768]{1,0:T(8,128)(2,1)S(1)}, bf16[576,768]{1,0:T(8,128)(2,1)S(1)}, u32[]{:S(2)}, u32[]{:S(2)}) collective-permute-start(bf16[576,768]{1,0:T(8,128)(2,1)S(1)} %pad_maximum_fusion.2), channel_id=1, source_target_pairs={{0,4},{1,5},{2,6},{3,7},{4,0},{5,1},{6,2},{7,3},{8,12},{9,13},{10,... | collective-permute-start | bytes 2654216 | tf_op jit(solution)/shard_map/ppermute | solution.py:38
  150.7 20.3 %collective-permute-start.43 = (bf16[576,768]{1,0:T(8,128)(2,1)S(1)}, bf16[576,768]{1,0:T(8,128)(2,1)S(1)}, u32[]{:S(2)}, u32[]{:S(2)}) collective-permute-start(bf16[576,768]{1,0:T(8,128)(2,1)S(1)} %pad_maximum_fusion.1), channel_id=1, source_target_pairs={{0,2},{1,3},{2,0},{3,1},{4,6},{5,7},{6,4},{7,5},{8,10},{9,11},{10,... | collective-permute-start | bytes 2654216 | tf_op jit(solution)/shard_map/ppermute | solution.py:38
  185.9 14.6 %collective-permute-start.53 = (bf16[192,768]{1,0:T(8,128)(2,1)}, bf16[192,768]{1,0:T(8,128)(2,1)S(1)}, u32[]{:S(2)}, u32[]{:S(2)}) collective-permute-start(bf16[192,768]{1,0:T(8,128)(2,1)} %get-tuple-element.262), channel_id=1, source_target_pairs={{0,4},{1,5},{2,6},{3,7},{4,0},{5,1},{6,2},{7,3},{8,12},{9,13},{10,... | collective-permute-start | bytes 884744 | tf_op jit(solution)/shard_map/ppermute | solution.py:38
  187.3 14.0 %collective-permute-start.54 = (bf16[192,768]{1,0:T(8,128)(2,1)S(1)}, bf16[192,768]{1,0:T(8,128)(2,1)S(1)}, u32[]{:S(2)}, u32[]{:S(2)}) collective-permute-start(bf16[192,768]{1,0:T(8,128)(2,1)S(1)} %get-tuple-element.261), channel_id=1, source_target_pairs={{0,2},{1,3},{2,0},{3,1},{4,6},{5,7},{6,4},{7,5},{8,10},{9,11},{10,... | collective-permute-start | bytes 884744 | tf_op jit(solution)/shard_map/ppermute | solution.py:38
  188.0 16.2 %collective-permute-start.52 = (bf16[384,768]{1,0:T(8,128)(2,1)S(1)}, bf16[384,768]{1,0:T(8,128)(2,1)S(1)}, u32[]{:S(2)}, u32[]{:S(2)}) collective-permute-start(bf16[384,768]{1,0:T(8,128)(2,1)S(1)} %pad_maximum_fusion.3), channel_id=1, source_target_pairs={{0,8},{24,16},{1,9},{25,17},{2,10},{26,18},{3,11},{27,19},{4,12},{... | collective-permute-start | bytes 1769480 | tf_op jit(solution)/shard_map/ppermute | solution.py:134
  196.1 20.0 %collective-permute-start.48 = (bf16[4,96,2304]{2,1,0:T(8,128)(2,1)S(1)}, bf16[4,96,2304]{2,1,0:T(8,128)(2,1)S(1)}, u32[]{:S(2)}, u32[]{:S(2)}) collective-permute-start(bf16[4,96,2304]{2,1,0:T(8,128)(2,1)S(1)} %get-tuple-element.205), channel_id=1, source_target_pairs={{0,1},{1,0},{2,3},{3,2},{4,5},{5,4},{6,7},{7,6},{8,9},{9,8},{10,11... | collective-permute-start | bytes 5308424 | tf_op jit(solution)/shard_map/ppermute | solution.py:38
  199.2 14.7 %collective-permute-start.51 = (bf16[2,176,768]{2,1,0:T(8,128)(2,1)S(1)}, bf16[2,176,768]{2,1,0:T(8,128)(2,1)S(1)}, u32[]{:S(2)}, u32[]{:S(2)}) collective-permute-start(bf16[2,176,768]{2,1,0:T(8,128)(2,1)S(1)} %add_convert_fusion.10), channel_id=1, source_target_pairs={{0,4},{1,5},{2,6},{3,7},{4,0},{5,1},{6,2},{7,3},{8,12},{9,13},{10,... | collective-permute-start | bytes 1622024 | tf_op jit(solution)/shard_map/ppermute | solution.py:38
  200.5 14.5 %collective-permute-start.50 = (bf16[2,176,768]{2,1,0:T(8,128)(2,1)S(1)}, bf16[2,176,768]{2,1,0:T(8,128)(2,1)S(1)}, u32[]{:S(2)}, u32[]{:S(2)}) collective-permute-start(bf16[2,176,768]{2,1,0:T(8,128)(2,1)S(1)} %add_convert_fusion.11), channel_id=1, source_target_pairs={{0,2},{1,3},{2,0},{3,1},{4,6},{5,7},{6,4},{7,5},{8,10},{9,11},{10,... | collective-permute-start | bytes 1622024 | tf_op jit(solution)/shard_map/ppermute | solution.py:38
  202.9 16.4 %collective-permute-start.60 = (bf16[384,768]{1,0:T(8,128)(2,1)S(1)}, bf16[384,768]{1,0:T(8,128)(2,1)S(1)}, u32[]{:S(2)}, u32[]{:S(2)}) collective-permute-start(bf16[384,768]{1,0:T(8,128)(2,1)S(1)} %pad_maximum_fusion.4), channel_id=1, source_target_pairs={{0,8},{24,16},{1,9},{25,17},{2,10},{26,18},{3,11},{27,19},{4,12},{... | collective-permute-start | bytes 1769480 | tf_op jit(solution)/shard_map/ppermute | solution.py:134
  204.4 16.4 %collective-permute-start.59 = (bf16[384,768]{1,0:T(8,128)(2,1)S(1)}, bf16[384,768]{1,0:T(8,128)(2,1)S(1)}, u32[]{:S(2)}, u32[]{:S(2)}) collective-permute-start(bf16[384,768]{1,0:T(8,128)(2,1)S(1)} %add_convert_fusion.3), channel_id=1, source_target_pairs={{8,16},{16,8},{9,17},{17,9},{10,18},{18,10},{11,19},{19,11},{12,20... | collective-permute-start | bytes 1769480 | tf_op jit(solution)/shard_map/ppermute | solution.py:134
  218.7 15.0 %collective-permute-start.56 = (bf16[2,48,2304]{2,1,0:T(8,128)(2,1)S(1)}, bf16[2,48,2304]{2,1,0:T(8,128)(2,1)S(1)}, u32[]{:S(2)}, u32[]{:S(2)}) collective-permute-start(bf16[2,48,2304]{2,1,0:T(8,128)(2,1)S(1)} %add_convert_fusion.14), channel_id=1, source_target_pairs={{0,4},{1,5},{2,6},{3,7},{4,0},{5,1},{6,2},{7,3},{8,12},{9,13},{10,... | collective-permute-start | bytes 1327112 | tf_op jit(solution)/shard_map/ppermute | solution.py:38
  219.4 15.0 %collective-permute-start.55 = (bf16[2,48,2304]{2,1,0:T(8,128)(2,1)S(1)}, bf16[2,48,2304]{2,1,0:T(8,128)(2,1)S(1)}, u32[]{:S(2)}, u32[]{:S(2)}) collective-permute-start(bf16[2,48,2304]{2,1,0:T(8,128)(2,1)S(1)} %add_convert_fusion.15), channel_id=1, source_target_pairs={{0,2},{1,3},{2,0},{3,1},{4,6},{5,7},{6,4},{7,5},{8,10},{9,11},{10,... | collective-permute-start | bytes 1327112 | tf_op jit(solution)/shard_map/ppermute | solution.py:38
  220.8 15.6 %collective-permute-start.64 = (bf16[384,768]{1,0:T(8,128)(2,1)S(1)}, bf16[384,768]{1,0:T(8,128)(2,1)S(1)}, u32[]{:S(2)}, u32[]{:S(2)}) collective-permute-start(bf16[384,768]{1,0:T(8,128)(2,1)S(1)} %add_convert_fusion.2), channel_id=1, source_target_pairs={{8,16},{16,8},{9,17},{17,9},{10,18},{18,10},{11,19},{19,11},{12,20... | collective-permute-start | bytes 1769480 | tf_op jit(solution)/shard_map/ppermute | solution.py:134
  225.9 23.9 %collective-permute-start.71 = (bf16[384,768]{1,0:T(8,128)(2,1)S(1)}, bf16[384,768]{1,0:T(8,128)(2,1)S(1)}, u32[]{:S(2)}, u32[]{:S(2)}) collective-permute-start(bf16[384,768]{1,0:T(8,128)(2,1)S(1)} %add_convert_fusion.1), channel_id=1, source_target_pairs={{8,0},{16,24},{9,1},{17,25},{10,2},{18,26},{11,3},{19,27},{12,4},{... | collective-permute-start | bytes 1769480 | tf_op jit(solution)/shard_map/ppermute | solution.py:134
  236.6 19.7 %collective-permute-start.70 = (bf16[384,768]{1,0:T(8,128)(2,1)S(1)}, bf16[384,768]{1,0:T(8,128)(2,1)S(1)}, u32[]{:S(2)}, u32[]{:S(2)}) collective-permute-start(bf16[384,768]{1,0:T(8,128)(2,1)S(1)} %add_convert_fusion), channel_id=1, source_target_pairs={{8,0},{16,24},{9,1},{17,25},{10,2},{18,26},{11,3},{19,27},{12,4},{... | collective-permute-start | bytes 1769480 | tf_op jit(solution)/shard_map/ppermute | solution.py:134
  256.5 16.6 %collective-permute-start.67 = (bf16[352,768]{1,0:T(8,128)(2,1)S(1)}, bf16[352,768]{1,0:T(8,128)(2,1)S(1)}, u32[]{:S(2)}, u32[]{:S(2)}) collective-permute-start(bf16[352,768]{1,0:T(8,128)(2,1)S(1)} %add_convert_fusion.8), channel_id=1, source_target_pairs={{8,0},{16,24},{9,1},{17,25},{10,2},{18,26},{11,3},{19,27},{12,4},{... | collective-permute-start | bytes 1622024 | tf_op jit(solution)/shard_map/ppermute | solution.py:134
  264.8 13.9 %collective-permute-start.69 = (bf16[96,2304]{1,0:T(8,128)(2,1)S(1)}, bf16[96,2304]{1,0:T(8,128)(2,1)S(1)}, u32[]{:S(2)}, u32[]{:S(2)}) collective-permute-start(bf16[96,2304]{1,0:T(8,128)(2,1)S(1)} %add_convert_fusion.12), channel_id=1, source_target_pairs={{8,0},{16,24},{9,1},{17,25},{10,2},{18,26},{11,3},{19,27},{12,4},{... | collective-permute-start | bytes 1327112 | tf_op jit(solution)/shard_map/ppermute | solution.py:134
  (76 other events, 646.5 us)

commit v4 on v3

--- a/solution.py
+++ b/solution.py
@@ -212,7 +212,7 @@
 
         return
 
-    @pl.loop(0, chips)
+    @pl.loop(0, chips, unroll=2)
     def _(j):
         for k in range(2):
             halves[k][j, :rows] = make(places[2 * j + k] * rows, rows).astype(LOW)

time: 280 us -> 279 us (level)
  no operation moved by 1% of the time
where the time goes in v4:
time: 279 us
  Pallas kernels  88.7 us (32%)
  waiting for transfers between devices  86.7 us (31%)
  starting transfers between devices  75.6 us (27%)
  other arithmetic  13.6 us (5%)
  local copies, waits for them, and re-layouts  12.5 us (4%)
    pallas_call x10, Pallas kernels, call(): pl.pallas_call(kernel, in_specs=[pl.BlockSpec(memory_space=space) for spa...  88.7 us
    ppermute x60, waiting for transfers between devices, swap(): return lax.ppermute(values, axis, [(i, i ^ step) for i in range(size)])  69 us
    ppermute x60, starting transfers between devices, swap(): return lax.ppermute(values, axis, [(i, i ^ step) for i in range(size)])  51 us
    ppermute x12, starting transfers between devices, step(): self.came = lax.ppermute(self.part, 'dp', self.pairs[self.number])  24.6 us
    ppermute x12, waiting for transfers between devices, step(): self.came = lax.ppermute(self.part, 'dp', self.pairs[self.number])  17.6 us
    convert_element_type x24, other arithmetic, add_low(): return total.astype(LOW)  9.11 us
  transfers between devices with their start and end apart: 72, of which 35 were waited for; matrix products, arithmetic and copies ran while one was open for 8% of the time, Pallas kernels for 26%

profile of v4, /device:TPU:0, one launch (start us, length us, event | category | flops | bytes accessed | tf_op | source)
XLA Modules:
  0.0 278.7 jit_solution(7333709838310404190)
XLA Ops:
  0.6 3.0 %collective-permute-start = (bf16[256,768]{1,0:T(8,128)(2,1)}, bf16[256,768]{1,0:T(8,128)(2,1)S(1)}, u32[]{:S(2)}, u32[]{:S(2)}) collective-permute-start(bf16[256,768]{1,0:T(8,128)(2,1)} %refs_0_.7), channel_id=1, source_target_pairs={{0,2},{1,3},{2,0},{3,1},{4,6},{5,7},{6,4},{7,5},{8,10},{9,11},{10,... | collective-permute-start | bytes 1179656 | tf_op jit(solution)/shard_map/ppermute | solution.py:38
  9.9 3.9 %collective-permute-done.refs_2_ = bf16[256,768]{1,0:T(8,128)(2,1)S(1)} collective-permute-done((bf16[256,768]{1,0:T(8,128)(2,1)}, bf16[256,768]{1,0:T(8,128)(2,1)S(1)}, u32[]{:S(2)}, u32[]{:S(2)}) %collective-permute-start) | collective-permute-done | bytes 393248 | tf_op jit(solution)/shard_map/ppermute | solution.py:38
  13.8 9.1 %collective-permute-done.1.refs_4_ = bf16[256,768]{1,0:T(8,128)(2,1)S(1)} collective-permute-done((bf16[256,768]{1,0:T(8,128)(2,1)}, bf16[256,768]{1,0:T(8,128)(2,1)S(1)}, u32[]{:S(2)}, u32[]{:S(2)}) %collective-permute-start.1) | collective-permute-done | bytes 393248 | tf_op jit(solution)/shard_map/ppermute | solution.py:38
  28.1 5.0 %project.1 = (f32[512,768]{1,0:T(8,128)S(1)}, f32[8,768]{1,0:T(8,128)S(1)}) custom-call(s32[8]{0:T(128)S(1)} %iota_xor_fusion.places, bf16[512,2048]{1,0:T(8,128)(2,1)} %bitcast.75, f32[8,768]{1,0:T(8,128)S(1)} %dynamic_update_slice.3.params_ref, bf16[256,768]{1,0:T(8,128)(2,1)} %refs_0_.7, bf16[256,768]{1,0:T(8,128)(2,1)S(1)} %collective-permute-done.3.refs_1_, ...), custom_call_target="tpu_custom_call" | custom-call | flops 1024 | bytes 1024 | tf_op jit(solution)/shard_map/project/pallas_call | solution.py:276
  36.0 2.3 collective-permute-done.8
  38.2 2.6 collective-permute-start.9
  40.8 2.1 collective-permute-done.9
  47.6 2.0 collective-permute-done.12
  55.2 11.7 %attend.1 = (bf16[2304,512]{1,0:T(8,128)(2,1)S(1)}, bf16[768,512]{1,0:T(8,128)(2,1)S(1)}, f32[12,512]{1,0:T(8,128)S(1)}) custom-call(s32[8]{0:T(128)S(1)} %iota_xor_fusion.places, f32[512,768]{1,0:T(8,128)S(1)} %get-tuple-element.140.projected_ref, f32[8,768]{1,0:T(8,128)S(1)} %add_add_fusion.1.sums_ref, s32[1,512]{1,0:T(1,128)S(1)} %copy-done.20, ...), custom_call_target="tpu_custom_call" | custom-call | flops 1024 | bytes 1024 | tf_op jit(solution)/shard_map/attend/pallas_call | solution.py:276
  72.7 6.0 %collective-permute-done.25 = bf16[48,3840]{1,0:T(8,128)(2,1)S(1)} collective-permute-done((bf16[48,3840]{1,0:T(8,128)(2,1)S(1)}, bf16[48,3840]{1,0:T(8,128)(2,1)S(1)}, u32[]{:S(2)}, u32[]{:S(2)}) %collective-permute-start.25) | collective-permute-done | bytes 368672 | tf_op jit(solution)/shard_map/ppermute | solution.py:38
  78.8 3.4 %collective-permute-done.26 = bf16[48,3840]{1,0:T(8,128)(2,1)S(1)} collective-permute-done((bf16[48,3840]{1,0:T(8,128)(2,1)S(1)}, bf16[48,3840]{1,0:T(8,128)(2,1)S(1)}, u32[]{:S(2)}, u32[]{:S(2)}) %collective-permute-start.26) | collective-permute-done | bytes 368672 | tf_op jit(solution)/shard_map/ppermute | solution.py:38
  84.7 13.3 %expand.1 = (f32[512,768]{1,0:T(8,128)S(1)}, f32[512,1]{1,0:T(8,128)S(1)}, bf16[512,3072]{1,0:T(8,128)(2,1)S(1)}, bf16[512,3072]{1,0:T(8,128)(2,1)S(1)}) custom-call(s32[8]{0:T(128)S(1)} %iota_xor_fusion.places, f32[512,768]{1,0:T(8,128)S(1)} %get-tuple-element.140.projected_ref, f32[8,768]{1,0:T(8,128)S(1)} %add_add_fusion.1.sums_ref, ...), custom_call_target="tpu_custom_call" | custom-call | flops 1024 | bytes 1024 | tf_op jit(solution)/shard_map/expand/pallas_call | solution.py:276
  102.0 5.8 %collective-permute-done.33 = bf16[192,768]{1,0:T(8,128)(2,1)S(1)} collective-permute-done((bf16[192,768]{1,0:T(8,128)(2,1)S(1)}, bf16[192,768]{1,0:T(8,128)(2,1)S(1)}, u32[]{:S(2)}, u32[]{:S(2)}) %collective-permute-start.33) | collective-permute-done | bytes 294944 | tf_op jit(solution)/shard_map/ppermute | solution.py:38
  110.5 9.5 %contract.1 = (bf16[4,384,768]{2,1,0:T(8,128)(2,1)S(1)}, bf16[4,384,768]{2,1,0:T(8,128)(2,1)S(1)}, bf16[512,768]{1,0:T(8,128)(2,1)}, f32[512,768]{1,0:T(8,128)S(1)}, f32[2,768]{1,0:T(2,128)S(1)}) custom-call(s32[8]{0:T(128)S(1)} %iota_xor_fusion.places, f32[512,768]{1,0:T(8,128)S(1)} %get-tuple-element.153.hat_ref, f32[8,768]{1,0:T(8,128)S(1)} %add_add_fusion.1.sums_ref, ...), custom_call_target="tpu_custom_call" | custom-call | flops 1024 | bytes 1024 | tf_op jit(solution)/shard_map/contract/pallas_call | solution.py:276
  120.2 11.3 %hidden_back.1 = (bf16[4,384,768]{2,1,0:T(8,128)(2,1)S(1)}, bf16[4,384,768]{2,1,0:T(8,128)(2,1)S(1)}, bf16[512,3072]{1,0:T(8,128)(2,1)S(1)}) custom-call(s32[8]{0:T(128)S(1)} %iota_xor_fusion.places, f32[512,768]{1,0:T(8,128)S(1)} %get-tuple-element.161.back_ref, f32[512,768]{1,0:T(8,128)S(1)} %get-tuple-element.153.hat_ref, ...), custom_call_target="tpu_custom_call" | custom-call | flops 1024 | bytes 1024 | tf_op jit(solution)/shard_map/hidden_back/pallas_call | solution.py:276
  134.4 12.7 %expand_back.1 = (f32[512,768]{1,0:T(8,128)S(1)}, bf16[512,768]{1,0:T(8,128)(2,1)S(1)}, bf16[768,512]{1,0:T(8,128)(2,1)S(1)}, f32[2,768]{1,0:T(2,128)S(1)}, bf16[1152,512]{1,0:T(8,128)(2,1)S(1)}) custom-call(s32[8]{0:T(128)S(1)} %iota_xor_fusion.places, f32[512,768]{1,0:T(8,128)S(1)} %get-tuple-element.161.back_ref, ...), custom_call_target="tpu_custom_call" | custom-call | flops 1024 | bytes 1024 | tf_op jit(solution)/shard_map/expand_back/pallas_call | solution.py:276
  151.8 8.4 %attend_back.1 = (bf16[2304,512]{1,0:T(8,128)(2,1)S(1)}, f32[512,768]{1,0:T(8,128)S(1)}, f32[2,768]{1,0:T(2,128)S(1)}) custom-call(s32[8]{0:T(128)S(1)} %iota_xor_fusion.places, bf16[2304,512]{1,0:T(8,128)(2,1)S(1)} %get-tuple-element.170.packed_ref, bf16[768,512]{1,0:T(8,128)(2,1)S(1)} %get-tuple-element.180.mixed_back_ref, ...), custom_call_target="tpu_custom_call" | custom-call | flops 1024 | bytes 1024 | tf_op jit(solution)/shard_map/attend_back/pallas_call | solution.py:276
  163.2 2.2 collective-permute-done.41
  165.4 2.6 collective-permute-start.42
  168.0 2.1 collective-permute-done.42
  177.5 5.4 %project_back.1 = (bf16[4,352,768]{2,1,0:T(8,128)(2,1)S(1)}, bf16[4,352,768]{2,1,0:T(8,128)(2,1)}, bf16[512,768]{1,0:T(8,128)(2,1)S(1)}) custom-call(s32[8]{0:T(128)S(1)} %iota_xor_fusion.places, f32[512,768]{1,0:T(8,128)S(1)} %get-tuple-element.182.embedded_ref, f32[512,768]{1,0:T(8,128)S(1)} %get-tuple-element.140.projected_ref, ...), custom_call_target="tpu_custom_call" | custom-call | flops 1024 | bytes 1024 | tf_op jit(solution)/shard_map/project_back/pallas_call | solution.py:276
  187.1 3.5 %collective-permute-start.52 = (bf16[384,768]{1,0:T(8,128)(2,1)S(1)}, bf16[384,768]{1,0:T(8,128)(2,1)S(1)}, u32[]{:S(2)}, u32[]{:S(2)}) collective-permute-start(bf16[384,768]{1,0:T(8,128)(2,1)S(1)} %pad_maximum_fusion.3), channel_id=1, source_target_pairs={{0,8},{24,16},{1,9},{25,17},{2,10},{26,18},{3,11},{27,19},{4,12},{... | collective-permute-start | bytes 1769480 | tf_op jit(solution)/shard_map/ppermute | solution.py:134
  190.7 4.5 %packed_gradient.1 = (bf16[4,96,2304]{2,1,0:T(8,128)(2,1)S(1)}, bf16[4,96,2304]{2,1,0:T(8,128)(2,1)S(1)}) custom-call(s32[8]{0:T(128)S(1)} %iota_xor_fusion.places, f32[512,768]{1,0:T(8,128)S(1)} %get-tuple-element.140.projected_ref, f32[8,768]{1,0:T(8,128)S(1)} %add_add_fusion.1.sums_ref, bf16[2304,512]{1,0:T(8,128)(2,1)} %copy-done.10), custom_call_target="tpu_custom_call" | custom-call | flops 1024 | bytes 1024 | tf_op jit(solution)/shard_map/packed_gradient/pallas_call | solution.py:276
  204.2 8.7 %collective-permute-done.51 = bf16[2,176,768]{2,1,0:T(8,128)(2,1)S(1)} collective-permute-done((bf16[2,176,768]{2,1,0:T(8,128)(2,1)S(1)}, bf16[2,176,768]{2,1,0:T(8,128)(2,1)S(1)}, u32[]{:S(2)}, u32[]{:S(2)}) %collective-permute-start.51) | collective-permute-done | bytes 540704 | tf_op jit(solution)/shard_map/ppermute | solution.py:38
  220.8 4.2 %collective-permute-done.57 = bf16[176,768]{1,0:T(8,128)(2,1)S(1)} collective-permute-done((bf16[176,768]{1,0:T(8,128)(2,1)S(1)}, bf16[176,768]{1,0:T(8,128)(2,1)S(1)}, u32[]{:S(2)}, u32[]{:S(2)}) %collective-permute-start.57) | collective-permute-done | bytes 270368 | tf_op jit(solution)/shard_map/ppermute | solution.py:38
  227.6 4.6 %collective-permute-start.63 = (bf16[352,768]{1,0:T(8,128)(2,1)S(1)}, bf16[352,768]{1,0:T(8,128)(2,1)S(1)}, u32[]{:S(2)}, u32[]{:S(2)}) collective-permute-start(bf16[352,768]{1,0:T(8,128)(2,1)S(1)} %pad_maximum_fusion.5), channel_id=1, source_target_pairs={{0,8},{24,16},{1,9},{25,17},{2,10},{26,18},{3,11},{27,19},{4,12},{... | collective-permute-start | bytes 1622024 | tf_op jit(solution)/shard_map/ppermute | solution.py:134
  237.0 3.4 %collective-permute-done.63 = bf16[352,768]{1,0:T(8,128)(2,1)S(1)} collective-permute-done((bf16[352,768]{1,0:T(8,128)(2,1)S(1)}, bf16[352,768]{1,0:T(8,128)(2,1)S(1)}, u32[]{:S(2)}, u32[]{:S(2)}) %collective-permute-start.63) | collective-permute-done | bytes 540704 | tf_op jit(solution)/shard_map/ppermute | solution.py:134
  241.5 7.3 %collective-permute-start.65 = (bf16[96,2304]{1,0:T(8,128)(2,1)S(1)}, bf16[96,2304]{1,0:T(8,128)(2,1)S(1)}, u32[]{:S(2)}, u32[]{:S(2)}) collective-permute-start(bf16[96,2304]{1,0:T(8,128)(2,1)S(1)} %pad_maximum_fusion.6), channel_id=1, source_target_pairs={{0,8},{24,16},{1,9},{25,17},{2,10},{26,18},{3,11},{27,19},{4,12},{... | collective-permute-start | bytes 1327112 | tf_op jit(solution)/shard_map/ppermute | solution.py:134
  250.0 4.5 %collective-permute-done.65 = bf16[96,2304]{1,0:T(8,128)(2,1)S(1)} collective-permute-done((bf16[96,2304]{1,0:T(8,128)(2,1)S(1)}, bf16[96,2304]{1,0:T(8,128)(2,1)S(1)}, u32[]{:S(2)}, u32[]{:S(2)}) %collective-permute-start.65) | collective-permute-done | bytes 442400 | tf_op jit(solution)/shard_map/ppermute | solution.py:134
  256.9 6.9 %input_gradient.1 = f32[512,2048]{1,0:T(8,128)} custom-call(s32[8]{0:T(128)S(1)} %iota_xor_fusion.places, bf16[512,768]{1,0:T(8,128)(2,1)S(1)} %get-tuple-element.201.low_ref, bf16[256,768]{1,0:T(8,128)(2,1)} %refs_0_.7, bf16[256,768]{1,0:T(8,128)(2,1)} %copy-done.16, bf16[256,768]{1,0:T(8,128)(2,1)} %copy-done.32, bf16[256,768]{1,0:T(8,128)(2,1)} %copy-done.17, ...), custom_call_target="tpu_custom_call" | custom-call | flops 1024 | bytes 1024 | tf_op jit(solution)/shard_map/input_gradient/pallas_call | solution.py:276
  266.3 5.8 %collective-permute-done.67 = bf16[352,768]{1,0:T(8,128)(2,1)S(1)} collective-permute-done((bf16[352,768]{1,0:T(8,128)(2,1)S(1)}, bf16[352,768]{1,0:T(8,128)(2,1)S(1)}, u32[]{:S(2)}, u32[]{:S(2)}) %collective-permute-start.67) | collective-permute-done | bytes 540704 | tf_op jit(solution)/shard_map/ppermute | solution.py:134
  273.9 3.9 %collective-permute-done.69 = bf16[96,2304]{1,0:T(8,128)(2,1)S(1)} collective-permute-done((bf16[96,2304]{1,0:T(8,128)(2,1)S(1)}, bf16[96,2304]{1,0:T(8,128)(2,1)S(1)}, u32[]{:S(2)}, u32[]{:S(2)}) %collective-permute-start.69) | collective-permute-done | bytes 442400 | tf_op jit(solution)/shard_map/ppermute | solution.py:134
  (274 shorter events, 95.4 us)
Async XLA Ops:
  3.7 19.2 %collective-permute-start.1 = (bf16[256,768]{1,0:T(8,128)(2,1)}, bf16[256,768]{1,0:T(8,128)(2,1)S(1)}, u32[]{:S(2)}, u32[]{:S(2)}) collective-permute-start(bf16[256,768]{1,0:T(8,128)(2,1)} %refs_0_.7), channel_id=1, source_target_pairs={{0,4},{1,5},{2,6},{3,7},{4,0},{5,1},{6,2},{7,3},{8,12},{9,13},{10,... | collective-permute-start | bytes 1179656 | tf_op jit(solution)/shard_map/ppermute | solution.py:38
  5.2 17.7 %collective-permute-start.2 = (bf16[256,768]{1,0:T(8,128)(2,1)}, bf16[256,768]{1,0:T(8,128)(2,1)S(1)}, u32[]{:S(2)}, u32[]{:S(2)}) collective-permute-start(bf16[256,768]{1,0:T(8,128)(2,1)} %refs_0_.7), channel_id=1, source_target_pairs={{0,6},{1,7},{2,4},{3,5},{4,2},{5,3},{6,0},{7,1},{8,14},{9,15},{10,... | collective-permute-start | bytes 1179656 | tf_op jit(solution)/shard_map/ppermute | solution.py:38
  24.0 20.8 %collective-permute-start.13 = (bf16[96,2304]{1,0:T(8,128)(2,1)}, bf16[96,2304]{1,0:T(8,128)(2,1)}, u32[]{:S(2)}, u32[]{:S(2)}) collective-permute-start(bf16[96,2304]{1,0:T(8,128)(2,1)} %refs_0_.6), channel_id=1, source_target_pairs={{0,2},{1,3},{2,0},{3,1},{4,6},{5,7},{6,4},{7,5},{8,10},{9,11},{10,... | collective-permute-start | bytes 1327112 | tf_op jit(solution)/shard_map/ppermute | solution.py:38
  25.1 21.3 %collective-permute-start.14 = (bf16[96,2304]{1,0:T(8,128)(2,1)}, bf16[96,2304]{1,0:T(8,128)(2,1)}, u32[]{:S(2)}, u32[]{:S(2)}) collective-permute-start(bf16[96,2304]{1,0:T(8,128)(2,1)} %refs_0_.6), channel_id=1, source_target_pairs={{0,4},{1,5},{2,6},{3,7},{4,0},{5,1},{6,2},{7,3},{8,12},{9,13},{10,... | collective-permute-start | bytes 1327112 | tf_op jit(solution)/shard_map/ppermute | solution.py:38
  26.4 21.0 %collective-permute-start.15 = (bf16[96,2304]{1,0:T(8,128)(2,1)}, bf16[96,2304]{1,0:T(8,128)(2,1)}, u32[]{:S(2)}, u32[]{:S(2)}) collective-permute-start(bf16[96,2304]{1,0:T(8,128)(2,1)} %refs_0_.6), channel_id=1, source_target_pairs={{0,6},{1,7},{2,4},{3,5},{4,2},{5,3},{6,0},{7,1},{8,14},{9,15},{10,... | collective-permute-start | bytes 1327112 | tf_op jit(solution)/shard_map/ppermute | solution.py:38
  49.5 17.5 %collective-permute-start.21 = (bf16[96,3840]{1,0:T(8,128)(2,1)}, bf16[96,3840]{1,0:T(8,128)(2,1)}, u32[]{:S(2)}, u32[]{:S(2)}) collective-permute-start(bf16[96,3840]{1,0:T(8,128)(2,1)} %constant_dynamic-update-slice_fusion.refs_0_), channel_id=1, source_target_pairs={{0,2},{1,3},{2,0},{3,1},{4,6},{5,7},{6,4},{7,5},{8,10},{9,11},{10,... | collective-permute-start | bytes 2211848 | tf_op jit(solution)/shard_map/ppermute | solution.py:38
  50.7 17.4 %collective-permute-start.22 = (bf16[96,3840]{1,0:T(8,128)(2,1)}, bf16[96,3840]{1,0:T(8,128)(2,1)}, u32[]{:S(2)}, u32[]{:S(2)}) collective-permute-start(bf16[96,3840]{1,0:T(8,128)(2,1)} %constant_dynamic-update-slice_fusion.refs_0_), channel_id=1, source_target_pairs={{0,4},{1,5},{2,6},{3,7},{4,0},{5,1},{6,2},{7,3},{8,12},{9,13},{10,... | collective-permute-start | bytes 2211848 | tf_op jit(solution)/shard_map/ppermute | solution.py:38
  69.6 14.5 %collective-permute-start.20 = (bf16[96,3840]{1,0:T(8,128)(2,1)}, bf16[96,3840]{1,0:T(8,128)(2,1)S(1)}, u32[]{:S(2)}, u32[]{:S(2)}) collective-permute-start(bf16[96,3840]{1,0:T(8,128)(2,1)} %constant_dynamic-update-slice_fusion.refs_0_), channel_id=1, source_target_pairs={{0,1},{1,0},{2,3},{3,2},{4,5},{5,4},{6,7},{7,6},{8,9},{9,8},{10,11... | collective-permute-start | bytes 2211848 | tf_op jit(solution)/shard_map/ppermute | solution.py:38
  70.6 14.1 %collective-permute-start.23 = (bf16[96,3840]{1,0:T(8,128)(2,1)}, bf16[96,3840]{1,0:T(8,128)(2,1)S(1)}, u32[]{:S(2)}, u32[]{:S(2)}) collective-permute-start(bf16[96,3840]{1,0:T(8,128)(2,1)} %collective-permute-done.21.refs_2_), channel_id=1, source_target_pairs={{0,1},{1,0},{2,3},{3,2},{4,5},{5,4},{6,7},{7,6},{8,9},{9,8},{10,11... | collective-permute-start | bytes 2211848 | tf_op jit(solution)/shard_map/ppermute | solution.py:38
  71.2 13.5 %collective-permute-start.24 = (bf16[96,3840]{1,0:T(8,128)(2,1)}, bf16[96,3840]{1,0:T(8,128)(2,1)S(1)}, u32[]{:S(2)}, u32[]{:S(2)}) collective-permute-start(bf16[96,3840]{1,0:T(8,128)(2,1)} %collective-permute-done.22.refs_4_), channel_id=1, source_target_pairs={{0,1},{1,0},{2,3},{3,2},{4,5},{5,4},{6,7},{7,6},{8,9},{9,8},{10,11... | collective-permute-start | bytes 2211848 | tf_op jit(solution)/shard_map/ppermute | solution.py:38
  82.3 15.7 %collective-permute-start.29 = (bf16[384,768]{1,0:T(8,128)(2,1)S(1)}, bf16[384,768]{1,0:T(8,128)(2,1)S(1)}, u32[]{:S(2)}, u32[]{:S(2)}) collective-permute-start(bf16[384,768]{1,0:T(8,128)(2,1)S(1)} %copy-done.25), channel_id=1, source_target_pairs={{0,2},{1,3},{2,0},{3,1},{4,6},{5,7},{6,4},{7,5},{8,10},{9,11},{10,... | collective-permute-start | bytes 1769480 | tf_op jit(solution)/shard_map/ppermute | solution.py:38
  84.1 15.4 %collective-permute-start.30 = (bf16[384,768]{1,0:T(8,128)(2,1)S(1)}, bf16[384,768]{1,0:T(8,128)(2,1)S(1)}, u32[]{:S(2)}, u32[]{:S(2)}) collective-permute-start(bf16[384,768]{1,0:T(8,128)(2,1)S(1)} %copy-done.25), channel_id=1, source_target_pairs={{0,4},{1,5},{2,6},{3,7},{4,0},{5,1},{6,2},{7,3},{8,12},{9,13},{10,... | collective-permute-start | bytes 1769480 | tf_op jit(solution)/shard_map/ppermute | solution.py:38
  131.5 15.5 %collective-permute-start.39 = (bf16[4,384,768]{2,1,0:T(8,128)(2,1)S(1)}, bf16[4,384,768]{2,1,0:T(8,128)(2,1)S(1)}, u32[]{:S(2)}, u32[]{:S(2)}) collective-permute-start(bf16[4,384,768]{2,1,0:T(8,128)(2,1)S(1)} %get-tuple-element.167), channel_id=1, source_target_pairs={{0,1},{1,0},{2,3},{3,2},{4,5},{5,4},{6,7},{7,6},{8,9},{9,8},{10,11... | collective-permute-start | bytes 7077896 | tf_op jit(solution)/shard_map/ppermute | solution.py:38
  132.1 15.4 %collective-permute-start.38 = (bf16[2,192,768]{2,1,0:T(8,128)(2,1)S(1)}, bf16[2,192,768]{2,1,0:T(8,128)(2,1)S(1)}, u32[]{:S(2)}, u32[]{:S(2)}) collective-permute-start(bf16[2,192,768]{2,1,0:T(8,128)(2,1)S(1)} %add_convert_fusion.6), channel_id=1, source_target_pairs={{0,4},{1,5},{2,6},{3,7},{4,0},{5,1},{6,2},{7,3},{8,12},{9,13},{10,... | collective-permute-start | bytes 1769480 | tf_op jit(solution)/shard_map/ppermute | solution.py:38
  133.5 15.2 %collective-permute-start.37 = (bf16[2,192,768]{2,1,0:T(8,128)(2,1)S(1)}, bf16[2,192,768]{2,1,0:T(8,128)(2,1)S(1)}, u32[]{:S(2)}, u32[]{:S(2)}) collective-permute-start(bf16[2,192,768]{2,1,0:T(8,128)(2,1)S(1)} %add_convert_fusion.7), channel_id=1, source_target_pairs={{0,2},{1,3},{2,0},{3,1},{4,6},{5,7},{6,4},{7,5},{8,10},{9,11},{10,... | collective-permute-start | bytes 1769480 | tf_op jit(solution)/shard_map/ppermute | solution.py:38
  149.2 21.0 %collective-permute-start.44 = (bf16[576,768]{1,0:T(8,128)(2,1)S(1)}, bf16[576,768]{1,0:T(8,128)(2,1)S(1)}, u32[]{:S(2)}, u32[]{:S(2)}) collective-permute-start(bf16[576,768]{1,0:T(8,128)(2,1)S(1)} %pad_maximum_fusion.2), channel_id=1, source_target_pairs={{0,4},{1,5},{2,6},{3,7},{4,0},{5,1},{6,2},{7,3},{8,12},{9,13},{10,... | collective-permute-start | bytes 2654216 | tf_op jit(solution)/shard_map/ppermute | solution.py:38
  150.4 20.3 %collective-permute-start.43 = (bf16[576,768]{1,0:T(8,128)(2,1)S(1)}, bf16[576,768]{1,0:T(8,128)(2,1)S(1)}, u32[]{:S(2)}, u32[]{:S(2)}) collective-permute-start(bf16[576,768]{1,0:T(8,128)(2,1)S(1)} %pad_maximum_fusion.1), channel_id=1, source_target_pairs={{0,2},{1,3},{2,0},{3,1},{4,6},{5,7},{6,4},{7,5},{8,10},{9,11},{10,... | collective-permute-start | bytes 2654216 | tf_op jit(solution)/shard_map/ppermute | solution.py:38
  185.0 14.6 %collective-permute-start.53 = (bf16[192,768]{1,0:T(8,128)(2,1)}, bf16[192,768]{1,0:T(8,128)(2,1)S(1)}, u32[]{:S(2)}, u32[]{:S(2)}) collective-permute-start(bf16[192,768]{1,0:T(8,128)(2,1)} %get-tuple-element.262), channel_id=1, source_target_pairs={{0,4},{1,5},{2,6},{3,7},{4,0},{5,1},{6,2},{7,3},{8,12},{9,13},{10,... | collective-permute-start | bytes 884744 | tf_op jit(solution)/shard_map/ppermute | solution.py:38
  186.4 14.1 %collective-permute-start.54 = (bf16[192,768]{1,0:T(8,128)(2,1)S(1)}, bf16[192,768]{1,0:T(8,128)(2,1)S(1)}, u32[]{:S(2)}, u32[]{:S(2)}) collective-permute-start(bf16[192,768]{1,0:T(8,128)(2,1)S(1)} %get-tuple-element.261), channel_id=1, source_target_pairs={{0,2},{1,3},{2,0},{3,1},{4,6},{5,7},{6,4},{7,5},{8,10},{9,11},{10,... | collective-permute-start | bytes 884744 | tf_op jit(solution)/shard_map/ppermute | solution.py:38
  187.1 16.2 %collective-permute-start.52 = (bf16[384,768]{1,0:T(8,128)(2,1)S(1)}, bf16[384,768]{1,0:T(8,128)(2,1)S(1)}, u32[]{:S(2)}, u32[]{:S(2)}) collective-permute-start(bf16[384,768]{1,0:T(8,128)(2,1)S(1)} %pad_maximum_fusion.3), channel_id=1, source_target_pairs={{0,8},{24,16},{1,9},{25,17},{2,10},{26,18},{3,11},{27,19},{4,12},{... | collective-permute-start | bytes 1769480 | tf_op jit(solution)/shard_map/ppermute | solution.py:134
  195.2 20.0 %collective-permute-start.48 = (bf16[4,96,2304]{2,1,0:T(8,128)(2,1)S(1)}, bf16[4,96,2304]{2,1,0:T(8,128)(2,1)S(1)}, u32[]{:S(2)}, u32[]{:S(2)}) collective-permute-start(bf16[4,96,2304]{2,1,0:T(8,128)(2,1)S(1)} %get-tuple-element.205), channel_id=1, source_target_pairs={{0,1},{1,0},{2,3},{3,2},{4,5},{5,4},{6,7},{7,6},{8,9},{9,8},{10,11... | collective-permute-start | bytes 5308424 | tf_op jit(solution)/shard_map/ppermute | solution.py:38
  198.2 14.7 %collective-permute-start.51 = (bf16[2,176,768]{2,1,0:T(8,128)(2,1)S(1)}, bf16[2,176,768]{2,1,0:T(8,128)(2,1)S(1)}, u32[]{:S(2)}, u32[]{:S(2)}) collective-permute-start(bf16[2,176,768]{2,1,0:T(8,128)(2,1)S(1)} %add_convert_fusion.10), channel_id=1, source_target_pairs={{0,4},{1,5},{2,6},{3,7},{4,0},{5,1},{6,2},{7,3},{8,12},{9,13},{10,... | collective-permute-start | bytes 1622024 | tf_op jit(solution)/shard_map/ppermute | solution.py:38
  199.6 14.5 %collective-permute-start.50 = (bf16[2,176,768]{2,1,0:T(8,128)(2,1)S(1)}, bf16[2,176,768]{2,1,0:T(8,128)(2,1)S(1)}, u32[]{:S(2)}, u32[]{:S(2)}) collective-permute-start(bf16[2,176,768]{2,1,0:T(8,128)(2,1)S(1)} %add_convert_fusion.11), channel_id=1, source_target_pairs={{0,2},{1,3},{2,0},{3,1},{4,6},{5,7},{6,4},{7,5},{8,10},{9,11},{10,... | collective-permute-start | bytes 1622024 | tf_op jit(solution)/shard_map/ppermute | solution.py:38
  202.0 16.4 %collective-permute-start.60 = (bf16[384,768]{1,0:T(8,128)(2,1)S(1)}, bf16[384,768]{1,0:T(8,128)(2,1)S(1)}, u32[]{:S(2)}, u32[]{:S(2)}) collective-permute-start(bf16[384,768]{1,0:T(8,128)(2,1)S(1)} %pad_maximum_fusion.4), channel_id=1, source_target_pairs={{0,8},{24,16},{1,9},{25,17},{2,10},{26,18},{3,11},{27,19},{4,12},{... | collective-permute-start | bytes 1769480 | tf_op jit(solution)/shard_map/ppermute | solution.py:134
  203.5 16.4 %collective-permute-start.59 = (bf16[384,768]{1,0:T(8,128)(2,1)S(1)}, bf16[384,768]{1,0:T(8,128)(2,1)S(1)}, u32[]{:S(2)}, u32[]{:S(2)}) collective-permute-start(bf16[384,768]{1,0:T(8,128)(2,1)S(1)} %add_convert_fusion.3), channel_id=1, source_target_pairs={{8,16},{16,8},{9,17},{17,9},{10,18},{18,10},{11,19},{19,11},{12,20... | collective-permute-start | bytes 1769480 | tf_op jit(solution)/shard_map/ppermute | solution.py:134
  217.8 15.0 %collective-permute-start.56 = (bf16[2,48,2304]{2,1,0:T(8,128)(2,1)S(1)}, bf16[2,48,2304]{2,1,0:T(8,128)(2,1)S(1)}, u32[]{:S(2)}, u32[]{:S(2)}) collective-permute-start(bf16[2,48,2304]{2,1,0:T(8,128)(2,1)S(1)} %add_convert_fusion.14), channel_id=1, source_target_pairs={{0,4},{1,5},{2,6},{3,7},{4,0},{5,1},{6,2},{7,3},{8,12},{9,13},{10,... | collective-permute-start | bytes 1327112 | tf_op jit(solution)/shard_map/ppermute | solution.py:38
  218.5 14.9 %collective-permute-start.55 = (bf16[2,48,2304]{2,1,0:T(8,128)(2,1)S(1)}, bf16[2,48,2304]{2,1,0:T(8,128)(2,1)S(1)}, u32[]{:S(2)}, u32[]{:S(2)}) collective-permute-start(bf16[2,48,2304]{2,1,0:T(8,128)(2,1)S(1)} %add_convert_fusion.15), channel_id=1, source_target_pairs={{0,2},{1,3},{2,0},{3,1},{4,6},{5,7},{6,4},{7,5},{8,10},{9,11},{10,... | collective-permute-start | bytes 1327112 | tf_op jit(solution)/shard_map/ppermute | solution.py:38
  219.9 15.7 %collective-permute-start.64 = (bf16[384,768]{1,0:T(8,128)(2,1)S(1)}, bf16[384,768]{1,0:T(8,128)(2,1)S(1)}, u32[]{:S(2)}, u32[]{:S(2)}) collective-permute-start(bf16[384,768]{1,0:T(8,128)(2,1)S(1)} %add_convert_fusion.2), channel_id=1, source_target_pairs={{8,16},{16,8},{9,17},{17,9},{10,18},{18,10},{11,19},{19,11},{12,20... | collective-permute-start | bytes 1769480 | tf_op jit(solution)/shard_map/ppermute | solution.py:134
  224.9 23.9 %collective-permute-start.71 = (bf16[384,768]{1,0:T(8,128)(2,1)S(1)}, bf16[384,768]{1,0:T(8,128)(2,1)S(1)}, u32[]{:S(2)}, u32[]{:S(2)}) collective-permute-start(bf16[384,768]{1,0:T(8,128)(2,1)S(1)} %add_convert_fusion.1), channel_id=1, source_target_pairs={{8,0},{16,24},{9,1},{17,25},{10,2},{18,26},{11,3},{19,27},{12,4},{... | collective-permute-start | bytes 1769480 | tf_op jit(solution)/shard_map/ppermute | solution.py:134
  235.7 19.7 %collective-permute-start.70 = (bf16[384,768]{1,0:T(8,128)(2,1)S(1)}, bf16[384,768]{1,0:T(8,128)(2,1)S(1)}, u32[]{:S(2)}, u32[]{:S(2)}) collective-permute-start(bf16[384,768]{1,0:T(8,128)(2,1)S(1)} %add_convert_fusion), channel_id=1, source_target_pairs={{8,0},{16,24},{9,1},{17,25},{10,2},{18,26},{11,3},{19,27},{12,4},{... | collective-permute-start | bytes 1769480 | tf_op jit(solution)/shard_map/ppermute | solution.py:134
  255.6 16.6 %collective-permute-start.67 = (bf16[352,768]{1,0:T(8,128)(2,1)S(1)}, bf16[352,768]{1,0:T(8,128)(2,1)S(1)}, u32[]{:S(2)}, u32[]{:S(2)}) collective-permute-start(bf16[352,768]{1,0:T(8,128)(2,1)S(1)} %add_convert_fusion.8), channel_id=1, source_target_pairs={{8,0},{16,24},{9,1},{17,25},{10,2},{18,26},{11,3},{19,27},{12,4},{... | collective-permute-start | bytes 1622024 | tf_op jit(solution)/shard_map/ppermute | solution.py:134
  263.9 13.9 %collective-permute-start.69 = (bf16[96,2304]{1,0:T(8,128)(2,1)S(1)}, bf16[96,2304]{1,0:T(8,128)(2,1)S(1)}, u32[]{:S(2)}, u32[]{:S(2)}) collective-permute-start(bf16[96,2304]{1,0:T(8,128)(2,1)S(1)} %add_convert_fusion.12), channel_id=1, source_target_pairs={{8,0},{16,24},{9,1},{17,25},{10,2},{18,26},{11,3},{19,27},{12,4},{... | collective-permute-start | bytes 1327112 | tf_op jit(solution)/shard_map/ppermute | solution.py:134
  (76 other events, 645.0 us)
